TPU v7x, 32 devices: a whole 2x2x4 slice. The times are simulated.
32 devices in a mesh: grp: 2 (over y), pulse: 16 (over z, x, core), rng: 1.
Axes of the slice: x: 2, y: 2, z: 4, core: 2. Of those that a mesh axis runs over, the one named last changes fastest.
Arguments:
- raw_echoes: bfloat16 [256, 64, 2, 128], P(('grp', 'pulse'), 'rng'), parts along dimension 0, may hold values from -6 to 6
- matched: float32 [2, 128], replicated, may hold values from -0.375 to 0.375
- delays: int32 [256, 16], P(('grp', 'pulse')), parts along dimension 0, may hold values from -24 to 24
- pulse_phase: float32 [256, 16], P(('grp', 'pulse')), parts along dimension 0, may hold values from -3.140625 to 3.140625
- beam_map: int32 [4, 2, 2, 16], replicated, may hold values from 0 to 15, as said below
- range_shift: int32 [4, 2, 2, 16], replicated, may hold values from -24 to 24
- phase_base: float32 [4, 2, 2, 16], replicated, may hold values from -3.140625 to 3.140625
- phase_rate: float32 [4, 2, 2, 16], replicated, may hold values from -4 to 4
- tap_offsets: int32 [4, 4], replicated, may hold values from -4 to 4, as said below
Outputs:
- final_image: float32 [2, 512, 8192], P(None, ('grp', 'pulse'), 'rng'), parts along dimension 1
There are 2 independent parts, one for each index of `grp`. A program takes and returns all parts, laid end to end along the dimension named above; an argument that names none is the same for every part. Nothing has to cross between parts.
Inputs may be any that keep to these rules, and one draw needn't show every extreme that they name: `beam_map`: entry [l, h, s, k] is h * 8 + k // 2 plus -1, 0 or 1, clamped to the range. `tap_offsets`: the 4 entries of one level are distinct.
All inputs are finite; a program needn't handle non-finite values.
Results may differ from a plain program's by a relative error of at most 0.0055.
Values may be sent and summed in bfloat16 or wider, within the bound.
No kernel may reach another device: no remote copies, remote signals or barrier semaphores. Data moves between devices by JAX's collectives and lax.ppermute only.
A program may use at most 64 MiB of HBM per device.

v0:
```python
import math

import jax
import jax.numpy as jnp
from jax import lax
from jax.sharding import PartitionSpec as P

R = 8192
BLOCK = 256
LEVELS = 4
SHIFT = 24
SPREAD = 4


SQRT_HALF = 0.7071067811865476


def shifted(array, axis, by):
    count = lax.axis_size(axis)
    pairs = [(i, i + by) for i in range(count) if 0 <= i + by < count]
    return lax.ppermute(array, axis, pairs)


def padded_2(block, sides, width):
    for axis, dim in sides:
        count = lax.axis_size(axis)
        forward = [(i, i + 1) for i in range(count - 1)]
        backward = [(target, source) for source, target in forward]
        low = lax.ppermute(
            lax.slice_in_dim(block, block.shape[dim] - width, None, axis=dim), axis, forward
        )
        high = lax.ppermute(lax.slice_in_dim(block, 0, width, axis=dim), axis, backward)
        block = jnp.concatenate([low, block, high], axis=dim)
    return block


def from_partner(block, axis, bit):
    count = lax.axis_size(axis)
    route = []
    for low in range(count):
        high = low | 1 << bit
        if high != low and high < count:
            route += [(low, high), (high, low)]
    return lax.ppermute(block, axis, route)


def tables(length):
    counter = jnp.arange(length, dtype=jnp.int32)
    product = counter[:, None] * counter[None, :] % length
    angles = product.astype(jnp.float32) * (2.0 * math.pi / length)
    cosine = jnp.cos(angles)
    sine_part = jnp.sin(angles)
    forward = jnp.concatenate(
        [
            jnp.concatenate([cosine, -sine_part], axis=1),
            jnp.concatenate([sine_part, cosine], axis=1),
        ],
        axis=0,
    )
    inverse = jnp.concatenate(
        [
            jnp.concatenate([cosine, sine_part], axis=1),
            jnp.concatenate([-sine_part, cosine], axis=1),
        ],
        axis=0,
    )
    return (forward, inverse)


def compress(echoes, tail, matched, forward_exact, forward, inverse_kept):
    pulses, blocks, parts, hop_bins = echoes.shape
    length = 2 * hop_bins
    previous = jnp.concatenate([tail[:, None], echoes[:, :-1]], axis=1)
    windows = jnp.concatenate([previous, echoes], axis=3).reshape(pulses * blocks, parts * length)
    taps_padded = jnp.concatenate(
        [matched, jnp.zeros((2, length - hop_bins), jnp.float32)], axis=1
    ).reshape(1, 2 * length)
    response = jnp.dot(taps_padded, forward_exact, precision=lax.Precision.HIGHEST)[0]
    resp_real = response[:length]
    resp_imag = response[length:]
    spectrum = jnp.dot(windows, forward, preferred_element_type=jnp.float32)
    spec_real = spectrum[:, :length]
    spec_imag = spectrum[:, length:]
    filt_real = spec_real * resp_real - spec_imag * resp_imag
    filt_imag = spec_real * resp_imag + spec_imag * resp_real
    shaped = jnp.concatenate([filt_real, filt_imag], axis=1).astype(jnp.bfloat16)
    restored = jnp.dot(shaped, inverse_kept, preferred_element_type=jnp.float32) * (1.0 / length)
    return restored.astype(jnp.bfloat16).reshape(pulses, blocks, parts, hop_bins)


def kept_columns(inverse, length):
    half = length // 2
    return jnp.concatenate([inverse[:, half:length], inverse[:, length + half :]], axis=1)


def inside_mask(first_cell, out_cells):
    global_cells = first_cell + jnp.arange(out_cells, dtype=jnp.int32)
    return ((global_cells >= 0) & (global_cells < R)).astype(jnp.float32)


def row_slices(rows, starts, width):

    def per_pulse(row, start_row):
        return jax.vmap(lambda start: lax.dynamic_slice_in_dim(row, start, width, 1))(start_row)

    return jax.vmap(per_pulse)(rows, starts)


def project(padded, delay_rows, phase_rows, offset_base, out_cells, first_cell):
    pulses = padded.shape[0]
    beam_count = delay_rows.shape[1]
    group_size = math.gcd(pulses, 4)
    block_count = pulses // group_size

    def accumulate(summed, block_index):
        first_row = block_index * group_size
        pulses_block = lax.dynamic_slice_in_dim(padded, first_row, group_size, 0)
        delay_block = lax.dynamic_slice_in_dim(delay_rows, first_row, group_size, 0)
        phase_block = lax.dynamic_slice_in_dim(phase_rows, first_row, group_size, 0)
        starts = delay_block + offset_base
        gathered = row_slices(pulses_block, starts, out_cells).astype(jnp.float32)
        cosine = jnp.cos(phase_block)[:, :, None]
        sine_part = jnp.sin(phase_block)[:, :, None]
        real_part = gathered[:, :, 0] * cosine - gathered[:, :, 1] * sine_part
        imag_part = gathered[:, :, 0] * sine_part + gathered[:, :, 1] * cosine
        return (summed + jnp.stack([jnp.sum(real_part, axis=0), jnp.sum(imag_part, axis=0)]), None)

    summed, unused = lax.scan(
        accumulate,
        jnp.zeros((2, beam_count, out_cells), jnp.float32),
        jnp.arange(block_count, dtype=jnp.int32),
    )
    return summed * inside_mask(first_cell, out_cells) * (1.0 / math.sqrt(pulses))


def tap_weights(tap_values):
    weights = SPREAD + 1.0 - jnp.abs(tap_values).astype(jnp.float32)
    return weights / jnp.sum(weights)


def merge_side(
    source,
    beam_rows,
    offsets,
    phase_zero,
    phase_slope,
    weights,
    tap_values,
    offset_base,
    out_cells,
    first_cell,
):
    picked = jnp.take(source, beam_rows, axis=1)
    span = out_cells + 2 * SPREAD
    starts = offsets + offset_base - SPREAD
    windows = jax.vmap(
        lambda beam_data, start: lax.dynamic_slice_in_dim(beam_data, start, span, 1),
        in_axes=(1, 0),
        out_axes=1,
    )(picked, starts)
    summed = jnp.zeros((2, beam_rows.shape[0], out_cells), jnp.float32)
    for tap_index in range(tap_values.shape[0]):
        tap_start = tap_values[tap_index] + SPREAD
        summed = summed + weights[tap_index] * lax.dynamic_slice_in_dim(
            windows, tap_start, out_cells, 2
        )
    positions = jnp.arange(out_cells, dtype=jnp.int32)
    global_cells = (first_cell + positions).astype(jnp.float32)
    angle_grid = (
        phase_zero[:, None] + 2.0 * math.pi / R * phase_slope[:, None] * global_cells[None, :]
    )
    cosine = jnp.cos(angle_grid)
    sine_part = jnp.sin(angle_grid)
    return jnp.stack(
        [summed[0] * cosine - summed[1] * sine_part, summed[0] * sine_part + summed[1] * cosine]
    )


def pick_sides(table, level_index, side_bit):
    half_rows = lax.dynamic_index_in_dim(table[level_index], side_bit, 0, keepdims=False)
    own_rows = lax.dynamic_index_in_dim(half_rows, side_bit, 0, keepdims=False)
    other_rows = lax.dynamic_index_in_dim(half_rows, 1 - side_bit, 0, keepdims=False)
    return (own_rows, other_rows)


def local(
    raw_echoes,
    matched,
    delays,
    pulse_phase,
    beam_map,
    range_shift,
    phase_base,
    phase_rate,
    tap_offsets,
):
    pulses = raw_echoes.shape[0]
    hop_bins = raw_echoes.shape[3]
    local_cells = raw_echoes.shape[1] * hop_bins
    forward_exact, inverse_exact = tables(BLOCK)
    forward = forward_exact.astype(jnp.bfloat16)
    inverse_kept = kept_columns(inverse_exact.astype(jnp.bfloat16), BLOCK)
    tail = shifted(raw_echoes[:, -1], "rng", 1)
    compressed = compress(raw_echoes, tail, matched, forward_exact, forward, inverse_kept)
    compressed = jnp.transpose(compressed, (0, 2, 1, 3)).reshape(pulses, 2, local_cells)
    first_cell = lax.axis_index("rng") * local_cells
    rim_cells = SHIFT + SPREAD
    margin_cells = LEVELS * rim_cells
    padded = padded_2(compressed, (("rng", 2),), SHIFT + margin_cells)
    polar_image = project(
        padded,
        delays,
        pulse_phase,
        SHIFT,
        local_cells + 2 * margin_cells,
        first_cell - margin_cells,
    )
    pulse_index = lax.axis_index("pulse")
    for level_index in range(LEVELS):
        side_bit = pulse_index // 2**level_index % 2
        own_beams, other_beams = pick_sides(beam_map, level_index, side_bit)
        own_offsets, other_offsets = pick_sides(range_shift, level_index, side_bit)
        own_zero, other_zero = pick_sides(phase_base, level_index, side_bit)
        own_slope, other_slope = pick_sides(phase_rate, level_index, side_bit)
        tap_values = tap_offsets[level_index]
        weights = tap_weights(tap_values)
        received = from_partner(polar_image, "pulse", level_index)
        own_source = polar_image
        out_margin = max(margin_cells - rim_cells * (level_index + 1), 0)
        out_cells = local_cells + 2 * out_margin
        start_cell = first_cell - out_margin
        own_side = merge_side(
            own_source,
            own_beams,
            own_offsets,
            own_zero,
            own_slope,
            weights,
            tap_values,
            rim_cells,
            out_cells,
            start_cell,
        )
        other_side = merge_side(
            received,
            other_beams,
            other_offsets,
            other_zero,
            other_slope,
            weights,
            tap_values,
            rim_cells,
            out_cells,
            start_cell,
        )
        polar_image = (own_side + other_side) * SQRT_HALF * inside_mask(start_cell, out_cells)
    return polar_image


def solution(mesh):
    in_specs = (
        P(("grp", "pulse"), "rng", None, None),
        P(),
        P(("grp", "pulse"), None),
        P(("grp", "pulse"), None),
        P(),
        P(),
        P(),
        P(),
        P(),
    )
    out_specs = P(None, ("grp", "pulse"), "rng")
    return jax.shard_map(local, mesh=mesh, in_specs=in_specs, out_specs=out_specs, check_vma=False)
```

profile of v0, /device:TPU:0, one launch (start us, length us, event | category | flops | bytes accessed | tf_op | source)
XLA Modules:
  0.0 847.6 jit_solution(4714250410205099282)
XLA Ops:
  17.8 2.5 broadcast_divide_fusion.3
  51.4 271.4 %while.33 = (s32[]{:T(128)}, f32[2,16,8416]{2,1,0:T(8,128)S(1)}, s32[2]{0:T(128)S(1)}, bf16[8,2,8464]{2,1,0:T(2,128)(2,1)}, s32[8,16]{1,0:T(8,128)}, /*index=5*/...) while((s32[]{:T(128)}, f32[2,16,8416]{2,1,0:T(8,128)S(1)}, ...), condition=%wide.region_7.8_spmd.clone, body=%wide.region_4.7_spmd.clone.sunk | while | flops 4848073 | bytes 17581828 | solution.py:128
  54.5 128.3 %while.34 = (s32[]{:T(128)}, bf16[4,2,8464]{2,1,0:T(2,128)(2,1)S(1)}, s32[64,3]{0,1:T(4,128)S(1)}, bf16[64,2,8416]{2,1,0:T(2,128)(2,1)S(1)}, s32[]{:T(128)}) while((s32[]{:T(128)}, bf16[4,2,8464]{2,1,0:T(2,128)(2,1)S(1)}, s32[64,3]{0,1:T(4,128)S(1)}, bf16[64,2,8416]{2,1,0:T(2,128)(2,1)S(1)}, s32[]{:T(128)}) %tuple.302), condition=%wide.while_cond, body=%wide.while_body.sunk | while | flops 2 | bytes 67709 | solution.py:104
  182.8 3.0 fusion.178
  190.2 128.3 %while.34 = (s32[]{:T(128)}, bf16[4,2,8464]{2,1,0:T(2,128)(2,1)S(1)}, s32[64,3]{0,1:T(4,128)S(1)}, bf16[64,2,8416]{2,1,0:T(2,128)(2,1)S(1)}, s32[]{:T(128)}) while((s32[]{:T(128)}, bf16[4,2,8464]{2,1,0:T(2,128)(2,1)S(1)}, s32[64,3]{0,1:T(4,128)S(1)}, bf16[64,2,8416]{2,1,0:T(2,128)(2,1)S(1)}, s32[]{:T(128)}) %tuple.302), condition=%wide.while_cond, body=%wide.while_body.sunk | while | flops 2 | bytes 67709 | solution.py:104
  318.4 3.0 fusion.178
  330.2 54.2 %while.24 = (s32[]{:T(128)}, f32[16,2,8416]{2,1,0:T(2,128)S(1)}, s32[16,3]{0,1:T(4,128)S(1)}, f32[16,2,8368]{2,0,1:T(8,128)S(1)}, s32[]{:T(128)}, /*index=5*/s32[]{:T(128)}) while((s32[]{:T(128)}, f32[16,2,8416]{2,1,0:T(2,128)S(1)}, s32[16,3]{0,1:T(4,128)S(1)}, f32[16,2,8368]{2,0,1:T(8,128)S(1)}, s32[]{:T(128)}, /*index=5*/s32[]{:T(128)}) %tuple.334), condition=%wide.while_cond.1, body=%wide.while_body.1.sunk | while | flops 2 | bytes 401797 | solution.py:157
  384.5 3.6 add_bitcast_fusion.1
  394.2 67.4 %while.25 = (s32[]{:T(128)}, f32[16,2,8416]{2,1,0:T(2,128)}, s32[16,3]{0,1:T(4,128)S(1)}, f32[16,2,8368]{2,0,1:T(8,128)S(1)}, s32[]{:T(128)}, /*index=5*/s32[]{:T(128)}) while((s32[]{:T(128)}, f32[16,2,8416]{2,1,0:T(2,128)}, s32[16,3]{0,1:T(4,128)S(1)}, f32[16,2,8368]{2,0,1:T(8,128)S(1)}, s32[]{:T(128)}, /*index=5*/s32[]{:T(128)}) %tuple.333), condition=%wide.while_cond.2, body=%wide.while_body.2.sunk | while | flops 2 | bytes 401797 | solution.py:157
  394.9 2.3 constant_dynamic-slice_fusion.71
  411.7 2.3 constant_dynamic-slice_fusion.71
  415.9 2.3 constant_dynamic-slice_fusion.71
  420.2 2.3 constant_dynamic-slice_fusion.71
  461.7 3.6 add_bitcast_fusion
  465.4 4.2 multiply_subtract_fusion
  469.7 2.6 collective-permute-start.4
  476.2 53.1 %while.26 = (s32[]{:T(128)}, f32[16,2,8360]{2,1,0:T(2,128)S(1)}, s32[16,3]{0,1:T(4,128)S(1)}, f32[16,2,8312]{2,0,1:T(8,128)S(1)}, s32[]{:T(128)}, /*index=5*/s32[]{:T(128)}) while((s32[]{:T(128)}, f32[16,2,8360]{2,1,0:T(2,128)S(1)}, s32[16,3]{0,1:T(4,128)S(1)}, f32[16,2,8312]{2,0,1:T(8,128)S(1)}, s32[]{:T(128)}, /*index=5*/s32[]{:T(128)}) %tuple.332), condition=%wide.while_cond.3, body=%wide.while_body.3.sunk | while | flops 2 | bytes 399109 | solution.py:157
  529.3 3.6 add_bitcast_fusion.5
  537.5 50.3 %while.27 = (s32[]{:T(128)}, f32[16,2,8360]{2,1,0:T(2,128)S(1)}, s32[16,3]{0,1:T(4,128)S(1)}, f32[16,2,8312]{2,0,1:T(8,128)S(1)}, s32[]{:T(128)}, /*index=5*/s32[]{:T(128)}) while((s32[]{:T(128)}, f32[16,2,8360]{2,1,0:T(2,128)S(1)}, s32[16,3]{0,1:T(4,128)S(1)}, f32[16,2,8312]{2,0,1:T(8,128)S(1)}, s32[]{:T(128)}, /*index=5*/s32[]{:T(128)}) %tuple.314), condition=%wide.while_cond.4, body=%wide.while_body.4.sunk | while | flops 2 | bytes 399109 | solution.py:157
  587.8 3.6 add_bitcast_fusion.4
  591.5 4.1 multiply_subtract_fusion.4
  600.4 50.2 %while.28 = (s32[]{:T(128)}, f32[16,2,8304]{2,1,0:T(2,128)S(1)}, s32[16,3]{0,1:T(4,128)S(1)}, f32[16,2,8256]{2,0,1:T(8,128)S(1)}, s32[]{:T(128)}, /*index=5*/s32[]{:T(128)}) while((s32[]{:T(128)}, f32[16,2,8304]{2,1,0:T(2,128)S(1)}, s32[16,3]{0,1:T(4,128)S(1)}, f32[16,2,8256]{2,0,1:T(8,128)S(1)}, s32[]{:T(128)}, /*index=5*/s32[]{:T(128)}) %tuple.323), condition=%wide.while_cond.5, body=%wide.while_body.5.sunk | while | flops 2 | bytes 396421 | solution.py:157
  650.6 3.8 add_bitcast_fusion.3
  658.7 52.3 %while.29 = (s32[]{:T(128)}, f32[16,2,8304]{2,1,0:T(2,128)S(1)}, s32[16,3]{0,1:T(4,128)S(1)}, f32[16,2,8256]{2,0,1:T(8,128)S(1)}, s32[]{:T(128)}, /*index=5*/s32[]{:T(128)}) while((s32[]{:T(128)}, f32[16,2,8304]{2,1,0:T(2,128)S(1)}, s32[16,3]{0,1:T(4,128)S(1)}, f32[16,2,8256]{2,0,1:T(8,128)S(1)}, s32[]{:T(128)}, /*index=5*/s32[]{:T(128)}) %tuple.320), condition=%wide.while_cond.6, body=%wide.while_body.6.sunk | while | flops 2 | bytes 396421 | solution.py:157
  711.0 3.8 add_bitcast_fusion.2
  714.8 4.1 multiply_subtract_fusion.2
  719.1 2.7 collective-permute-start.6
  724.8 53.4 %while.30 = (s32[]{:T(128)}, f32[16,2,8248]{2,1,0:T(2,128)S(1)}, s32[16,3]{0,1:T(4,128)S(1)}, f32[16,2,8200]{2,0,1:T(8,128)S(1)}, s32[]{:T(128)}, /*index=5*/s32[]{:T(128)}) while((s32[]{:T(128)}, f32[16,2,8248]{2,1,0:T(2,128)S(1)}, s32[16,3]{0,1:T(4,128)S(1)}, f32[16,2,8200]{2,0,1:T(8,128)S(1)}, s32[]{:T(128)}, /*index=5*/s32[]{:T(128)}) %tuple.329), condition=%wide.while_cond.7, body=%wide.while_body.7.sunk | while | flops 2 | bytes 393733 | solution.py:157
  778.1 3.6 add_bitcast_fusion.7
  786.0 52.3 %while.31 = (s32[]{:T(128)}, f32[16,2,8248]{2,1,0:T(2,128)S(1)}, s32[16,3]{0,1:T(4,128)S(1)}, f32[16,2,8200]{2,0,1:T(8,128)S(1)}, s32[]{:T(128)}, /*index=5*/s32[]{:T(128)}) while((s32[]{:T(128)}, f32[16,2,8248]{2,1,0:T(2,128)S(1)}, s32[16,3]{0,1:T(4,128)S(1)}, f32[16,2,8200]{2,0,1:T(8,128)S(1)}, s32[]{:T(128)}, /*index=5*/s32[]{:T(128)}) %tuple.326), condition=%wide.while_cond.8, body=%wide.while_body.8.sunk | while | flops 2 | bytes 393733 | solution.py:157
  838.3 3.6 add_bitcast_fusion.6
  842.0 4.0 multiply_subtract_fusion.6
  (1236 shorter events, 747.2 us)
Async XLA Ops:
  0.0 6.0 copy-start.5
  0.0 9.9 %copy-start.38 = (f32[2,128]{1,0:T(2,128)S(1)}, f32[2,128]{1,0:T(2,128)}, u32[]{:S(2)}) copy-start(f32[2,128]{1,0:T(2,128)} %param.20) | copy-start | bytes 3076
  0.7 36.0 %collective-permute-start = (bf16[8,2,128]{2,1,0:T(2,128)(2,1)S(1)}, bf16[8,2,128]{2,1,0:T(2,128)(2,1)S(1)}, u32[]{:S(2)}, u32[]{:S(2)}) collective-permute-start(bf16[8,2,128]{2,1,0:T(2,128)(2,1)S(1)} %slice_bitcast_fusion), channel_id=1, source_target_pairs={} | collective-permute-start | bytes 12296 | tf_op jit(solution)/shard_map/ppermute | solution.py:21
  6.0 4.5 copy-start.10
  6.0 5.8 copy-start.11
  7.4 4.4 copy-start.12
  7.4 4.4 copy-start.13
  9.9 26.8 %copy-start = (bf16[8,64,2,128]{3,2,1,0:T(2,128)(2,1)S(1)}, bf16[8,64,2,128]{3,2,1,0:T(2,128)(2,1)}, u32[]{:S(2)}) copy-start(bf16[8,64,2,128]{3,2,1,0:T(2,128)(2,1)} %param.19) | copy-start | bytes 786436
  9.9 26.8 %slice-start = ((bf16[8,64,2,128]{3,2,1,0:T(2,128)(2,1)}), bf16[8,63,2,128]{3,2,1,0:T(2,128)(2,1)S(1)}, s32[]{:S(2)}) async-start(bf16[8,64,2,128]{3,2,1,0:T(2,128)(2,1)} %param.19), calls=%async_computation | async-start | bytes 516096 | tf_op jit(solution)/shard_map/slice | solution.py:73
  38.7 10.5 %collective-permute-start.1 = (bf16[8,2,136]{2,1,0:T(2,128)(2,1)S(1)}, bf16[8,2,136]{2,1,0:T(2,128)(2,1)S(1)}, u32[]{:S(2)}, u32[]{:S(2)}) collective-permute-start(bf16[8,2,136]{2,1,0:T(2,128)(2,1)S(1)} %get-tuple-element.360), channel_id=1, source_target_pairs={} | collective-permute-start | bytes 13064 | tf_op jit(solution)/shard_map/ppermute | solution.py:29
  39.4 9.8 %collective-permute-start.2 = (bf16[8,2,136]{2,1,0:T(2,128)(2,1)S(1)}, bf16[8,2,136]{2,1,0:T(2,128)(2,1)S(1)}, u32[]{:S(2)}, u32[]{:S(2)}) collective-permute-start(bf16[8,2,136]{2,1,0:T(2,128)(2,1)S(1)} %get-tuple-element.359), channel_id=1, source_target_pairs={} | collective-permute-start | bytes 13064 | tf_op jit(solution)/shard_map/ppermute | solution.py:32
  324.6 63.5 %collective-permute-start.3 = (f32[2,16,8416]{2,1,0:T(8,128)}, f32[2,16,8416]{2,1,0:T(8,128)}, u32[]{:S(2)}, u32[]{:S(2)}) collective-permute-start(f32[2,16,8416]{2,1,0:T(8,128)} %multiply_multiply_fusion), channel_id=1, source_target_pairs={{0,1},{1,0},{2,3},{3,2},{4,5},{5,4},{6,7},{7,6},{8,9},{9,8},{10,11... | collective-permute-start | bytes 3231752 | tf_op jit(solution)/shard_map/ppermute | solution.py:44
  461.7 3.7 copy-start.22
  465.4 4.2 copy-start.2
  469.7 63.2 %collective-permute-start.4 = (f32[2,16,8360]{2,1,0:T(8,128)S(1)}, f32[2,16,8360]{2,1,0:T(8,128)}, u32[]{:S(2)}, u32[]{:S(2)}) collective-permute-start(f32[2,16,8360]{2,1,0:T(8,128)S(1)} %fusion.6), channel_id=1, source_target_pairs={{0,2},{2,0},{1,3},{3,1},{4,6},{6,4},{5,7},{7,5},{8,10},{10,8},{9,1... | collective-permute-start | bytes 3210248 | tf_op jit(solution)/shard_map/ppermute | solution.py:44
  587.8 3.7 copy-start.18
  587.8 3.7 copy-start.19
  587.8 3.7 copy-start.20
  587.8 3.7 copy-start.21
  591.5 4.1 copy-start.1
  595.8 58.7 %collective-permute-start.5 = (f32[2,16,8304]{2,1,0:T(8,128)S(1)}, f32[2,16,8304]{2,1,0:T(8,128)}, u32[]{:S(2)}, u32[]{:S(2)}) collective-permute-start(f32[2,16,8304]{2,1,0:T(8,128)S(1)} %fusion.7), channel_id=1, source_target_pairs={{0,4},{4,0},{1,5},{5,1},{2,6},{6,2},{3,7},{7,3},{8,12},{12,8},{9,1... | collective-permute-start | bytes 3188744 | tf_op jit(solution)/shard_map/ppermute | solution.py:44
  710.9 3.8 copy-start.14
  711.0 3.8 copy-start.15
  711.0 3.8 copy-start.16
  711.0 3.8 copy-start.17
  719.1 62.7 %collective-permute-start.6 = (f32[2,16,8248]{2,1,0:T(8,128)S(1)}, f32[2,16,8248]{2,1,0:T(8,128)}, u32[]{:S(2)}, u32[]{:S(2)}) collective-permute-start(f32[2,16,8248]{2,1,0:T(8,128)S(1)} %fusion.8), channel_id=1, source_target_pairs={{0,8},{8,0},{1,9},{9,1},{2,10},{10,2},{3,11},{11,3},{4,12},{12,4},... | collective-permute-start | bytes 3167240 | tf_op jit(solution)/shard_map/ppermute | solution.py:44
  838.3 3.7 copy-start.4
  838.3 3.7 copy-start.34
  838.3 3.7 copy-start.35
  838.3 3.7 copy-start.36
  838.3 3.7 copy-start.37
  842.0 4.1 copy-start.3
  (20 other events, 37.5 us)
where the time goes:
time: 860 us; the launch traced here: 848 us
  local copies, waits for them, and re-layouts  725 us (84%)
  other arithmetic  79.5 us (9%)
  between operations  22 us (3%)
  loops' own time  9.77 us (1%)
  starting transfers between devices  9.46 us (1%)
    gather x1024, local copies, waits for them, and re-layouts  681 us
    add x8, other arithmetic, merge_side(): summed + weights[tap_index] * lax.dynamic_slice_in_dim(windows, tap_start...  29.3 us
  transfers between devices with their start and end apart: 7, of which 0 were waited for; matrix products, arithmetic and copies ran while one was open for 31% of the time, Pallas kernels for 0%

commit v1 on v0

--- a/solution.py
+++ b/solution.py
@@ -1,18 +1,370 @@
+import functools
 import math
 
 import jax
 import jax.numpy as jnp
+import numpy as np
 from jax import lax
+from jax.experimental import pallas as pl
+from jax.experimental.pallas import tpu as pltpu
 from jax.sharding import PartitionSpec as P
 
-R = 8192
-BLOCK = 256
-LEVELS = 4
+SPREAD = 4
 SHIFT = 24
-SPREAD = 4
-
-
+HALO = 32
+LANES = 128
+HALF = 64
 SQRT_HALF = 0.7071067811865476
+VMEM_LIMIT = 24 * 2**20
+
+COS_COEFFS = (
+    1.0,
+    -19.73920440673828,
+    64.93911743164062,
+    -85.45014190673828,
+    60.16762924194336,
+    -25.967599868774414,
+    6.528658390045166,
+)
+SIN_COEFFS = (
+    6.2831854820251465,
+    -41.34170150756836,
+    81.60513305664062,
+    -76.70301818847656,
+    42.02592849731445,
+    -14.899847030639648,
+    3.2381374835968018,
+)
+
+SMEM_SPEC = pl.BlockSpec(memory_space=pltpu.SMEM)
+VMEM_SPEC = pl.BlockSpec(memory_space=pltpu.VMEM)
+
+
+def cos_sin_turns(turns):
+    f = turns - jnp.round(turns)
+    u = f * f
+    c = jnp.full_like(u, COS_COEFFS[-1])
+    for a in COS_COEFFS[-2::-1]:
+        c = c * u + a
+    s = jnp.full_like(u, SIN_COEFFS[-1])
+    for a in SIN_COEFFS[-2::-1]:
+        s = s * u + a
+    return c, s * f
+
+
+def lane_iota(rows):
+    return lax.broadcasted_iota(jnp.int32, (rows, LANES), 1)
+
+
+def store_extended(ext_ref, where, low, high, body):
+    lane = lane_iota(HALO)
+    ext_ref[(*where, pl.ds(HALO, HALF))] = body
+    after = jnp.where(lane < HALF, pltpu.roll(high, HALF, 1), pltpu.roll(high, HALF - 1, 1))
+    ext_ref[(*where, pl.ds(HALO + HALF, HALO))] = jnp.where(lane == LANES - 1, 0.0, after)
+    before = jnp.where(lane < HALF, pltpu.roll(low, HALF + 1, 1), pltpu.roll(low, HALF, 1))
+    ext_ref[(*where, pl.ds(0, HALO))] = jnp.where(lane == 0, 0.0, before)
+
+
+def front_kernel(
+    index_ref, raw_ref, matched_ref, delays_ref, phase_ref, image_ref, send_ref,
+    raw32, taps, windows, ext, trig, trig_smem, sem,
+):
+    pulses, beams = phase_ref.shape
+    rows = raw_ref.shape[0] // 2
+    blocks = rows // pulses
+    side_bit = index_ref[0] % 2
+    scale = 1.0 / math.sqrt(pulses)
+    c, s = cos_sin_turns(phase_ref[...] * (0.5 / math.pi))
+    trig[0] = c * scale
+    trig[1] = s * scale
+    copy = pltpu.make_async_copy(trig, trig_smem, sem)
+    copy.start()
+    raw32[0:16] = jnp.zeros((16, LANES), jnp.float32)
+    raw32[16 : 16 + 2 * rows] = raw_ref[...].astype(jnp.float32)
+    first = lax.broadcasted_iota(jnp.int32, (rows, LANES), 0) % blocks == 0
+    for part in range(2):
+        previous = raw32[pl.ds(14 + part, rows, stride=2), :]
+        windows[:, part * LANES : (part + 1) * LANES] = jnp.where(first, 0.0, previous).astype(jnp.bfloat16)
+        current = raw32[pl.ds(16 + part, rows, stride=2), :]
+        windows[:, (2 + part) * LANES : (3 + part) * LANES] = current.astype(jnp.bfloat16)
+    row = lax.broadcasted_iota(jnp.int32, (LANES, LANES), 0)
+    column = lax.broadcasted_iota(jnp.int32, (LANES, LANES), 1)
+    for part in range(2):
+        line = jnp.broadcast_to(matched_ref[part : part + 1, :], (LANES, LANES))
+        circulant = pltpu.roll(line, 0, 1, stride=1, stride_axis=0).T
+        now = jnp.where(column <= row, circulant, 0.0).astype(jnp.bfloat16)
+        before = jnp.where(column > row, circulant, 0.0).astype(jnp.bfloat16)
+        if part == 0:
+            taps[0:LANES, 0:LANES] = before
+            taps[LANES:, LANES : 2 * LANES] = before
+            taps[0:LANES, 2 * LANES : 3 * LANES] = now
+            taps[LANES:, 3 * LANES :] = now
+        else:
+            taps[0:LANES, LANES : 2 * LANES] = -before
+            taps[LANES:, 0:LANES] = before
+            taps[0:LANES, 3 * LANES :] = -now
+            taps[LANES:, 2 * LANES : 3 * LANES] = now
+    lane = lane_iota(HALF)
+    for pair in range(rows // LANES):
+        made = lax.dot_general(
+            taps[...],
+            windows[pair * LANES : (pair + 1) * LANES, :],
+            (((1,), (1,)), ((), ())),
+            preferred_element_type=jnp.float32,
+        )
+        for part in range(2):
+            a = made[part * LANES : part * LANES + HALF]
+            b = made[part * LANES + HALF : (part + 1) * LANES]
+            even = jnp.where(lane < HALF, a, pltpu.roll(b, HALF, 1))
+            odd = jnp.where(lane < HALF, pltpu.roll(a, HALF, 1), b)
+            for which, body in ((0, even), (1, odd)):
+                store_extended(ext, (2 * pair + which, part), body[HALF - HALO :], body[:HALO], body)
+    copy.wait()
+    send_first = (1 - side_bit) * 7
+
+    def beam(k, carry):
+        for piece in range(HALF // 32):
+            real = jnp.zeros((32, LANES), jnp.float32)
+            imag = jnp.zeros((32, LANES), jnp.float32)
+            for p in range(pulses):
+                start = delays_ref[p, k] + (HALO + piece * 32)
+                x = ext[p, 0, pl.ds(start, 32), :]
+                y = ext[p, 1, pl.ds(start, 32), :]
+                cosine = trig_smem[0, p, k]
+                sine = trig_smem[1, p, k]
+                real = real + (x * cosine - y * sine)
+                imag = imag + (x * sine + y * cosine)
+            image_ref[k, 0, pl.ds(piece * 32, 32)] = real
+            image_ref[k, 1, pl.ds(piece * 32, 32)] = imag
+            slot = k - send_first
+
+            @pl.when((slot >= 0) & (slot < send_ref.shape[0]))
+            def _():
+                send_ref[slot, 0, pl.ds(piece * 32, 32)] = real.astype(jnp.bfloat16)
+                send_ref[slot, 1, pl.ds(piece * 32, 32)] = imag.astype(jnp.bfloat16)
+
+        return carry
+
+    lax.fori_loop(0, beams, beam, 0)
+
+
+def tap_factors(taps_ref, level):
+    count = taps_ref.shape[1]
+    offsets = [taps_ref[level, t] for t in range(count)]
+    weights = [(SPREAD + 1.0) - jnp.abs(o).astype(jnp.float32) for o in offsets]
+    return offsets, weights
+
+
+def filtered(ext, slot, part, start, offsets, weights):
+    total = None
+    for offset, weight in zip(offsets, weights):
+        term = ext[slot, part, pl.ds(start + offset, HALF), :] * weight
+        total = term if total is None else total + term
+    return total
+
+
+def cells():
+    t = lax.broadcasted_iota(jnp.int32, (HALF, LANES), 0)
+    lane = lane_iota(HALF)
+    return (t + (lane % HALF) * LANES + (lane // HALF) * HALF).astype(jnp.float32)
+
+
+def own_kernel(
+    level, bins, index_ref, beam_ref, shift_ref, base_ref, rate_ref, taps_ref, image_ref, partial_ref, turn_ref, ext,
+):
+    side_bit = (index_ref[0] >> level) % 2
+    beams = image_ref.shape[0]
+    low_beam = side_bit * 7
+
+    def extend(slot, carry):
+        for part in range(2):
+            body = image_ref[low_beam + slot, part]
+            store_extended(ext, (slot, part), body[HALF - HALO :], body[:HALO], body)
+        return carry
+
+    lax.fori_loop(0, ext.shape[0], extend, 0)
+    offsets, weights = tap_factors(taps_ref, level)
+    position = cells() * (1.0 / bins)
+
+    def beam(k, carry):
+        own = (level, side_bit, side_bit, k)
+        other = (level, side_bit, 1 - side_bit, k)
+        slot = beam_ref[own] - low_beam
+        start = shift_ref[own] + HALO
+        real = filtered(ext, slot, 0, start, offsets, weights)
+        imag = filtered(ext, slot, 1, start, offsets, weights)
+        c, s = cos_sin_turns(position * rate_ref[own] + base_ref[own] * (0.5 / math.pi))
+        partial_ref[k, 0] = real * c - imag * s
+        partial_ref[k, 1] = real * s + imag * c
+        c, s = cos_sin_turns(position * rate_ref[other] + base_ref[other] * (0.5 / math.pi))
+        turn_ref[k, 0] = c
+        turn_ref[k, 1] = s
+        return carry
+
+    lax.fori_loop(0, beams, beam, 0)
+
+
+def merged(level, side_bit, k, scale, beam_ref, shift_ref, offsets, weights, ext, partial_ref, turn_ref):
+    other = (level, side_bit, 1 - side_bit, k)
+    slot = beam_ref[other] - side_bit * 7
+    start = shift_ref[other] + HALO
+    real = filtered(ext, slot, 0, start, offsets, weights)
+    imag = filtered(ext, slot, 1, start, offsets, weights)
+    c = turn_ref[k, 0]
+    s = turn_ref[k, 1]
+    return (
+        (real * c - imag * s + partial_ref[k, 0]) * scale,
+        (real * s + imag * c + partial_ref[k, 1]) * scale,
+    )
+
+
+def extend_received(received_ref, ext):
+    def extend(slot, carry):
+        for part in range(2):
+            body = received_ref[slot, part].astype(jnp.float32)
+            store_extended(ext, (slot, part), body[HALF - HALO :], body[:HALO], body)
+        return carry
+
+    lax.fori_loop(0, ext.shape[0], extend, 0)
+
+
+def total_scale(weights):
+    total = weights[0]
+    for w in weights[1:]:
+        total = total + w
+    return SQRT_HALF / total
+
+
+def middle_kernel(
+    level, index_ref, beam_ref, shift_ref, taps_ref, received_ref, partial_ref, turn_ref, image_ref, send_ref, ext,
+):
+    side_bit = (index_ref[0] >> level) % 2
+    next_bit = (index_ref[0] >> (level + 1)) % 2
+    send_first = (1 - next_bit) * 7
+    extend_received(received_ref, ext)
+    offsets, weights = tap_factors(taps_ref, level)
+    scale = total_scale(weights)
+
+    def beam(k, carry):
+        real, imag = merged(
+            level, side_bit, k, scale, beam_ref, shift_ref, offsets, weights, ext, partial_ref, turn_ref
+        )
+        image_ref[k, 0] = real
+        image_ref[k, 1] = imag
+        slot = k - send_first
+
+        @pl.when((slot >= 0) & (slot < send_ref.shape[0]))
+        def _():
+            send_ref[slot, 0] = real.astype(jnp.bfloat16)
+            send_ref[slot, 1] = imag.astype(jnp.bfloat16)
+
+        return carry
+
+    lax.fori_loop(0, image_ref.shape[0], beam, 0)
+
+
+def last_kernel(
+    level, index_ref, beam_ref, shift_ref, taps_ref, received_ref, partial_ref, turn_ref, out_ref, ext,
+):
+    side_bit = (index_ref[0] >> level) % 2
+    extend_received(received_ref, ext)
+    offsets, weights = tap_factors(taps_ref, level)
+    scale = total_scale(weights)
+    lane = lane_iota(HALF)
+
+    def pair(m, carry):
+        even = merged(
+            level, side_bit, 2 * m, scale, beam_ref, shift_ref, offsets, weights, ext, partial_ref, turn_ref
+        )
+        odd = merged(
+            level, side_bit, 2 * m + 1, scale, beam_ref, shift_ref, offsets, weights, ext, partial_ref, turn_ref
+        )
+        high, low = m // 4, 2 * (m % 4)
+        for part in range(2):
+            turned = jnp.concatenate([even[part], odd[part]], axis=0).T
+            a = turned[:HALF]
+            b = turned[HALF:]
+            out_ref[part, high, pl.ds(low, HALF, stride=8), :] = jnp.where(lane < HALF, a, pltpu.roll(b, HALF, 1))
+            out_ref[part, high, pl.ds(low + 1, HALF, stride=8), :] = jnp.where(lane < HALF, pltpu.roll(a, HALF, 1), b)
+        return carry
+
+    lax.fori_loop(0, partial_ref.shape[0] // 2, pair, 0)
+
+
+def params():
+    return pltpu.CompilerParams(vmem_limit_bytes=VMEM_LIMIT)
+
+
+def route(axis, bit):
+    count = lax.axis_size(axis)
+    return [(i, i ^ (1 << bit)) for i in range(count) if i ^ (1 << bit) < count]
+
+
+def local(raw_echoes, matched, delays, pulse_phase, beam_map, range_shift, phase_base, phase_rate, tap_offsets):
+    pulses, blocks, parts, hop = raw_echoes.shape
+    beams = delays.shape[1]
+    levels = tap_offsets.shape[0]
+    bins = blocks * hop
+    slots = beams // 2 + 1
+    index = lax.axis_index("pulse").astype(jnp.int32).reshape(1)
+    f32, bf16 = jnp.float32, jnp.bfloat16
+    image_shape = jax.ShapeDtypeStruct((beams, 2, HALF, LANES), f32)
+    send_shape = jax.ShapeDtypeStruct((slots, 2, HALF, LANES), bf16)
+    ext_scratch = pltpu.VMEM((slots, 2, HALF + 2 * HALO, LANES), f32)
+    rows = pulses * blocks
+    image, send = pl.pallas_call(
+        front_kernel,
+        out_shape=(image_shape, send_shape),
+        in_specs=[SMEM_SPEC, VMEM_SPEC, VMEM_SPEC, SMEM_SPEC, VMEM_SPEC],
+        out_specs=(VMEM_SPEC, VMEM_SPEC),
+        scratch_shapes=[
+            pltpu.VMEM((16 + 2 * rows, LANES), f32),
+            pltpu.VMEM((2 * LANES, 4 * LANES), bf16),
+            pltpu.VMEM((rows, 4 * LANES), bf16),
+            pltpu.VMEM((pulses, 2, HALF + 2 * HALO, LANES), f32),
+            pltpu.VMEM((2, pulses, beams), f32),
+            pltpu.SMEM((2, pulses, beams), f32),
+            pltpu.SemaphoreType.DMA,
+        ],
+        compiler_params=params(),
+        name="front",
+    )(index, raw_echoes.reshape(pulses * blocks * parts, hop), matched, delays, pulse_phase)
+    for level in range(levels):
+        received = lax.ppermute(send, "pulse", route("pulse", level))
+        partial, turn = pl.pallas_call(
+            functools.partial(own_kernel, level, bins),
+            out_shape=(image_shape, image_shape),
+            in_specs=[SMEM_SPEC] * 6 + [VMEM_SPEC],
+            out_specs=(VMEM_SPEC, VMEM_SPEC),
+            scratch_shapes=[ext_scratch],
+            compiler_params=params(),
+            cost_estimate=pl.CostEstimate(flops=4 * 10**6, bytes_accessed=3 * 2**20, transcendentals=0),
+            name=f"own{level}",
+        )(index, beam_map, range_shift, phase_base, phase_rate, tap_offsets, image)
+        operands = (index, beam_map, range_shift, tap_offsets, received, partial, turn)
+        in_specs = [SMEM_SPEC] * 4 + [VMEM_SPEC] * 3
+        if level < levels - 1:
+            image, send = pl.pallas_call(
+                functools.partial(middle_kernel, level),
+                out_shape=(image_shape, send_shape),
+                in_specs=in_specs,
+                out_specs=(VMEM_SPEC, VMEM_SPEC),
+                scratch_shapes=[ext_scratch],
+                compiler_params=params(),
+                name=f"middle{level}",
+            )(*operands)
+        else:
+            out = pl.pallas_call(
+                functools.partial(last_kernel, level),
+                out_shape=jax.ShapeDtypeStruct((2, beams // 8, HALF * 8, LANES), f32),
+                in_specs=in_specs,
+                out_specs=VMEM_SPEC,
+                scratch_shapes=[ext_scratch],
+                compiler_params=params(),
+                name="last",
+            )(*operands)
+    out = out.reshape(2, beams // 8, HALF, 8, LANES)
+    return jnp.transpose(out, (0, 1, 3, 2, 4)).reshape(2, beams, bins)
 
 
 def shifted(array, axis, by):
@@ -93,9 +445,9 @@
     return jnp.concatenate([inverse[:, half:length], inverse[:, length + half :]], axis=1)
 
 
-def inside_mask(first_cell, out_cells):
+def inside_mask(first_cell, out_cells, bins):
     global_cells = first_cell + jnp.arange(out_cells, dtype=jnp.int32)
-    return ((global_cells >= 0) & (global_cells < R)).astype(jnp.float32)
+    return ((global_cells >= 0) & (global_cells < bins)).astype(jnp.float32)
 
 
 def row_slices(rows, starts, width):
@@ -106,7 +458,7 @@
     return jax.vmap(per_pulse)(rows, starts)
 
 
-def project(padded, delay_rows, phase_rows, offset_base, out_cells, first_cell):
+def project(padded, delay_rows, phase_rows, offset_base, out_cells, first_cell, bins):
     pulses = padded.shape[0]
     beam_count = delay_rows.shape[1]
     group_size = math.gcd(pulses, 4)
@@ -130,7 +482,7 @@
         jnp.zeros((2, beam_count, out_cells), jnp.float32),
         jnp.arange(block_count, dtype=jnp.int32),
     )
-    return summed * inside_mask(first_cell, out_cells) * (1.0 / math.sqrt(pulses))
+    return summed * inside_mask(first_cell, out_cells, bins) * (1.0 / math.sqrt(pulses))
 
 
 def tap_weights(tap_values):
@@ -149,15 +501,14 @@
     offset_base,
     out_cells,
     first_cell,
+    bins,
 ):
-    picked = jnp.take(source, beam_rows, axis=1)
     span = out_cells + 2 * SPREAD
     starts = offsets + offset_base - SPREAD
     windows = jax.vmap(
-        lambda beam_data, start: lax.dynamic_slice_in_dim(beam_data, start, span, 1),
-        in_axes=(1, 0),
+        lambda beam, start: lax.dynamic_slice(source, (0, beam, start), (2, 1, span))[:, 0],
         out_axes=1,
-    )(picked, starts)
+    )(beam_rows, starts)
     summed = jnp.zeros((2, beam_rows.shape[0], out_cells), jnp.float32)
     for tap_index in range(tap_values.shape[0]):
         tap_start = tap_values[tap_index] + SPREAD
@@ -167,7 +518,7 @@
     positions = jnp.arange(out_cells, dtype=jnp.int32)
     global_cells = (first_cell + positions).astype(jnp.float32)
     angle_grid = (
-        phase_zero[:, None] + 2.0 * math.pi / R * phase_slope[:, None] * global_cells[None, :]
+        phase_zero[:, None] + 2.0 * math.pi / bins * phase_slope[:, None] * global_cells[None, :]
     )
     cosine = jnp.cos(angle_grid)
     sine_part = jnp.sin(angle_grid)
@@ -183,7 +534,7 @@
     return (own_rows, other_rows)
 
 
-def local(
+def local_split(
     raw_echoes,
     matched,
     delays,
@@ -197,15 +548,18 @@
     pulses = raw_echoes.shape[0]
     hop_bins = raw_echoes.shape[3]
     local_cells = raw_echoes.shape[1] * hop_bins
-    forward_exact, inverse_exact = tables(BLOCK)
+    bins = local_cells * lax.axis_size("rng")
+    length = 2 * hop_bins
+    levels = tap_offsets.shape[0]
+    forward_exact, inverse_exact = tables(length)
     forward = forward_exact.astype(jnp.bfloat16)
-    inverse_kept = kept_columns(inverse_exact.astype(jnp.bfloat16), BLOCK)
+    inverse_kept = kept_columns(inverse_exact.astype(jnp.bfloat16), length)
     tail = shifted(raw_echoes[:, -1], "rng", 1)
     compressed = compress(raw_echoes, tail, matched, forward_exact, forward, inverse_kept)
     compressed = jnp.transpose(compressed, (0, 2, 1, 3)).reshape(pulses, 2, local_cells)
     first_cell = lax.axis_index("rng") * local_cells
     rim_cells = SHIFT + SPREAD
-    margin_cells = LEVELS * rim_cells
+    margin_cells = levels * rim_cells
     padded = padded_2(compressed, (("rng", 2),), SHIFT + margin_cells)
     polar_image = project(
         padded,
@@ -214,9 +568,10 @@
         SHIFT,
         local_cells + 2 * margin_cells,
         first_cell - margin_cells,
+        bins,
     )
     pulse_index = lax.axis_index("pulse")
-    for level_index in range(LEVELS):
+    for level_index in range(levels):
         side_bit = pulse_index // 2**level_index % 2
         own_beams, other_beams = pick_sides(beam_map, level_index, side_bit)
         own_offsets, other_offsets = pick_sides(range_shift, level_index, side_bit)
@@ -240,6 +595,7 @@
             rim_cells,
             out_cells,
             start_cell,
+            bins,
         )
         other_side = merge_side(
             received,
@@ -252,8 +608,9 @@
             rim_cells,
             out_cells,
             start_cell,
-        )
-        polar_image = (own_side + other_side) * SQRT_HALF * inside_mask(start_cell, out_cells)
+            bins,
+        )
+        polar_image = (own_side + other_side) * SQRT_HALF * inside_mask(start_cell, out_cells, bins)
     return polar_image
 
 
@@ -270,4 +627,5 @@
         P(),
     )
     out_specs = P(None, ("grp", "pulse"), "rng")
-    return jax.shard_map(local, mesh=mesh, in_specs=in_specs, out_specs=out_specs, check_vma=False)
+    whole_range = mesh.shape["rng"] == 1
+    return jax.shard_map(local if whole_range else local_split, mesh=mesh, in_specs=in_specs, out_specs=out_specs, check_vma=False)

time: 860 us -> 54.9 us (0.06); the launches traced: 848 us -> 54.7 us
  local copies, waits for them, and re-layouts: 725 us -> 1.82 us
  other arithmetic: 79.5 us -> 0 us
  Pallas kernels: 0 us -> 30.3 us
  between operations: 22 us -> 0.09 us
  waiting for transfers between devices: 0.02 us -> 14.5 us
  loops' own time: 9.77 us -> 0 us
    gather x1034 -> x0, local copies, waits for them, and re-layouts: 696 us -> none
    add x14 -> x0, other arithmetic: 32.3 us -> none  [the longest x8 29.3 us: merge_side(): summed + weights[tap_index] * lax.dynamic_slice_in_dim(windows, tap_start...]
    pallas_call x0 -> x9, Pallas kernels: none -> 30.3 us  [the longest x4 14.7 us: local(): pl.pallas_call(functools.partial(own_kernel, level, bins), out_shape=(ima...]
    sub x4 -> x0, other arithmetic: 16.4 us -> none  [merge_side(): summed[0] * cosine - summed[1] * sine_part]
    ppermute x7 -> x4, waiting for transfers between devices: 0.02 us -> 14.5 us  [local(): received = lax.ppermute(send, 'pulse', route('pulse', level))]
    another operation x11 -> x0, loops' own time: 9.77 us -> none  [the longest x8 6.05 us: merge_side(): lax.dynamic_slice_in_dim(beam_data, start, span, 1)]
  transfers between devices with their start and end apart: 7 -> 4, of which waited for: 0 -> 3; matrix products, arithmetic and copies ran while one was open for 31% -> 0% of each run, Pallas kernels for 0% -> 27%
where the time goes in v1:
time: 54.9 us; the launch traced here: 54.7 us
  Pallas kernels  30.3 us (55%)
  waiting for transfers between devices  14.5 us (26%)
  starting transfers between devices  7.99 us (15%)
  local copies, waits for them, and re-layouts  1.82 us (3%)
    pallas_call x4, Pallas kernels, local(): pl.pallas_call(functools.partial(own_kernel, level, bins), out_shape=(ima...  14.7 us
    ppermute x4, waiting for transfers between devices, local(): received = lax.ppermute(send, 'pulse', route('pulse', level))  14.5 us
    ppermute x4, starting transfers between devices, local(): received = lax.ppermute(send, 'pulse', route('pulse', level))  7.99 us
    pallas_call x3, Pallas kernels, local(): pl.pallas_call(functools.partial(middle_kernel, level), out_shape=(image_...  7.33 us
    pallas_call x1, Pallas kernels, local(): pl.pallas_call(functools.partial(last_kernel, level), out_shape=jax.Shape...  4.41 us
    pallas_call x1, Pallas kernels, local(): pl.pallas_call(front_kernel, out_shape=(image_shape, send_shape), in_spec...  3.79 us
    unnamed x18, local copies, waits for them, and re-layouts  1.82 us
  transfers between devices with their start and end apart: 4, of which 3 were waited for; matrix products, arithmetic and copies ran while one was open for 0% of the time, Pallas kernels for 27%

profile of v1, /device:TPU:0, one launch (start us, length us, event | category | flops | bytes accessed | tf_op | source)
XLA Modules:
  0.0 54.7 jit_solution(6864776386317211109)
XLA Ops:
  0.0 0.0 copy-start.7
  0.0 0.0 copy-start.6
  0.0 0.0 copy-start.8
  0.0 0.7 %copy-done.7 = f32[8,16]{1,0:T(8,128)S(1)} copy-done((f32[8,16]{1,0:T(8,128)S(1)}, f32[8,16]{1,0:T(8,128)}, u32[]{:S(2)}) %copy-start.7) | copy-done | bytes 536
  0.7 0.0 copy-done.6
  0.7 0.0 copy-done.8
  0.7 0.0 copy-start.2
  0.7 0.9 %copy-done.2 = bf16[8,64,2,128]{3,2,1,0:T(2,128)(2,1)S(1)} copy-done((bf16[8,64,2,128]{3,2,1,0:T(2,128)(2,1)S(1)}, bf16[8,64,2,128]{3,2,1,0:T(2,128)(2,1)}, u32[]{:S(2)}) %copy-start.2) | copy-done | bytes 262168
  1.7 0.0 copy-start.1
  1.7 3.8 %front.1 = (f32[16,2,64,128]{3,2,1,0:T(8,128)S(1)}, bf16[9,2,64,128]{3,2,1,0:T(8,128)(2,1)S(1)}) custom-call(s32[1]{0:T(128)} %bitcast.index_ref, bf16[1024,128]{1,0:T(8,128)(2,1)S(1)} %bitcast.7, f32[2,128]{1,0:T(2,128)S(1)} %copy-done.8, s32[8,16]{1,0:T(8,128)S(1)} %copy-done.6, f32[8,16]{1,0:T(8,128)S(1)} %copy-done.7), custom_call_target="tpu_custom_call" | custom-call | tf_op jit(solution)/shard_map/front/pallas_call | solution.py:315
  5.5 0.0 copy-start.5
  5.5 0.5 collective-permute-start
  6.0 0.0 copy-done
  6.0 0.0 copy-done.1
  6.0 0.0 copy-done.3
  6.0 0.0 copy-done.4
  6.0 0.1 copy-done.5
  6.2 3.7 %own0.1 = (f32[16,2,64,128]{3,2,1,0:T(8,128)S(1)}, f32[16,2,64,128]{3,2,1,0:T(8,128)S(1)}) custom-call(s32[1]{0:T(128)} %bitcast.index_ref, s32[4,2,2,16]{3,2,1,0:T(2,128)S(1)} %copy-done, s32[4,2,2,16]{3,2,1,0:T(2,128)S(1)} %copy-done.1, f32[4,2,2,16]{3,2,1,0:T(2,128)S(1)} %copy-done.3, f32[4,2,2,16]{3,2,1,0:T(2,128)S(1)} %copy-done.4, ...), custom_call_target="tpu_custom_call" | custom-call | flops 4000000 | bytes 3145728 | tf_op jit(solution)/shard_map/own0/pallas_call | solution.py:334
  9.8 0.0 collective-permute-done.received_ref
  9.9 2.5 %middle0.1 = (f32[16,2,64,128]{3,2,1,0:T(8,128)S(1)}, bf16[9,2,64,128]{3,2,1,0:T(8,128)(2,1)S(1)}) custom-call(s32[1]{0:T(128)} %bitcast.index_ref, s32[4,2,2,16]{3,2,1,0:T(2,128)S(1)} %copy-done, s32[4,2,2,16]{3,2,1,0:T(2,128)S(1)} %copy-done.1, s32[4,4]{1,0:T(4,128)S(1)} %copy-done.5, bf16[9,2,64,128]{3,2,1,0:T(8,128)(2,1)S(1)} %collective-permute-done.received_ref, ...), custom_call_target="tpu_custom_call" | custom-call | tf_op jit(solution)/shard_map/middle0/pallas_call | solution.py:347
  12.3 3.0 %collective-permute-start.1 = (bf16[9,2,64,128]{3,2,1,0:T(8,128)(2,1)S(1)}, bf16[9,2,64,128]{3,2,1,0:T(8,128)(2,1)S(1)}, u32[]{:S(2)}, u32[]{:S(2)}) collective-permute-start(bf16[9,2,64,128]{3,2,1,0:T(8,128)(2,1)S(1)} %get-tuple-element.25), channel_id=1, source_target_pairs={{0,2},{1,3},{2,0},{3,1},{4,6},{5,7},{6,4},{7,5},{8,10},{9,11},{10,... | collective-permute-start | bytes 884744 | tf_op jit(solution)/shard_map/ppermute | solution.py:333
  15.3 3.7 %own1.1 = (f32[16,2,64,128]{3,2,1,0:T(8,128)S(1)}, f32[16,2,64,128]{3,2,1,0:T(8,128)S(1)}) custom-call(s32[1]{0:T(128)} %bitcast.index_ref, s32[4,2,2,16]{3,2,1,0:T(2,128)S(1)} %copy-done, s32[4,2,2,16]{3,2,1,0:T(2,128)S(1)} %copy-done.1, f32[4,2,2,16]{3,2,1,0:T(2,128)S(1)} %copy-done.3, f32[4,2,2,16]{3,2,1,0:T(2,128)S(1)} %copy-done.4, ...), custom_call_target="tpu_custom_call" | custom-call | flops 4000000 | bytes 3145728 | tf_op jit(solution)/shard_map/own1/pallas_call | solution.py:334
  19.0 3.4 %collective-permute-done.1.received_ref = bf16[9,2,64,128]{3,2,1,0:T(8,128)(2,1)S(1)} collective-permute-done((bf16[9,2,64,128]{3,2,1,0:T(8,128)(2,1)S(1)}, bf16[9,2,64,128]{3,2,1,0:T(8,128)(2,1)S(1)}, u32[]{:S(2)}, u32[]{:S(2)}) %collective-permute-start.1) | collective-permute-done | bytes 294944 | tf_op jit(solution)/shard_map/ppermute | solution.py:333
  22.4 2.4 %middle1.1 = (f32[16,2,64,128]{3,2,1,0:T(8,128)S(1)}, bf16[9,2,64,128]{3,2,1,0:T(8,128)(2,1)S(1)}) custom-call(s32[1]{0:T(128)} %bitcast.index_ref, s32[4,2,2,16]{3,2,1,0:T(2,128)S(1)} %copy-done, s32[4,2,2,16]{3,2,1,0:T(2,128)S(1)} %copy-done.1, s32[4,4]{1,0:T(4,128)S(1)} %copy-done.5, bf16[9,2,64,128]{3,2,1,0:T(8,128)(2,1)S(1)} %collective-permute-done.1.received_ref, ...), custom_call_target="tpu_custom_call" | custom-call | tf_op jit(solution)/shard_map/middle1/pallas_call | solution.py:347
  24.9 1.9 %collective-permute-start.2 = (bf16[9,2,64,128]{3,2,1,0:T(8,128)(2,1)S(1)}, bf16[9,2,64,128]{3,2,1,0:T(8,128)(2,1)S(1)}, u32[]{:S(2)}, u32[]{:S(2)}) collective-permute-start(bf16[9,2,64,128]{3,2,1,0:T(8,128)(2,1)S(1)} %get-tuple-element.29), channel_id=1, source_target_pairs={{0,4},{1,5},{2,6},{3,7},{4,0},{5,1},{6,2},{7,3},{8,12},{9,13},{10,... | collective-permute-start | bytes 884744 | tf_op jit(solution)/shard_map/ppermute | solution.py:333
  26.7 3.7 %own2.1 = (f32[16,2,64,128]{3,2,1,0:T(8,128)S(1)}, f32[16,2,64,128]{3,2,1,0:T(8,128)S(1)}) custom-call(s32[1]{0:T(128)} %bitcast.index_ref, s32[4,2,2,16]{3,2,1,0:T(2,128)S(1)} %copy-done, s32[4,2,2,16]{3,2,1,0:T(2,128)S(1)} %copy-done.1, f32[4,2,2,16]{3,2,1,0:T(2,128)S(1)} %copy-done.3, f32[4,2,2,16]{3,2,1,0:T(2,128)S(1)} %copy-done.4, ...), custom_call_target="tpu_custom_call" | custom-call | flops 4000000 | bytes 3145728 | tf_op jit(solution)/shard_map/own2/pallas_call | solution.py:334
  30.4 2.8 %collective-permute-done.2.received_ref = bf16[9,2,64,128]{3,2,1,0:T(8,128)(2,1)S(1)} collective-permute-done((bf16[9,2,64,128]{3,2,1,0:T(8,128)(2,1)S(1)}, bf16[9,2,64,128]{3,2,1,0:T(8,128)(2,1)S(1)}, u32[]{:S(2)}, u32[]{:S(2)}) %collective-permute-start.2) | collective-permute-done | bytes 294944 | tf_op jit(solution)/shard_map/ppermute | solution.py:333
  33.2 2.4 %middle2.1 = (f32[16,2,64,128]{3,2,1,0:T(8,128)S(1)}, bf16[9,2,64,128]{3,2,1,0:T(8,128)(2,1)S(1)}) custom-call(s32[1]{0:T(128)} %bitcast.index_ref, s32[4,2,2,16]{3,2,1,0:T(2,128)S(1)} %copy-done, s32[4,2,2,16]{3,2,1,0:T(2,128)S(1)} %copy-done.1, s32[4,4]{1,0:T(4,128)S(1)} %copy-done.5, bf16[9,2,64,128]{3,2,1,0:T(8,128)(2,1)S(1)} %collective-permute-done.2.received_ref, ...), custom_call_target="tpu_custom_call" | custom-call | tf_op jit(solution)/shard_map/middle2/pallas_call | solution.py:347
  35.7 2.6 %collective-permute-start.3 = (bf16[9,2,64,128]{3,2,1,0:T(8,128)(2,1)S(1)}, bf16[9,2,64,128]{3,2,1,0:T(8,128)(2,1)S(1)}, u32[]{:S(2)}, u32[]{:S(2)}) collective-permute-start(bf16[9,2,64,128]{3,2,1,0:T(8,128)(2,1)S(1)} %get-tuple-element.33), channel_id=1, source_target_pairs={{0,8},{1,9},{2,10},{3,11},{4,12},{5,13},{6,14},{7,15},{8,0},{9,1},... | collective-permute-start | bytes 884744 | tf_op jit(solution)/shard_map/ppermute | solution.py:333
  38.2 3.7 %own3.1 = (f32[16,2,64,128]{3,2,1,0:T(8,128)S(1)}, f32[16,2,64,128]{3,2,1,0:T(8,128)S(1)}) custom-call(s32[1]{0:T(128)} %bitcast.index_ref, s32[4,2,2,16]{3,2,1,0:T(2,128)S(1)} %copy-done, s32[4,2,2,16]{3,2,1,0:T(2,128)S(1)} %copy-done.1, f32[4,2,2,16]{3,2,1,0:T(2,128)S(1)} %copy-done.3, f32[4,2,2,16]{3,2,1,0:T(2,128)S(1)} %copy-done.4, ...), custom_call_target="tpu_custom_call" | custom-call | flops 4000000 | bytes 3145728 | tf_op jit(solution)/shard_map/own3/pallas_call | solution.py:334
  41.9 8.4 %collective-permute-done.3.received_ref = bf16[9,2,64,128]{3,2,1,0:T(8,128)(2,1)S(1)} collective-permute-done((bf16[9,2,64,128]{3,2,1,0:T(8,128)(2,1)S(1)}, bf16[9,2,64,128]{3,2,1,0:T(8,128)(2,1)S(1)}, u32[]{:S(2)}, u32[]{:S(2)}) %collective-permute-start.3) | collective-permute-done | bytes 294944 | tf_op jit(solution)/shard_map/ppermute | solution.py:333
  50.3 4.4 %last.1 = f32[2,2,512,128]{3,2,1,0:T(8,128)} custom-call(s32[1]{0:T(128)} %bitcast.index_ref, s32[4,2,2,16]{3,2,1,0:T(2,128)S(1)} %copy-done, s32[4,2,2,16]{3,2,1,0:T(2,128)S(1)} %copy-done.1, s32[4,4]{1,0:T(4,128)S(1)} %copy-done.5, bf16[9,2,64,128]{3,2,1,0:T(8,128)(2,1)S(1)} %collective-permute-done.3.received_ref, ...), custom_call_target="tpu_custom_call" | custom-call | tf_op jit(solution)/shard_map/last/pallas_call | solution.py:357
  (3 shorter events, 0.0 us)
Async XLA Ops:
  0.0 0.7 %copy-start.7 = (f32[8,16]{1,0:T(8,128)S(1)}, f32[8,16]{1,0:T(8,128)}, u32[]{:S(2)}) copy-start(f32[8,16]{1,0:T(8,128)} %phase_ref.1) | copy-start | bytes 1540
  0.0 0.7 %copy-start.6 = (s32[8,16]{1,0:T(8,128)S(1)}, s32[8,16]{1,0:T(8,128)}, u32[]{:S(2)}) copy-start(s32[8,16]{1,0:T(8,128)} %delays_ref.1) | copy-start | bytes 1540
  0.0 0.7 %copy-start.8 = (f32[2,128]{1,0:T(2,128)S(1)}, f32[2,128]{1,0:T(2,128)}, u32[]{:S(2)}) copy-start(f32[2,128]{1,0:T(2,128)} %matched_ref.1) | copy-start | bytes 3076
  0.7 0.9 %copy-start.2 = (bf16[8,64,2,128]{3,2,1,0:T(2,128)(2,1)S(1)}, bf16[8,64,2,128]{3,2,1,0:T(2,128)(2,1)}, u32[]{:S(2)}) copy-start(bf16[8,64,2,128]{3,2,1,0:T(2,128)(2,1)} %param.9) | copy-start | bytes 786436
  1.7 4.3 %copy-start = (s32[4,2,2,16]{3,2,1,0:T(2,128)S(1)}, s32[4,2,2,16]{3,2,1,0:T(2,128)}, u32[]{:S(2)}) copy-start(s32[4,2,2,16]{3,2,1,0:T(2,128)} %beam_ref.15) | copy-start | bytes 3076
  1.7 4.3 %copy-start.1 = (s32[4,2,2,16]{3,2,1,0:T(2,128)S(1)}, s32[4,2,2,16]{3,2,1,0:T(2,128)}, u32[]{:S(2)}) copy-start(s32[4,2,2,16]{3,2,1,0:T(2,128)} %shift_ref.15) | copy-start | bytes 3076
  1.7 4.3 %copy-start.3 = (f32[4,2,2,16]{3,2,1,0:T(2,128)S(1)}, f32[4,2,2,16]{3,2,1,0:T(2,128)}, u32[]{:S(2)}) copy-start(f32[4,2,2,16]{3,2,1,0:T(2,128)} %base_ref.7) | copy-start | bytes 3076
  1.7 4.3 %copy-start.4 = (f32[4,2,2,16]{3,2,1,0:T(2,128)S(1)}, f32[4,2,2,16]{3,2,1,0:T(2,128)}, u32[]{:S(2)}) copy-start(f32[4,2,2,16]{3,2,1,0:T(2,128)} %rate_ref.7) | copy-start | bytes 3076
  5.5 0.7 %copy-start.5 = (s32[4,4]{1,0:T(4,128)S(1)}, s32[4,4]{1,0:T(4,128)}, u32[]{:S(2)}) copy-start(s32[4,4]{1,0:T(4,128)} %taps_ref.15) | copy-start | bytes 196
  5.5 4.4 %collective-permute-start = (bf16[9,2,64,128]{3,2,1,0:T(8,128)(2,1)S(1)}, bf16[9,2,64,128]{3,2,1,0:T(8,128)(2,1)S(1)}, u32[]{:S(2)}, u32[]{:S(2)}) collective-permute-start(bf16[9,2,64,128]{3,2,1,0:T(8,128)(2,1)S(1)} %get-tuple-element.21), channel_id=1, source_target_pairs={{0,1},{1,0},{2,3},{3,2},{4,5},{5,4},{6,7},{7,6},{8,9},{9,8},{10,11... | collective-permute-start | bytes 884744 | tf_op jit(solution)/shard_map/ppermute | solution.py:333
  12.3 10.1 %collective-permute-start.1 = (bf16[9,2,64,128]{3,2,1,0:T(8,128)(2,1)S(1)}, bf16[9,2,64,128]{3,2,1,0:T(8,128)(2,1)S(1)}, u32[]{:S(2)}, u32[]{:S(2)}) collective-permute-start(bf16[9,2,64,128]{3,2,1,0:T(8,128)(2,1)S(1)} %get-tuple-element.25), channel_id=1, source_target_pairs={{0,2},{1,3},{2,0},{3,1},{4,6},{5,7},{6,4},{7,5},{8,10},{9,11},{10,... | collective-permute-start | bytes 884744 | tf_op jit(solution)/shard_map/ppermute | solution.py:333
  24.9 8.4 %collective-permute-start.2 = (bf16[9,2,64,128]{3,2,1,0:T(8,128)(2,1)S(1)}, bf16[9,2,64,128]{3,2,1,0:T(8,128)(2,1)S(1)}, u32[]{:S(2)}, u32[]{:S(2)}) collective-permute-start(bf16[9,2,64,128]{3,2,1,0:T(8,128)(2,1)S(1)} %get-tuple-element.29), channel_id=1, source_target_pairs={{0,4},{1,5},{2,6},{3,7},{4,0},{5,1},{6,2},{7,3},{8,12},{9,13},{10,... | collective-permute-start | bytes 884744 | tf_op jit(solution)/shard_map/ppermute | solution.py:333
  35.7 14.7 %collective-permute-start.3 = (bf16[9,2,64,128]{3,2,1,0:T(8,128)(2,1)S(1)}, bf16[9,2,64,128]{3,2,1,0:T(8,128)(2,1)S(1)}, u32[]{:S(2)}, u32[]{:S(2)}) collective-permute-start(bf16[9,2,64,128]{3,2,1,0:T(8,128)(2,1)S(1)} %get-tuple-element.33), channel_id=1, source_target_pairs={{0,8},{1,9},{2,10},{3,11},{4,12},{5,13},{6,14},{7,15},{8,0},{9,1},... | collective-permute-start | bytes 884744 | tf_op jit(solution)/shard_map/ppermute | solution.py:333

commit v2 on v1

--- a/solution.py
+++ b/solution.py
@@ -38,6 +38,7 @@
 
 SMEM_SPEC = pl.BlockSpec(memory_space=pltpu.SMEM)
 VMEM_SPEC = pl.BlockSpec(memory_space=pltpu.VMEM)
+HBM_SPEC = pl.BlockSpec(memory_space=pltpu.HBM)
 
 
 def cos_sin_turns(turns):
@@ -52,12 +53,17 @@
     return c, s * f
 
 
+def times(x, y):
+    return x[0] * y[0] - x[1] * y[1], x[0] * y[1] + x[1] * y[0]
+
+
 def lane_iota(rows):
     return lax.broadcasted_iota(jnp.int32, (rows, LANES), 1)
 
 
-def store_extended(ext_ref, where, low, high, body):
+def store_extended(ext_ref, where, body):
     lane = lane_iota(HALO)
+    high, low = body[:HALO], body[HALF - HALO :]
     ext_ref[(*where, pl.ds(HALO, HALF))] = body
     after = jnp.where(lane < HALF, pltpu.roll(high, HALF, 1), pltpu.roll(high, HALF - 1, 1))
     ext_ref[(*where, pl.ds(HALO + HALF, HALO))] = jnp.where(lane == LANES - 1, 0.0, after)
@@ -66,31 +72,51 @@
 
 
 def front_kernel(
-    index_ref, raw_ref, matched_ref, delays_ref, phase_ref, image_ref, send_ref,
-    raw32, taps, windows, ext, trig, trig_smem, sem,
+    index_ref, raw_hbm, matched_hbm, delays_hbm, phase_hbm, *rest
 ):
-    pulses, beams = phase_ref.shape
-    rows = raw_ref.shape[0] // 2
+    tables, rest = rest[:5], rest[5:]
+    send_ref, rest_ref, rest = rest[0], rest[1], rest[2:]
+    copied, rest = rest[:5], rest[5:]
+    raw, matched, phase, delays, raw32, taps, windows, ext, trig, trig_smem, sems = rest
+    pulses, beams = phase.shape
+    rows = raw.shape[0] // 2
     blocks = rows // pulses
+    pairs = rows // LANES
+    size = raw.shape[0] // pairs
     side_bit = index_ref[0] % 2
+
+    small = [
+        pltpu.make_async_copy(matched_hbm, matched, sems.at[0]),
+        pltpu.make_async_copy(phase_hbm, phase, sems.at[1]),
+        pltpu.make_async_copy(delays_hbm, delays, sems.at[2]),
+    ]
+    small += [
+        pltpu.make_async_copy(source, target, sems.at[4 + i]) for i, (source, target) in enumerate(zip(tables, copied))
+    ]
+    large = [
+        pltpu.make_async_copy(
+            raw_hbm.at[pl.ds(pair * size, size)], raw.at[pl.ds(pair * size, size)], sems.at[4 + len(tables) + pair]
+        )
+        for pair in range(pairs)
+    ]
+    small[1].start()
+    small[0].start()
+    for copy in large:
+        copy.start()
+    for copy in small[2:]:
+        copy.start()
+    small[1].wait()
     scale = 1.0 / math.sqrt(pulses)
-    c, s = cos_sin_turns(phase_ref[...] * (0.5 / math.pi))
+    c, s = cos_sin_turns(phase[...] * (0.5 / math.pi))
     trig[0] = c * scale
     trig[1] = s * scale
-    copy = pltpu.make_async_copy(trig, trig_smem, sem)
-    copy.start()
-    raw32[0:16] = jnp.zeros((16, LANES), jnp.float32)
-    raw32[16 : 16 + 2 * rows] = raw_ref[...].astype(jnp.float32)
-    first = lax.broadcasted_iota(jnp.int32, (rows, LANES), 0) % blocks == 0
-    for part in range(2):
-        previous = raw32[pl.ds(14 + part, rows, stride=2), :]
-        windows[:, part * LANES : (part + 1) * LANES] = jnp.where(first, 0.0, previous).astype(jnp.bfloat16)
-        current = raw32[pl.ds(16 + part, rows, stride=2), :]
-        windows[:, (2 + part) * LANES : (3 + part) * LANES] = current.astype(jnp.bfloat16)
+    factors = pltpu.make_async_copy(trig, trig_smem, sems.at[3])
+    factors.start()
+    small[0].wait()
     row = lax.broadcasted_iota(jnp.int32, (LANES, LANES), 0)
     column = lax.broadcasted_iota(jnp.int32, (LANES, LANES), 1)
     for part in range(2):
-        line = jnp.broadcast_to(matched_ref[part : part + 1, :], (LANES, LANES))
+        line = jnp.broadcast_to(matched[part : part + 1, :], (LANES, LANES))
         circulant = pltpu.roll(line, 0, 1, stride=1, stride_axis=0).T
         now = jnp.where(column <= row, circulant, 0.0).astype(jnp.bfloat16)
         before = jnp.where(column > row, circulant, 0.0).astype(jnp.bfloat16)
@@ -104,8 +130,19 @@
             taps[LANES:, 0:LANES] = before
             taps[0:LANES, 3 * LANES :] = -now
             taps[LANES:, 2 * LANES : 3 * LANES] = now
+    raw32[0:16] = jnp.zeros((16, LANES), jnp.float32)
+    first = lax.broadcasted_iota(jnp.int32, (LANES, LANES), 0) % blocks == 0
     lane = lane_iota(HALF)
-    for pair in range(rows // LANES):
+    for pair in range(pairs):
+        large[pair].wait()
+        raw32[16 + pair * size : 16 + (pair + 1) * size] = raw[pair * size : (pair + 1) * size, :].astype(jnp.float32)
+        mine = slice(pair * LANES, (pair + 1) * LANES)
+        for part in range(2):
+            previous = raw32[pl.ds(14 + pair * size + part, LANES, stride=2), :]
+            windows[mine, part * LANES : (part + 1) * LANES] = jnp.where(first, 0.0, previous).astype(jnp.bfloat16)
+            current = raw32[pl.ds(16 + pair * size + part, LANES, stride=2), :]
+            windows[mine, (2 + part) * LANES : (3 + part) * LANES] = current.astype(jnp.bfloat16)
+    for pair in range(pairs):
         made = lax.dot_general(
             taps[...],
             windows[pair * LANES : (pair + 1) * LANES, :],
@@ -115,152 +152,170 @@
         for part in range(2):
             a = made[part * LANES : part * LANES + HALF]
             b = made[part * LANES + HALF : (part + 1) * LANES]
-            even = jnp.where(lane < HALF, a, pltpu.roll(b, HALF, 1))
-            odd = jnp.where(lane < HALF, pltpu.roll(a, HALF, 1), b)
-            for which, body in ((0, even), (1, odd)):
-                store_extended(ext, (2 * pair + which, part), body[HALF - HALO :], body[:HALO], body)
-    copy.wait()
-    send_first = (1 - side_bit) * 7
-
-    def beam(k, carry):
-        for piece in range(HALF // 32):
-            real = jnp.zeros((32, LANES), jnp.float32)
-            imag = jnp.zeros((32, LANES), jnp.float32)
+            store_extended(ext, (2 * pair, part), jnp.where(lane < HALF, a, pltpu.roll(b, HALF, 1)))
+            store_extended(ext, (2 * pair + 1, part), jnp.where(lane < HALF, pltpu.roll(a, HALF, 1), b))
+    factors.wait()
+    small[2].wait()
+    urgent = (1 - side_bit) * 7
+    count = send_ref.shape[0]
+    piece = 32
+
+    def beam(m, carry, sent):
+        k = (urgent + m) % beams
+        for first_row in range(0, HALF, piece):
+            real = imag = None
             for p in range(pulses):
-                start = delays_ref[p, k] + (HALO + piece * 32)
-                x = ext[p, 0, pl.ds(start, 32), :]
-                y = ext[p, 1, pl.ds(start, 32), :]
+                start = delays[p, k] + (HALO + first_row)
+                x = ext[p, 0, pl.ds(start, piece), :]
+                y = ext[p, 1, pl.ds(start, piece), :]
                 cosine = trig_smem[0, p, k]
                 sine = trig_smem[1, p, k]
-                real = real + (x * cosine - y * sine)
-                imag = imag + (x * sine + y * cosine)
-            image_ref[k, 0, pl.ds(piece * 32, 32)] = real
-            image_ref[k, 1, pl.ds(piece * 32, 32)] = imag
-            slot = k - send_first
-
-            @pl.when((slot >= 0) & (slot < send_ref.shape[0]))
-            def _():
-                send_ref[slot, 0, pl.ds(piece * 32, 32)] = real.astype(jnp.bfloat16)
-                send_ref[slot, 1, pl.ds(piece * 32, 32)] = imag.astype(jnp.bfloat16)
-
+                re = x * cosine - y * sine
+                im = x * sine + y * cosine
+                real = re if real is None else real + re
+                imag = im if imag is None else imag + im
+            rows_here = pl.ds(first_row, piece)
+            if sent:
+                send_ref[m, 0, rows_here] = real.astype(jnp.bfloat16)
+                send_ref[m, 1, rows_here] = imag.astype(jnp.bfloat16)
+            else:
+                rest_ref[m - count, 0, rows_here] = real
+                rest_ref[m - count, 1, rows_here] = imag
         return carry
 
-    lax.fori_loop(0, beams, beam, 0)
+    lax.fori_loop(0, count, functools.partial(beam, sent=True), 0, unroll=3)
+    lax.fori_loop(count, beams, functools.partial(beam, sent=False), 0, unroll=7)
+    for copy in small[3:]:
+        copy.wait()
 
 
 def tap_factors(taps_ref, level):
     count = taps_ref.shape[1]
     offsets = [taps_ref[level, t] for t in range(count)]
     weights = [(SPREAD + 1.0) - jnp.abs(o).astype(jnp.float32) for o in offsets]
-    return offsets, weights
-
-
-def filtered(ext, slot, part, start, offsets, weights):
-    total = None
-    for offset, weight in zip(offsets, weights):
-        term = ext[slot, part, pl.ds(start + offset, HALF), :] * weight
-        total = term if total is None else total + term
-    return total
-
-
-def cells():
-    t = lax.broadcasted_iota(jnp.int32, (HALF, LANES), 0)
-    lane = lane_iota(HALF)
-    return (t + (lane % HALF) * LANES + (lane // HALF) * HALF).astype(jnp.float32)
+    total = weights[0]
+    for w in weights[1:]:
+        total = total + w
+    scale = SQRT_HALF / total
+    return offsets, [w * scale for w in weights]
+
+
+def filtered(ext, slot, start, rows, offsets, weights):
+    sums = []
+    for part in range(2):
+        total = None
+        for offset, weight in zip(offsets, weights):
+            term = ext[slot, part, pl.ds(start + offset, rows), :] * weight
+            total = term if total is None else total + term
+        sums.append(total)
+    return tuple(sums)
+
+
+def merged(level, side_bit, k, first_row, rows, tables, factors, ext, partial_ref, turn_ref):
+    beam_ref, shift_ref = tables
+    other = (level, side_bit, 1 - side_bit, k)
+    slot = beam_ref[other] - side_bit * 7
+    start = shift_ref[other] + (HALO + first_row)
+    here = pl.ds(first_row, rows)
+    real, imag = times(filtered(ext, slot, start, rows, *factors), (turn_ref[k, 0, here], turn_ref[k, 1, here]))
+    return real + partial_ref[k, 0, here], imag + partial_ref[k, 1, here]
+
+
+def turns(base, rate, bins):
+    t = lax.broadcasted_iota(jnp.int32, (8, LANES), 0)
+    lane = lane_iota(8)
+    position = (t + (lane % HALF) * LANES + (lane // HALF) * HALF).astype(jnp.float32) * (1.0 / bins)
+    groups = [cos_sin_turns(position * rate + base * (0.5 / math.pi))]
+    step = cos_sin_turns(jnp.full((8, LANES), rate * (8.0 / bins)))
+    while len(groups) < HALF // 8:
+        groups += [times(g, step) for g in groups]
+        step = times(step, step)
+    return tuple(jnp.concatenate([g[i] for g in groups], axis=0) for i in range(2))
 
 
 def own_kernel(
-    level, bins, index_ref, beam_ref, shift_ref, base_ref, rate_ref, taps_ref, image_ref, partial_ref, turn_ref, ext,
+    level, bins, index_ref, beam_ref, shift_ref, base_ref, rate_ref, taps_ref, send_ref, *rest
 ):
+    if level == 0:
+        (rest_ref, partial_ref, turn_ref, ext) = rest
+    else:
+        (received_ext, last_partial, last_turn, partial_ref, turn_ref, ext) = rest
     side_bit = (index_ref[0] >> level) % 2
-    beams = image_ref.shape[0]
+    beams = partial_ref.shape[0]
+    count = send_ref.shape[0]
+    shared = 2 * count - beams
     low_beam = side_bit * 7
-
-    def extend(slot, carry):
+    urgent = (1 - side_bit) * 7
+
+    for i in range(shared):
         for part in range(2):
-            body = image_ref[low_beam + slot, part]
-            store_extended(ext, (slot, part), body[HALF - HALO :], body[:HALO], body)
+            body = send_ref[7 * side_bit + i, part].astype(jnp.float32)
+            store_extended(ext, (7 * (1 - side_bit) + i, part), body)
+    if level > 0:
+        last_bit = (index_ref[0] >> (level - 1)) % 2
+        last_factors = tap_factors(taps_ref, level - 1)
+
+    def remaining(m, carry):
+        k = (urgent + m) % beams
+        if level == 0:
+            pair = rest_ref[m - count, 0], rest_ref[m - count, 1]
+        else:
+            pair = merged(
+                level - 1, last_bit, k, 0, HALF, (beam_ref, shift_ref), last_factors, received_ext, last_partial, last_turn
+            )
+        for part in range(2):
+            store_extended(ext, (k - low_beam, part), pair[part])
         return carry
 
-    lax.fori_loop(0, ext.shape[0], extend, 0)
-    offsets, weights = tap_factors(taps_ref, level)
-    position = cells() * (1.0 / bins)
+    lax.fori_loop(count, beams, remaining, 0, unroll=7)
+    factors = tap_factors(taps_ref, level)
 
     def beam(k, carry):
         own = (level, side_bit, side_bit, k)
         other = (level, side_bit, 1 - side_bit, k)
         slot = beam_ref[own] - low_beam
         start = shift_ref[own] + HALO
-        real = filtered(ext, slot, 0, start, offsets, weights)
-        imag = filtered(ext, slot, 1, start, offsets, weights)
-        c, s = cos_sin_turns(position * rate_ref[own] + base_ref[own] * (0.5 / math.pi))
-        partial_ref[k, 0] = real * c - imag * s
-        partial_ref[k, 1] = real * s + imag * c
-        c, s = cos_sin_turns(position * rate_ref[other] + base_ref[other] * (0.5 / math.pi))
-        turn_ref[k, 0] = c
-        turn_ref[k, 1] = s
+        turn = turns(base_ref[own], rate_ref[own], bins)
+        for first_row in range(0, HALF, 32):
+            here = slice(first_row, first_row + 32)
+            real, imag = times(
+                filtered(ext, slot, start + first_row, 32, *factors), (turn[0][here], turn[1][here])
+            )
+            partial_ref[k, 0, here] = real
+            partial_ref[k, 1, here] = imag
+        turn_ref[k, 0], turn_ref[k, 1] = turns(base_ref[other], rate_ref[other], bins)
         return carry
 
-    lax.fori_loop(0, beams, beam, 0)
-
-
-def merged(level, side_bit, k, scale, beam_ref, shift_ref, offsets, weights, ext, partial_ref, turn_ref):
-    other = (level, side_bit, 1 - side_bit, k)
-    slot = beam_ref[other] - side_bit * 7
-    start = shift_ref[other] + HALO
-    real = filtered(ext, slot, 0, start, offsets, weights)
-    imag = filtered(ext, slot, 1, start, offsets, weights)
-    c = turn_ref[k, 0]
-    s = turn_ref[k, 1]
-    return (
-        (real * c - imag * s + partial_ref[k, 0]) * scale,
-        (real * s + imag * c + partial_ref[k, 1]) * scale,
-    )
+    lax.fori_loop(0, beams, beam, 0, unroll=2)
 
 
 def extend_received(received_ref, ext):
     def extend(slot, carry):
         for part in range(2):
-            body = received_ref[slot, part].astype(jnp.float32)
-            store_extended(ext, (slot, part), body[HALF - HALO :], body[:HALO], body)
+            store_extended(ext, (slot, part), received_ref[slot, part].astype(jnp.float32))
         return carry
 
-    lax.fori_loop(0, ext.shape[0], extend, 0)
-
-
-def total_scale(weights):
-    total = weights[0]
-    for w in weights[1:]:
-        total = total + w
-    return SQRT_HALF / total
+    lax.fori_loop(0, ext.shape[0], extend, 0, unroll=3)
 
 
 def middle_kernel(
-    level, index_ref, beam_ref, shift_ref, taps_ref, received_ref, partial_ref, turn_ref, image_ref, send_ref, ext,
+    level, index_ref, beam_ref, shift_ref, taps_ref, received_ref, partial_ref, turn_ref, send_ref, ext,
 ):
     side_bit = (index_ref[0] >> level) % 2
-    next_bit = (index_ref[0] >> (level + 1)) % 2
-    send_first = (1 - next_bit) * 7
+    urgent = (1 - (index_ref[0] >> (level + 1)) % 2) * 7
     extend_received(received_ref, ext)
-    offsets, weights = tap_factors(taps_ref, level)
-    scale = total_scale(weights)
-
-    def beam(k, carry):
-        real, imag = merged(
-            level, side_bit, k, scale, beam_ref, shift_ref, offsets, weights, ext, partial_ref, turn_ref
-        )
-        image_ref[k, 0] = real
-        image_ref[k, 1] = imag
-        slot = k - send_first
-
-        @pl.when((slot >= 0) & (slot < send_ref.shape[0]))
-        def _():
-            send_ref[slot, 0] = real.astype(jnp.bfloat16)
-            send_ref[slot, 1] = imag.astype(jnp.bfloat16)
-
+    factors = tap_factors(taps_ref, level)
+
+    def beam(m, carry):
+        for first_row in range(0, HALF, 32):
+            pair = merged(
+                level, side_bit, urgent + m, first_row, 32, (beam_ref, shift_ref), factors, ext, partial_ref, turn_ref
+            )
+            for part in range(2):
+                send_ref[m, part, pl.ds(first_row, 32)] = pair[part].astype(jnp.bfloat16)
         return carry
 
-    lax.fori_loop(0, image_ref.shape[0], beam, 0)
+    lax.fori_loop(0, send_ref.shape[0], beam, 0, unroll=9)
 
 
 def last_kernel(
@@ -268,17 +323,13 @@
 ):
     side_bit = (index_ref[0] >> level) % 2
     extend_received(received_ref, ext)
-    offsets, weights = tap_factors(taps_ref, level)
-    scale = total_scale(weights)
+    factors = tap_factors(taps_ref, level)
     lane = lane_iota(HALF)
+    tables = (beam_ref, shift_ref)
 
     def pair(m, carry):
-        even = merged(
-            level, side_bit, 2 * m, scale, beam_ref, shift_ref, offsets, weights, ext, partial_ref, turn_ref
-        )
-        odd = merged(
-            level, side_bit, 2 * m + 1, scale, beam_ref, shift_ref, offsets, weights, ext, partial_ref, turn_ref
-        )
+        even = merged(level, side_bit, 2 * m, 0, HALF, tables, factors, ext, partial_ref, turn_ref)
+        odd = merged(level, side_bit, 2 * m + 1, 0, HALF, tables, factors, ext, partial_ref, turn_ref)
         high, low = m // 4, 2 * (m % 4)
         for part in range(2):
             turned = jnp.concatenate([even[part], odd[part]], axis=0).T
@@ -288,7 +339,7 @@
             out_ref[part, high, pl.ds(low + 1, HALF, stride=8), :] = jnp.where(lane < HALF, pltpu.roll(a, HALF, 1), b)
         return carry
 
-    lax.fori_loop(0, partial_ref.shape[0] // 2, pair, 0)
+    lax.fori_loop(0, partial_ref.shape[0] // 2, pair, 0, unroll=2)
 
 
 def params():
@@ -309,47 +360,56 @@
     index = lax.axis_index("pulse").astype(jnp.int32).reshape(1)
     f32, bf16 = jnp.float32, jnp.bfloat16
     image_shape = jax.ShapeDtypeStruct((beams, 2, HALF, LANES), f32)
+    rest_shape = jax.ShapeDtypeStruct((beams - slots, 2, HALF, LANES), f32)
     send_shape = jax.ShapeDtypeStruct((slots, 2, HALF, LANES), bf16)
-    ext_scratch = pltpu.VMEM((slots, 2, HALF + 2 * HALO, LANES), f32)
+    ext_dims = (slots, 2, HALF + 2 * HALO, LANES)
     rows = pulses * blocks
-    image, send = pl.pallas_call(
+    inputs = (beam_map, range_shift, phase_base, phase_rate, tap_offsets)
+    sources = (raw_echoes.reshape(rows * parts, hop), matched, delays, pulse_phase, *inputs)
+    send, rest, *tables = pl.pallas_call(
         front_kernel,
-        out_shape=(image_shape, send_shape),
-        in_specs=[SMEM_SPEC, VMEM_SPEC, VMEM_SPEC, SMEM_SPEC, VMEM_SPEC],
-        out_specs=(VMEM_SPEC, VMEM_SPEC),
+        out_shape=(send_shape, rest_shape, *(pltpu.SMEM(x.shape, x.dtype) for x in inputs)),
+        in_specs=[SMEM_SPEC] + [HBM_SPEC] * (4 + len(inputs)),
+        out_specs=(VMEM_SPEC, VMEM_SPEC, *(SMEM_SPEC for x in inputs)),
         scratch_shapes=[
-            pltpu.VMEM((16 + 2 * rows, LANES), f32),
+            pltpu.VMEM((parts * rows, LANES), bf16),
+            pltpu.VMEM(matched.shape, f32),
+            pltpu.VMEM(pulse_phase.shape, f32),
+            pltpu.SMEM(delays.shape, jnp.int32),
+            pltpu.VMEM((16 + parts * rows, LANES), f32),
             pltpu.VMEM((2 * LANES, 4 * LANES), bf16),
             pltpu.VMEM((rows, 4 * LANES), bf16),
             pltpu.VMEM((pulses, 2, HALF + 2 * HALO, LANES), f32),
             pltpu.VMEM((2, pulses, beams), f32),
             pltpu.SMEM((2, pulses, beams), f32),
-            pltpu.SemaphoreType.DMA,
+            pltpu.SemaphoreType.DMA((4 + len(inputs) + rows // LANES,)),
         ],
         compiler_params=params(),
         name="front",
-    )(index, raw_echoes.reshape(pulses * blocks * parts, hop), matched, delays, pulse_phase)
+    )(index, *(pltpu.with_memory_space_constraint(x, pltpu.HBM) for x in sources))
+    beam_table, shift_table, base_table, rate_table, tap_table = tables
+    received_ext = partial = turn = None
     for level in range(levels):
         received = lax.ppermute(send, "pulse", route("pulse", level))
+        before = (rest,) if level == 0 else (received_ext, partial, turn)
         partial, turn = pl.pallas_call(
             functools.partial(own_kernel, level, bins),
             out_shape=(image_shape, image_shape),
-            in_specs=[SMEM_SPEC] * 6 + [VMEM_SPEC],
+            in_specs=[SMEM_SPEC] * 6 + [VMEM_SPEC] * (1 + len(before)),
             out_specs=(VMEM_SPEC, VMEM_SPEC),
-            scratch_shapes=[ext_scratch],
+            scratch_shapes=[pltpu.VMEM(ext_dims, f32)],
             compiler_params=params(),
             cost_estimate=pl.CostEstimate(flops=4 * 10**6, bytes_accessed=3 * 2**20, transcendentals=0),
             name=f"own{level}",
-        )(index, beam_map, range_shift, phase_base, phase_rate, tap_offsets, image)
-        operands = (index, beam_map, range_shift, tap_offsets, received, partial, turn)
+        )(index, *tables, send, *before)
+        operands = (index, beam_table, shift_table, tap_table, received, partial, turn)
         in_specs = [SMEM_SPEC] * 4 + [VMEM_SPEC] * 3
         if level < levels - 1:
-            image, send = pl.pallas_call(
+            send, received_ext = pl.pallas_call(
                 functools.partial(middle_kernel, level),
-                out_shape=(image_shape, send_shape),
+                out_shape=(send_shape, jax.ShapeDtypeStruct(ext_dims, f32)),
                 in_specs=in_specs,
                 out_specs=(VMEM_SPEC, VMEM_SPEC),
-                scratch_shapes=[ext_scratch],
                 compiler_params=params(),
                 name=f"middle{level}",
             )(*operands)
@@ -359,7 +419,7 @@
                 out_shape=jax.ShapeDtypeStruct((2, beams // 8, HALF * 8, LANES), f32),
                 in_specs=in_specs,
                 out_specs=VMEM_SPEC,
-                scratch_shapes=[ext_scratch],
+                scratch_shapes=[pltpu.VMEM(ext_dims, f32)],
                 compiler_params=params(),
                 name="last",
             )(*operands)

time: 54.9 us -> 44.4 us (0.81)
  Pallas kernels: 30.3 us -> 13.8 us
  waiting for transfers between devices: 14.5 us -> 22.6 us
  local copies, waits for them, and re-layouts: 1.82 us -> 0 us
    pallas_call x4, Pallas kernels: 14.7 us -> 5.8 us  [local(): pl.pallas_call(functools.partial(own_kernel, level, bins), out_shape=(ima...]
    ppermute x4, waiting for transfers between devices: 14.5 us -> 22.6 us  [local(): received = lax.ppermute(send, 'pulse', route('pulse', level))]
    pallas_call x4, Pallas kernels: 11.1 us -> 5.24 us  [the longest x1 3.21 us: local(): pl.pallas_call(front_kernel, out_shape=(send_shape, rest_shape, *(pltpu.S...]
    unnamed x18 -> x0, local copies, waits for them, and re-layouts: 1.82 us -> none
    pallas_call x1, Pallas kernels: 4.41 us -> 2.8 us  [local(): pl.pallas_call(functools.partial(last_kernel, level), out_shape=jax.Shape...]
  transfers between devices with their start and end apart: 4 -> 4, of which waited for: 3 -> 3; matrix products, arithmetic and copies ran while one was open for 0% -> 0% of each run, Pallas kernels for 27% -> 13%
where the time goes in v2:
time: 44.4 us; the launch traced here: 44.2 us
  waiting for transfers between devices  22.6 us (51%)
  Pallas kernels  13.8 us (31%)
  starting transfers between devices  7.73 us (17%)
    ppermute x4, waiting for transfers between devices, local(): received = lax.ppermute(send, 'pulse', route('pulse', level))  22.6 us
    ppermute x4, starting transfers between devices, local(): received = lax.ppermute(send, 'pulse', route('pulse', level))  7.73 us
    pallas_call x4, Pallas kernels, local(): pl.pallas_call(functools.partial(own_kernel, level, bins), out_shape=(ima...  5.8 us
    pallas_call x1, Pallas kernels, local(): pl.pallas_call(front_kernel, out_shape=(send_shape, rest_shape, *(pltpu.S...  3.21 us
    pallas_call x1, Pallas kernels, local(): pl.pallas_call(functools.partial(last_kernel, level), out_shape=jax.Shape...  2.8 us
    pallas_call x3, Pallas kernels, local(): pl.pallas_call(functools.partial(middle_kernel, level), out_shape=(send_s...  2.03 us
  transfers between devices with their start and end apart: 4, of which 3 were waited for; matrix products, arithmetic and copies ran while one was open for 0% of the time, Pallas kernels for 13%

profile of v2, /device:TPU:0, one launch (start us, length us, event | category | flops | bytes accessed | tf_op | source)
XLA Modules:
  0.0 44.2 jit_solution(332320982960212795)
XLA Ops:
  0.0 3.2 %front.1 = (bf16[9,2,64,128]{3,2,1,0:T(8,128)(2,1)S(1)}, f32[7,2,64,128]{3,2,1,0:T(8,128)S(1)}, s32[4,2,2,16]{3,2,1,0:T(2,128)S(4)}, s32[4,2,2,16]{3,2,1,0:T(2,1...) custom-call(s32[1]{0:T(128)} %bitcast.index_ref, ...), custom_call_target="tpu_custom_call" | custom-call | tf_op jit(solution)/shard_map/front/pallas_call | solution.py:369
  3.2 0.5 %collective-permute-start = (bf16[9,2,64,128]{3,2,1,0:T(8,128)(2,1)S(1)}, bf16[9,2,64,128]{3,2,1,0:T(8,128)(2,1)S(1)}, u32[]{:S(2)}, u32[]{:S(2)}) collective-permute-start(bf16[9,2,64,128]{3,2,1,0:T(8,128)(2,1)S(1)} %get-tuple-element.29.send_ref), channel_id=1, source_target_pairs={{0,1},{1,0},{2,3},{3,2},{4,5},{5,4},{6,7},{7,6},{8,9},{9,8},{10,11... | collective-permute-start | bytes 884744 | tf_op jit(solution)/shard_map/ppermute | solution.py:393
  3.7 1.4 %own0.1 = (f32[16,2,64,128]{3,2,1,0:T(8,128)S(1)}, f32[16,2,64,128]{3,2,1,0:T(8,128)S(1)}) custom-call(s32[1]{0:T(128)} %bitcast.index_ref, s32[4,2,2,16]{3,2,1,0:T(2,128)S(4)} %get-tuple-element.26.beam_ref, s32[4,2,2,16]{3,2,1,0:T(2,128)S(4)} %get-tuple-element.27.shift_ref, f32[4,2,2,16]{3,2,1,0:T(2,128)S(4)} %get-tuple-element.30.base_ref, ...), custom_call_target="tpu_custom_call" | custom-call | flops 4000000 | bytes 3145728 | tf_op jit(solution)/shard_map/own0/pallas_call | solution.py:395
  5.1 0.0 collective-permute-done.received_ref
  5.1 0.7 %middle0.1 = (bf16[9,2,64,128]{3,2,1,0:T(8,128)(2,1)S(1)}, f32[9,2,128,128]{3,2,1,0:T(8,128)S(1)}) custom-call(s32[1]{0:T(128)} %bitcast.index_ref, s32[4,2,2,16]{3,2,1,0:T(2,128)S(4)} %get-tuple-element.26.beam_ref, s32[4,2,2,16]{3,2,1,0:T(2,128)S(4)} %get-tuple-element.27.shift_ref, s32[4,4]{1,0:T(4,128)S(4)} %get-tuple-element.28.taps_ref, ...), custom_call_target="tpu_custom_call" | custom-call | tf_op jit(solution)/shard_map/middle0/pallas_call | solution.py:408
  5.8 2.8 %collective-permute-start.1 = (bf16[9,2,64,128]{3,2,1,0:T(8,128)(2,1)S(1)}, bf16[9,2,64,128]{3,2,1,0:T(8,128)(2,1)S(1)}, u32[]{:S(2)}, u32[]{:S(2)}) collective-permute-start(bf16[9,2,64,128]{3,2,1,0:T(8,128)(2,1)S(1)} %get-tuple-element.35.send_ref), channel_id=1, source_target_pairs={{0,2},{1,3},{2,0},{3,1},{4,6},{5,7},{6,4},{7,5},{8,10},{9,11},{10,... | collective-permute-start | bytes 884744 | tf_op jit(solution)/shard_map/ppermute | solution.py:393
  8.6 1.5 %own1.1 = (f32[16,2,64,128]{3,2,1,0:T(8,128)S(1)}, f32[16,2,64,128]{3,2,1,0:T(8,128)S(1)}) custom-call(s32[1]{0:T(128)} %bitcast.index_ref, s32[4,2,2,16]{3,2,1,0:T(2,128)S(4)} %get-tuple-element.26.beam_ref, s32[4,2,2,16]{3,2,1,0:T(2,128)S(4)} %get-tuple-element.27.shift_ref, f32[4,2,2,16]{3,2,1,0:T(2,128)S(4)} %get-tuple-element.30.base_ref, ...), custom_call_target="tpu_custom_call" | custom-call | flops 4000000 | bytes 3145728 | tf_op jit(solution)/shard_map/own1/pallas_call | solution.py:395
  10.0 6.0 %collective-permute-done.1.received_ref = bf16[9,2,64,128]{3,2,1,0:T(8,128)(2,1)S(1)} collective-permute-done((bf16[9,2,64,128]{3,2,1,0:T(8,128)(2,1)S(1)}, bf16[9,2,64,128]{3,2,1,0:T(8,128)(2,1)S(1)}, u32[]{:S(2)}, u32[]{:S(2)}) %collective-permute-start.1) | collective-permute-done | bytes 294944 | tf_op jit(solution)/shard_map/ppermute | solution.py:393
  16.0 0.7 %middle1.1 = (bf16[9,2,64,128]{3,2,1,0:T(8,128)(2,1)S(1)}, f32[9,2,128,128]{3,2,1,0:T(8,128)S(1)}) custom-call(s32[1]{0:T(128)} %bitcast.index_ref, s32[4,2,2,16]{3,2,1,0:T(2,128)S(4)} %get-tuple-element.26.beam_ref, s32[4,2,2,16]{3,2,1,0:T(2,128)S(4)} %get-tuple-element.27.shift_ref, s32[4,4]{1,0:T(4,128)S(4)} %get-tuple-element.28.taps_ref, ...), custom_call_target="tpu_custom_call" | custom-call | tf_op jit(solution)/shard_map/middle1/pallas_call | solution.py:408
  16.7 1.9 %collective-permute-start.2 = (bf16[9,2,64,128]{3,2,1,0:T(8,128)(2,1)S(1)}, bf16[9,2,64,128]{3,2,1,0:T(8,128)(2,1)S(1)}, u32[]{:S(2)}, u32[]{:S(2)}) collective-permute-start(bf16[9,2,64,128]{3,2,1,0:T(8,128)(2,1)S(1)} %get-tuple-element.39.send_ref), channel_id=1, source_target_pairs={{0,4},{1,5},{2,6},{3,7},{4,0},{5,1},{6,2},{7,3},{8,12},{9,13},{10,... | collective-permute-start | bytes 884744 | tf_op jit(solution)/shard_map/ppermute | solution.py:393
  18.6 1.5 %own2.1 = (f32[16,2,64,128]{3,2,1,0:T(8,128)S(1)}, f32[16,2,64,128]{3,2,1,0:T(8,128)S(1)}) custom-call(s32[1]{0:T(128)} %bitcast.index_ref, s32[4,2,2,16]{3,2,1,0:T(2,128)S(4)} %get-tuple-element.26.beam_ref, s32[4,2,2,16]{3,2,1,0:T(2,128)S(4)} %get-tuple-element.27.shift_ref, f32[4,2,2,16]{3,2,1,0:T(2,128)S(4)} %get-tuple-element.30.base_ref, ...), custom_call_target="tpu_custom_call" | custom-call | flops 4000000 | bytes 3145728 | tf_op jit(solution)/shard_map/own2/pallas_call | solution.py:395
  20.1 5.4 %collective-permute-done.2.received_ref = bf16[9,2,64,128]{3,2,1,0:T(8,128)(2,1)S(1)} collective-permute-done((bf16[9,2,64,128]{3,2,1,0:T(8,128)(2,1)S(1)}, bf16[9,2,64,128]{3,2,1,0:T(8,128)(2,1)S(1)}, u32[]{:S(2)}, u32[]{:S(2)}) %collective-permute-start.2) | collective-permute-done | bytes 294944 | tf_op jit(solution)/shard_map/ppermute | solution.py:393
  25.5 0.7 %middle2.1 = (bf16[9,2,64,128]{3,2,1,0:T(8,128)(2,1)S(1)}, f32[9,2,128,128]{3,2,1,0:T(8,128)S(1)}) custom-call(s32[1]{0:T(128)} %bitcast.index_ref, s32[4,2,2,16]{3,2,1,0:T(2,128)S(4)} %get-tuple-element.26.beam_ref, s32[4,2,2,16]{3,2,1,0:T(2,128)S(4)} %get-tuple-element.27.shift_ref, s32[4,4]{1,0:T(4,128)S(4)} %get-tuple-element.28.taps_ref, ...), custom_call_target="tpu_custom_call" | custom-call | tf_op jit(solution)/shard_map/middle2/pallas_call | solution.py:408
  26.2 2.6 %collective-permute-start.3 = (bf16[9,2,64,128]{3,2,1,0:T(8,128)(2,1)S(1)}, bf16[9,2,64,128]{3,2,1,0:T(8,128)(2,1)S(1)}, u32[]{:S(2)}, u32[]{:S(2)}) collective-permute-start(bf16[9,2,64,128]{3,2,1,0:T(8,128)(2,1)S(1)} %get-tuple-element.43.send_ref), channel_id=1, source_target_pairs={{0,8},{1,9},{2,10},{3,11},{4,12},{5,13},{6,14},{7,15},{8,0},{9,1},... | collective-permute-start | bytes 884744 | tf_op jit(solution)/shard_map/ppermute | solution.py:393
  28.8 1.5 %own3.1 = (f32[16,2,64,128]{3,2,1,0:T(8,128)S(1)}, f32[16,2,64,128]{3,2,1,0:T(8,128)S(1)}) custom-call(s32[1]{0:T(128)} %bitcast.index_ref, s32[4,2,2,16]{3,2,1,0:T(2,128)S(4)} %get-tuple-element.26.beam_ref, s32[4,2,2,16]{3,2,1,0:T(2,128)S(4)} %get-tuple-element.27.shift_ref, f32[4,2,2,16]{3,2,1,0:T(2,128)S(4)} %get-tuple-element.30.base_ref, ...), custom_call_target="tpu_custom_call" | custom-call | flops 4000000 | bytes 3145728 | tf_op jit(solution)/shard_map/own3/pallas_call | solution.py:395
  30.3 11.1 %collective-permute-done.3.received_ref = bf16[9,2,64,128]{3,2,1,0:T(8,128)(2,1)S(1)} collective-permute-done((bf16[9,2,64,128]{3,2,1,0:T(8,128)(2,1)S(1)}, bf16[9,2,64,128]{3,2,1,0:T(8,128)(2,1)S(1)}, u32[]{:S(2)}, u32[]{:S(2)}) %collective-permute-start.3) | collective-permute-done | bytes 294944 | tf_op jit(solution)/shard_map/ppermute | solution.py:393
  41.4 2.8 %last.1 = f32[2,2,512,128]{3,2,1,0:T(8,128)} custom-call(s32[1]{0:T(128)} %bitcast.index_ref, s32[4,2,2,16]{3,2,1,0:T(2,128)S(4)} %get-tuple-element.26.beam_ref, s32[4,2,2,16]{3,2,1,0:T(2,128)S(4)} %get-tuple-element.27.shift_ref, s32[4,4]{1,0:T(4,128)S(4)} %get-tuple-element.28.taps_ref, bf16[9,2,64,128]{3,2,1,0:T(8,128)(2,1)S(1)} %collective-permute-done.3.received_ref, ...), custom_call_target="tpu_custom_call" | custom-call | tf_op jit(solution)/shard_map/last/pallas_call | solution.py:417
Async XLA Ops:
  3.2 1.9 %collective-permute-start = (bf16[9,2,64,128]{3,2,1,0:T(8,128)(2,1)S(1)}, bf16[9,2,64,128]{3,2,1,0:T(8,128)(2,1)S(1)}, u32[]{:S(2)}, u32[]{:S(2)}) collective-permute-start(bf16[9,2,64,128]{3,2,1,0:T(8,128)(2,1)S(1)} %get-tuple-element.29.send_ref), channel_id=1, source_target_pairs={{0,1},{1,0},{2,3},{3,2},{4,5},{5,4},{6,7},{7,6},{8,9},{9,8},{10,11... | collective-permute-start | bytes 884744 | tf_op jit(solution)/shard_map/ppermute | solution.py:393
  5.8 10.3 %collective-permute-start.1 = (bf16[9,2,64,128]{3,2,1,0:T(8,128)(2,1)S(1)}, bf16[9,2,64,128]{3,2,1,0:T(8,128)(2,1)S(1)}, u32[]{:S(2)}, u32[]{:S(2)}) collective-permute-start(bf16[9,2,64,128]{3,2,1,0:T(8,128)(2,1)S(1)} %get-tuple-element.35.send_ref), channel_id=1, source_target_pairs={{0,2},{1,3},{2,0},{3,1},{4,6},{5,7},{6,4},{7,5},{8,10},{9,11},{10,... | collective-permute-start | bytes 884744 | tf_op jit(solution)/shard_map/ppermute | solution.py:393
  16.7 8.8 %collective-permute-start.2 = (bf16[9,2,64,128]{3,2,1,0:T(8,128)(2,1)S(1)}, bf16[9,2,64,128]{3,2,1,0:T(8,128)(2,1)S(1)}, u32[]{:S(2)}, u32[]{:S(2)}) collective-permute-start(bf16[9,2,64,128]{3,2,1,0:T(8,128)(2,1)S(1)} %get-tuple-element.39.send_ref), channel_id=1, source_target_pairs={{0,4},{1,5},{2,6},{3,7},{4,0},{5,1},{6,2},{7,3},{8,12},{9,13},{10,... | collective-permute-start | bytes 884744 | tf_op jit(solution)/shard_map/ppermute | solution.py:393
  26.2 15.2 %collective-permute-start.3 = (bf16[9,2,64,128]{3,2,1,0:T(8,128)(2,1)S(1)}, bf16[9,2,64,128]{3,2,1,0:T(8,128)(2,1)S(1)}, u32[]{:S(2)}, u32[]{:S(2)}) collective-permute-start(bf16[9,2,64,128]{3,2,1,0:T(8,128)(2,1)S(1)} %get-tuple-element.43.send_ref), channel_id=1, source_target_pairs={{0,8},{1,9},{2,10},{3,11},{4,12},{5,13},{6,14},{7,15},{8,0},{9,1},... | collective-permute-start | bytes 884744 | tf_op jit(solution)/shard_map/ppermute | solution.py:393

commit v3 on v2

--- a/solution.py
+++ b/solution.py
@@ -14,6 +14,8 @@
 HALO = 32
 LANES = 128
 HALF = 64
+FIRST = 5
+ORDERED = (1, 2)
 SQRT_HALF = 0.7071067811865476
 VMEM_LIMIT = 24 * 2**20
 
@@ -211,10 +213,34 @@
     return tuple(sums)
 
 
-def merged(level, side_bit, k, first_row, rows, tables, factors, ext, partial_ref, turn_ref):
+def order_start(level, index):
+    first, second, third = (index >> 1) & 1, (index >> 2) & 1, (index >> 3) & 1
+    if level == 1:
+        low = (1 - third) * first
+        high = third * (2 + first) + (1 - third) * 4
+        return second * low + (1 - second) * high
+    if level == 2:
+        return (1 - third) * (2 + second)
+    return 0
+
+
+def place_of(slot, start, count):
+    place = slot - start
+    return jnp.where(place < 0, place + count, place)
+
+
+def slot_at(place, start, count):
+    slot = start + place
+    return jnp.where(slot >= count, slot - count, slot)
+
+
+def merged(level, index, k, first_row, rows, tables, factors, count, ext, partial_ref, turn_ref):
     beam_ref, shift_ref = tables
+    side_bit = (index >> level) % 2
     other = (level, side_bit, 1 - side_bit, k)
     slot = beam_ref[other] - side_bit * 7
+    if level in ORDERED:
+        slot = place_of(slot, order_start(level, index), count)
     start = shift_ref[other] + (HALO + first_row)
     here = pl.ds(first_row, rows)
     real, imag = times(filtered(ext, slot, start, rows, *factors), (turn_ref[k, 0, here], turn_ref[k, 1, here]))
@@ -234,25 +260,35 @@
 
 
 def own_kernel(
-    level, bins, index_ref, beam_ref, shift_ref, base_ref, rate_ref, taps_ref, send_ref, *rest
+    level, bins, count, index_ref, beam_ref, shift_ref, base_ref, rate_ref, taps_ref, *rest
 ):
     if level == 0:
-        (rest_ref, partial_ref, turn_ref, ext) = rest
+        (send_ref, rest_ref, partial_ref, turn_ref, ext) = rest
     else:
-        (received_ext, last_partial, last_turn, partial_ref, turn_ref, ext) = rest
-    side_bit = (index_ref[0] >> level) % 2
+        (first_ref, second_ref, received_ext, last_partial, last_turn, partial_ref, turn_ref, ext) = rest
+    index = index_ref[0]
+    side_bit = (index >> level) % 2
     beams = partial_ref.shape[0]
-    count = send_ref.shape[0]
     shared = 2 * count - beams
     low_beam = side_bit * 7
     urgent = (1 - side_bit) * 7
 
+    start = order_start(level, index ^ (1 << level))
     for i in range(shared):
+        slot = 7 * side_bit + i
         for part in range(2):
-            body = send_ref[7 * side_bit + i, part].astype(jnp.float32)
+            if level == 0:
+                body = send_ref[slot, part].astype(jnp.float32)
+            else:
+                place = place_of(slot, start, count)
+                in_first = place < FIRST
+                body = jnp.where(
+                    in_first,
+                    first_ref[jnp.minimum(place, FIRST - 1), part].astype(jnp.float32),
+                    second_ref[jnp.maximum(place - FIRST, 0), part].astype(jnp.float32),
+                )
             store_extended(ext, (7 * (1 - side_bit) + i, part), body)
     if level > 0:
-        last_bit = (index_ref[0] >> (level - 1)) % 2
         last_factors = tap_factors(taps_ref, level - 1)
 
     def remaining(m, carry):
@@ -261,7 +297,7 @@
             pair = rest_ref[m - count, 0], rest_ref[m - count, 1]
         else:
             pair = merged(
-                level - 1, last_bit, k, 0, HALF, (beam_ref, shift_ref), last_factors, received_ext, last_partial, last_turn
+                level - 1, index, k, 0, HALF, (beam_ref, shift_ref), last_factors, count, received_ext, last_partial, last_turn
             )
         for part in range(2):
             store_extended(ext, (k - low_beam, part), pair[part])
@@ -289,57 +325,110 @@
     lax.fori_loop(0, beams, beam, 0, unroll=2)
 
 
-def extend_received(received_ref, ext):
+def extend_received(received_ref, ext, first, unroll):
     def extend(slot, carry):
         for part in range(2):
-            store_extended(ext, (slot, part), received_ref[slot, part].astype(jnp.float32))
+            store_extended(ext, (first + slot, part), received_ref[slot, part].astype(jnp.float32))
         return carry
 
-    lax.fori_loop(0, ext.shape[0], extend, 0, unroll=3)
-
-
-def middle_kernel(
-    level, index_ref, beam_ref, shift_ref, taps_ref, received_ref, partial_ref, turn_ref, send_ref, ext,
+    lax.fori_loop(0, received_ref.shape[0], extend, 0, unroll=unroll)
+
+
+def copy_extended(source, target):
+    for slot in range(source.shape[0]):
+        target[slot] = source[slot]
+
+
+def send_parents(level, index, places, sends, tables, factors, count, ext, partial_ref, turn_ref):
+    next_bit = (index >> (level + 1)) % 2
+    start = order_start(level + 1, index ^ (2 << level))
+    for place in places:
+        k = (1 - next_bit) * 7 + slot_at(place, start, count)
+        target, at = (sends[0], place) if place < FIRST else (sends[-1], place - FIRST)
+        for first_row in range(0, HALF, 32):
+            pair = merged(level, index, k, first_row, 32, tables, factors, count, ext, partial_ref, turn_ref)
+            for part in range(2):
+                target[at, part, pl.ds(first_row, 32)] = pair[part].astype(jnp.bfloat16)
+
+
+def bottom_kernel(
+    count, index_ref, beam_ref, shift_ref, taps_ref, received_ref, partial_ref, turn_ref, first_ref, second_ref, ext,
 ):
-    side_bit = (index_ref[0] >> level) % 2
-    urgent = (1 - (index_ref[0] >> (level + 1)) % 2) * 7
-    extend_received(received_ref, ext)
+    extend_received(received_ref, ext, 0, 3)
+    send_parents(
+        0, index_ref[0], range(count), (first_ref, second_ref), (beam_ref, shift_ref), tap_factors(taps_ref, 0), count,
+        ext, partial_ref, turn_ref,
+    )
+
+
+def middle_first_kernel(
+    level, count, index_ref, beam_ref, shift_ref, taps_ref, received_ref, partial_ref, turn_ref, send_ref, ext,
+):
+    extend_received(received_ref, ext, 0, 5)
+    send_parents(
+        level, index_ref[0], range(FIRST), (send_ref,), (beam_ref, shift_ref), tap_factors(taps_ref, level), count,
+        ext, partial_ref, turn_ref,
+    )
+
+
+def middle_second_kernel(
+    level, count, index_ref, beam_ref, shift_ref, taps_ref, received_ref, first_ext, partial_ref, turn_ref, send_ref, ext,
+):
+    extend_received(received_ref, ext, FIRST, 4)
+    copy_extended(first_ext, ext)
+    send_parents(
+        level, index_ref[0], range(FIRST, count), (send_ref,), (beam_ref, shift_ref), tap_factors(taps_ref, level), count,
+        ext, partial_ref, turn_ref,
+    )
+
+
+def place_pair(level, index, m, out_ref, high, low, tables, factors, count, ext, partial_ref, turn_ref):
+    lane = lane_iota(HALF)
+    even = merged(level, index, 2 * m, 0, HALF, tables, factors, count, ext, partial_ref, turn_ref)
+    odd = merged(level, index, 2 * m + 1, 0, HALF, tables, factors, count, ext, partial_ref, turn_ref)
+    for part in range(2):
+        turned = jnp.concatenate([even[part], odd[part]], axis=0).T
+        a = turned[:HALF]
+        b = turned[HALF:]
+        where = (part,) if high is None else (part, high)
+        out_ref[(*where, pl.ds(low, HALF, stride=8))] = jnp.where(lane < HALF, a, pltpu.roll(b, HALF, 1))
+        out_ref[(*where, pl.ds(low + 1, HALF, stride=8))] = jnp.where(lane < HALF, pltpu.roll(a, HALF, 1), b)
+
+
+EARLY = 3
+
+
+def last_first_kernel(
+    level, count, index_ref, beam_ref, shift_ref, taps_ref, received_ref, partial_ref, turn_ref, tiles_ref, ext,
+):
+    extend_received(received_ref, ext, 0, 5)
     factors = tap_factors(taps_ref, level)
-
-    def beam(m, carry):
-        for first_row in range(0, HALF, 32):
-            pair = merged(
-                level, side_bit, urgent + m, first_row, 32, (beam_ref, shift_ref), factors, ext, partial_ref, turn_ref
-            )
-            for part in range(2):
-                send_ref[m, part, pl.ds(first_row, 32)] = pair[part].astype(jnp.bfloat16)
-        return carry
-
-    lax.fori_loop(0, send_ref.shape[0], beam, 0, unroll=9)
-
-
-def last_kernel(
-    level, index_ref, beam_ref, shift_ref, taps_ref, received_ref, partial_ref, turn_ref, out_ref, ext,
+    for m in range(EARLY):
+        place_pair(
+            level, index_ref[0], m, tiles_ref, None, 2 * m, (beam_ref, shift_ref), factors, count, ext, partial_ref, turn_ref
+        )
+
+
+def last_second_kernel(
+    level, count, index_ref, beam_ref, shift_ref, taps_ref, received_ref, first_ext, tiles_ref, partial_ref, turn_ref, out_hbm,
+    ext, tiles, sems,
 ):
-    side_bit = (index_ref[0] >> level) % 2
-    extend_received(received_ref, ext)
+    tiles[:, 0] = tiles_ref[...]
+    extend_received(received_ref, ext, FIRST, 4)
+    copy_extended(first_ext, ext)
     factors = tap_factors(taps_ref, level)
-    lane = lane_iota(HALF)
-    tables = (beam_ref, shift_ref)
-
-    def pair(m, carry):
-        even = merged(level, side_bit, 2 * m, 0, HALF, tables, factors, ext, partial_ref, turn_ref)
-        odd = merged(level, side_bit, 2 * m + 1, 0, HALF, tables, factors, ext, partial_ref, turn_ref)
+    copies = []
+    for m in range(EARLY, partial_ref.shape[0] // 2):
         high, low = m // 4, 2 * (m % 4)
-        for part in range(2):
-            turned = jnp.concatenate([even[part], odd[part]], axis=0).T
-            a = turned[:HALF]
-            b = turned[HALF:]
-            out_ref[part, high, pl.ds(low, HALF, stride=8), :] = jnp.where(lane < HALF, a, pltpu.roll(b, HALF, 1))
-            out_ref[part, high, pl.ds(low + 1, HALF, stride=8), :] = jnp.where(lane < HALF, pltpu.roll(a, HALF, 1), b)
-        return carry
-
-    lax.fori_loop(0, partial_ref.shape[0] // 2, pair, 0, unroll=2)
+        place_pair(
+            level, index_ref[0], m, tiles, high, low, (beam_ref, shift_ref), factors, count, ext, partial_ref, turn_ref
+        )
+        if low == 6:
+            copy = pltpu.make_async_copy(tiles.at[:, high], out_hbm.at[:, high], sems.at[high])
+            copy.start()
+            copies.append(copy)
+    for copy in copies:
+        copy.wait()
 
 
 def params():
@@ -362,7 +451,6 @@
     image_shape = jax.ShapeDtypeStruct((beams, 2, HALF, LANES), f32)
     rest_shape = jax.ShapeDtypeStruct((beams - slots, 2, HALF, LANES), f32)
     send_shape = jax.ShapeDtypeStruct((slots, 2, HALF, LANES), bf16)
-    ext_dims = (slots, 2, HALF + 2 * HALO, LANES)
     rows = pulses * blocks
     inputs = (beam_map, range_shift, phase_base, phase_rate, tap_offsets)
     sources = (raw_echoes.reshape(rows * parts, hop), matched, delays, pulse_phase, *inputs)
@@ -388,41 +476,77 @@
         name="front",
     )(index, *(pltpu.with_memory_space_constraint(x, pltpu.HBM) for x in sources))
     beam_table, shift_table, base_table, rate_table, tap_table = tables
-    received_ext = partial = turn = None
-    for level in range(levels):
-        received = lax.ppermute(send, "pulse", route("pulse", level))
-        before = (rest,) if level == 0 else (received_ext, partial, turn)
-        partial, turn = pl.pallas_call(
-            functools.partial(own_kernel, level, bins),
-            out_shape=(image_shape, image_shape),
-            in_specs=[SMEM_SPEC] * 6 + [VMEM_SPEC] * (1 + len(before)),
-            out_specs=(VMEM_SPEC, VMEM_SPEC),
-            scratch_shapes=[pltpu.VMEM(ext_dims, f32)],
+    scalars = (index, beam_table, shift_table, tap_table)
+
+    def shape(number, dtype=bf16, rows=HALF):
+        return jax.ShapeDtypeStruct((number, 2, rows, LANES), dtype)
+
+    def kernel(function, out_shape, operands, name, scratch=(), out_specs=None, scalar_count=len(scalars)):
+        return pl.pallas_call(
+            function,
+            out_shape=out_shape,
+            in_specs=[SMEM_SPEC] * scalar_count + [VMEM_SPEC] * (len(operands) - scalar_count),
+            out_specs=jax.tree.map(lambda x: VMEM_SPEC, out_shape) if out_specs is None else out_specs,
+            scratch_shapes=list(scratch),
             compiler_params=params(),
-            cost_estimate=pl.CostEstimate(flops=4 * 10**6, bytes_accessed=3 * 2**20, transcendentals=0),
-            name=f"own{level}",
-        )(index, *tables, send, *before)
-        operands = (index, beam_table, shift_table, tap_table, received, partial, turn)
-        in_specs = [SMEM_SPEC] * 4 + [VMEM_SPEC] * 3
+            cost_estimate=pl.CostEstimate(flops=2 * 10**6, bytes_accessed=2**20, transcendentals=0),
+            name=name,
+        )(*operands)
+
+    own_scalars = (index, *tables)
+    second = slots - FIRST
+    long = HALF + 2 * HALO
+    images = (image_shape, image_shape)
+    ext_scratch = [pltpu.VMEM((slots, 2, long, LANES), f32)]
+
+    def own(level, *operands):
+        return kernel(
+            functools.partial(own_kernel, level, bins, slots), images, own_scalars + operands, f"own{level}", ext_scratch,
+            scalar_count=len(own_scalars),
+        )
+
+    received = lax.ppermute(send, "pulse", route("pulse", 0))
+    partial, turn = own(0, send, rest)
+    *sends, ext = kernel(
+        functools.partial(bottom_kernel, slots),
+        (shape(FIRST), shape(second), shape(slots, f32, long)),
+        (*scalars, received, partial, turn),
+        "bottom",
+    )
+    for level in range(1, levels):
+        received = [lax.ppermute(x, "pulse", route("pulse", level)) for x in sends]
+        partial, turn = own(level, *sends, ext, partial, turn)
         if level < levels - 1:
-            send, received_ext = pl.pallas_call(
-                functools.partial(middle_kernel, level),
-                out_shape=(send_shape, jax.ShapeDtypeStruct(ext_dims, f32)),
-                in_specs=in_specs,
-                out_specs=(VMEM_SPEC, VMEM_SPEC),
-                compiler_params=params(),
-                name=f"middle{level}",
-            )(*operands)
+            early, first_ext = kernel(
+                functools.partial(middle_first_kernel, level, slots),
+                (shape(FIRST), shape(FIRST, f32, long)),
+                (*scalars, received[0], partial, turn),
+                f"middle{level}first",
+            )
+            late, ext = kernel(
+                functools.partial(middle_second_kernel, level, slots),
+                (shape(second), shape(slots, f32, long)),
+                (*scalars, received[1], first_ext, partial, turn),
+                f"middle{level}second",
+            )
+            sends = (early, late)
         else:
-            out = pl.pallas_call(
-                functools.partial(last_kernel, level),
-                out_shape=jax.ShapeDtypeStruct((2, beams // 8, HALF * 8, LANES), f32),
-                in_specs=in_specs,
-                out_specs=VMEM_SPEC,
-                scratch_shapes=[pltpu.VMEM(ext_dims, f32)],
-                compiler_params=params(),
-                name="last",
-            )(*operands)
+            tiles = jax.ShapeDtypeStruct((2, HALF * 8, LANES), f32)
+            tiles, first_ext = kernel(
+                functools.partial(last_first_kernel, level, slots),
+                (tiles, shape(FIRST, f32, long)),
+                (*scalars, received[0], partial, turn),
+                "lastfirst",
+            )
+            out = kernel(
+                functools.partial(last_second_kernel, level, slots),
+                jax.ShapeDtypeStruct((2, beams // 8, HALF * 8, LANES), f32),
+                (*scalars, received[1], first_ext, tiles, partial, turn),
+                "lastsecond",
+                ext_scratch
+                + [pltpu.VMEM((2, beams // 8, HALF * 8, LANES), f32), pltpu.SemaphoreType.DMA((beams // 8,))],
+                HBM_SPEC,
+            )
     out = out.reshape(2, beams // 8, HALF, 8, LANES)
     return jnp.transpose(out, (0, 1, 3, 2, 4)).reshape(2, beams, bins)
 

time: 44.4 us -> 37.2 us (0.84)
  waiting for transfers between devices: 22.6 us -> 10.7 us
  starting transfers between devices: 7.73 us -> 13.3 us
  Pallas kernels: 13.8 us -> 13 us
    ppermute x4 -> x7, waiting for transfers between devices: 22.6 us -> 10.7 us  [the longest x6 10.7 us: local(): received = [lax.ppermute(x, 'pulse', route('pulse', level)) for x in sends]]
    ppermute x4 -> x7, starting transfers between devices: 7.73 us -> 13.3 us  [the longest x6 12.7 us: local(): received = [lax.ppermute(x, 'pulse', route('pulse', level)) for x in sends]]
    pallas_call x8 -> x11, Pallas kernels: 10.6 us -> 9.76 us  [kernel(): pl.pallas_call(function, out_shape=out_shape, in_specs=[SMEM_SPEC] * scal...]
  transfers between devices with their start and end apart: 4 -> 7, of which waited for: 3 -> 4; matrix products, arithmetic and copies ran while one was open for 0% -> 0% of each run, Pallas kernels for 13% -> 20%
where the time goes in v3:
time: 37.2 us; the launch traced here: 37 us
  starting transfers between devices  13.3 us (36%)
  Pallas kernels  13 us (35%)
  waiting for transfers between devices  10.7 us (29%)
    ppermute x6, starting transfers between devices, local(): received = [lax.ppermute(x, 'pulse', route('pulse', level)) for x in sends]  12.7 us
    ppermute x6, waiting for transfers between devices, local(): received = [lax.ppermute(x, 'pulse', route('pulse', level)) for x in sends]  10.7 us
    pallas_call x11, Pallas kernels, kernel(): pl.pallas_call(function, out_shape=out_shape, in_specs=[SMEM_SPEC] * scal...  9.76 us
    pallas_call x1, Pallas kernels, local(): pl.pallas_call(front_kernel, out_shape=(send_shape, rest_shape, *(pltpu.S...  3.22 us
  transfers between devices with their start and end apart: 7, of which 4 were waited for; matrix products, arithmetic and copies ran while one was open for 0% of the time, Pallas kernels for 20%

profile of v3, /device:TPU:0, one launch (start us, length us, event | category | flops | bytes accessed | tf_op | source)
XLA Modules:
  0.0 37.0 jit_solution(6530170085341872234)
XLA Ops:
  0.0 3.2 %front.1 = (bf16[9,2,64,128]{3,2,1,0:T(8,128)(2,1)S(1)}, f32[7,2,64,128]{3,2,1,0:T(8,128)S(1)}, s32[4,2,2,16]{3,2,1,0:T(2,128)S(4)}, s32[4,2,2,16]{3,2,1,0:T(2,1...) custom-call(s32[1]{0:T(128)} %bitcast.index_ref, ...), custom_call_target="tpu_custom_call" | custom-call | tf_op jit(solution)/shard_map/front/pallas_call | solution.py:457
  3.2 0.5 %collective-permute-start = (bf16[9,2,64,128]{3,2,1,0:T(8,128)(2,1)S(1)}, bf16[9,2,64,128]{3,2,1,0:T(8,128)(2,1)S(1)}, u32[]{:S(2)}, u32[]{:S(2)}) collective-permute-start(bf16[9,2,64,128]{3,2,1,0:T(8,128)(2,1)S(1)} %get-tuple-element.36.rest_0_), channel_id=1, source_target_pairs={{0,1},{1,0},{2,3},{3,2},{4,5},{5,4},{6,7},{7,6},{8,9},{9,8},{10,11... | collective-permute-start | bytes 884744 | tf_op jit(solution)/shard_map/ppermute | solution.py:508
  3.7 1.4 %own0.1 = (f32[16,2,64,128]{3,2,1,0:T(8,128)S(1)}, f32[16,2,64,128]{3,2,1,0:T(8,128)S(1)}) custom-call(s32[1]{0:T(128)} %bitcast.index_ref, s32[4,2,2,16]{3,2,1,0:T(2,128)S(4)} %get-tuple-element.33.beam_ref, s32[4,2,2,16]{3,2,1,0:T(2,128)S(4)} %get-tuple-element.34.shift_ref, f32[4,2,2,16]{3,2,1,0:T(2,128)S(4)} %get-tuple-element.37.base_ref, ...), custom_call_target="tpu_custom_call" | custom-call | flops 2000000 | bytes 1048576 | tf_op jit(solution)/shard_map/own0/pallas_call | solution.py:485
  5.1 0.0 collective-permute-done.received_ref
  5.1 0.7 %bottom.1 = (bf16[5,2,64,128]{3,2,1,0:T(8,128)(2,1)S(1)}, bf16[4,2,64,128]{3,2,1,0:T(8,128)(2,1)S(1)}, f32[9,2,128,128]{3,2,1,0:T(8,128)S(1)}) custom-call(s32[1]{0:T(128)} %bitcast.index_ref, s32[4,2,2,16]{3,2,1,0:T(2,128)S(4)} %get-tuple-element.33.beam_ref, s32[4,2,2,16]{3,2,1,0:T(2,128)S(4)} %get-tuple-element.34.shift_ref, ...), custom_call_target="tpu_custom_call" | custom-call | flops 2000000 | bytes 1048576 | tf_op jit(solution)/shard_map/bottom/pallas_call | solution.py:485
  5.8 2.8 %collective-permute-start.2 = (bf16[5,2,64,128]{3,2,1,0:T(8,128)(2,1)S(1)}, bf16[5,2,64,128]{3,2,1,0:T(8,128)(2,1)S(1)}, u32[]{:S(2)}, u32[]{:S(2)}) collective-permute-start(bf16[5,2,64,128]{3,2,1,0:T(8,128)(2,1)S(1)} %get-tuple-element.43.rest_0_), channel_id=1, source_target_pairs={{0,2},{1,3},{2,0},{3,1},{4,6},{5,7},{6,4},{7,5},{8,10},{9,11},{10,... | collective-permute-start | bytes 491528 | tf_op jit(solution)/shard_map/ppermute | solution.py:517
  8.6 0.1 collective-permute-start.1
  8.6 1.5 %own1.1 = (f32[16,2,64,128]{3,2,1,0:T(8,128)S(1)}, f32[16,2,64,128]{3,2,1,0:T(8,128)S(1)}) custom-call(s32[1]{0:T(128)} %bitcast.index_ref, s32[4,2,2,16]{3,2,1,0:T(2,128)S(4)} %get-tuple-element.33.beam_ref, s32[4,2,2,16]{3,2,1,0:T(2,128)S(4)} %get-tuple-element.34.shift_ref, f32[4,2,2,16]{3,2,1,0:T(2,128)S(4)} %get-tuple-element.37.base_ref, ...), custom_call_target="tpu_custom_call" | custom-call | flops 2000000 | bytes 1048576 | tf_op jit(solution)/shard_map/own1/pallas_call | solution.py:485
  10.1 3.4 %collective-permute-done.2.received_ref = bf16[5,2,64,128]{3,2,1,0:T(8,128)(2,1)S(1)} collective-permute-done((bf16[5,2,64,128]{3,2,1,0:T(8,128)(2,1)S(1)}, bf16[5,2,64,128]{3,2,1,0:T(8,128)(2,1)S(1)}, u32[]{:S(2)}, u32[]{:S(2)}) %collective-permute-start.2) | collective-permute-done | bytes 163872 | tf_op jit(solution)/shard_map/ppermute | solution.py:517
  13.5 0.3 middle1first.1
  13.8 2.2 %collective-permute-start.4 = (bf16[5,2,64,128]{3,2,1,0:T(8,128)(2,1)S(1)}, bf16[5,2,64,128]{3,2,1,0:T(8,128)(2,1)S(1)}, u32[]{:S(2)}, u32[]{:S(2)}) collective-permute-start(bf16[5,2,64,128]{3,2,1,0:T(8,128)(2,1)S(1)} %get-tuple-element.49.rest_0_), channel_id=1, source_target_pairs={{0,4},{1,5},{2,6},{3,7},{4,0},{5,1},{6,2},{7,3},{8,12},{9,13},{10,... | collective-permute-start | bytes 491528 | tf_op jit(solution)/shard_map/ppermute | solution.py:517
  16.0 0.0 collective-permute-done.1.received_ref
  16.0 0.3 middle1second.1
  16.3 1.9 %collective-permute-start.3 = (bf16[4,2,64,128]{3,2,1,0:T(8,128)(2,1)S(1)}, bf16[4,2,64,128]{3,2,1,0:T(8,128)(2,1)S(1)}, u32[]{:S(2)}, u32[]{:S(2)}) collective-permute-start(bf16[4,2,64,128]{3,2,1,0:T(8,128)(2,1)S(1)} %get-tuple-element.48.rest_1_), channel_id=1, source_target_pairs={{0,4},{1,5},{2,6},{3,7},{4,0},{5,1},{6,2},{7,3},{8,12},{9,13},{10,... | collective-permute-start | bytes 393224 | tf_op jit(solution)/shard_map/ppermute | solution.py:517
  18.2 1.5 %own2.1 = (f32[16,2,64,128]{3,2,1,0:T(8,128)S(1)}, f32[16,2,64,128]{3,2,1,0:T(8,128)S(1)}) custom-call(s32[1]{0:T(128)} %bitcast.index_ref, s32[4,2,2,16]{3,2,1,0:T(2,128)S(4)} %get-tuple-element.33.beam_ref, s32[4,2,2,16]{3,2,1,0:T(2,128)S(4)} %get-tuple-element.34.shift_ref, f32[4,2,2,16]{3,2,1,0:T(2,128)S(4)} %get-tuple-element.37.base_ref, ...), custom_call_target="tpu_custom_call" | custom-call | flops 2000000 | bytes 1048576 | tf_op jit(solution)/shard_map/own2/pallas_call | solution.py:485
  19.7 0.6 %collective-permute-done.4.received_ref = bf16[5,2,64,128]{3,2,1,0:T(8,128)(2,1)S(1)} collective-permute-done((bf16[5,2,64,128]{3,2,1,0:T(8,128)(2,1)S(1)}, bf16[5,2,64,128]{3,2,1,0:T(8,128)(2,1)S(1)}, u32[]{:S(2)}, u32[]{:S(2)}) %collective-permute-start.4) | collective-permute-done | bytes 163872 | tf_op jit(solution)/shard_map/ppermute | solution.py:517
  20.2 0.3 middle2first.1
  20.5 3.3 %collective-permute-start.6 = (bf16[5,2,64,128]{3,2,1,0:T(8,128)(2,1)S(1)}, bf16[5,2,64,128]{3,2,1,0:T(8,128)(2,1)S(1)}, u32[]{:S(2)}, u32[]{:S(2)}) collective-permute-start(bf16[5,2,64,128]{3,2,1,0:T(8,128)(2,1)S(1)} %get-tuple-element.55.rest_0_), channel_id=1, source_target_pairs={{0,8},{1,9},{2,10},{3,11},{4,12},{5,13},{6,14},{7,15},{8,0},{9,1},... | collective-permute-start | bytes 491528 | tf_op jit(solution)/shard_map/ppermute | solution.py:517
  23.9 0.0 collective-permute-done.3.received_ref
  23.9 0.3 middle2second.1
  24.1 2.5 %collective-permute-start.5 = (bf16[4,2,64,128]{3,2,1,0:T(8,128)(2,1)S(1)}, bf16[4,2,64,128]{3,2,1,0:T(8,128)(2,1)S(1)}, u32[]{:S(2)}, u32[]{:S(2)}) collective-permute-start(bf16[4,2,64,128]{3,2,1,0:T(8,128)(2,1)S(1)} %get-tuple-element.54.rest_1_), channel_id=1, source_target_pairs={{0,8},{1,9},{2,10},{3,11},{4,12},{5,13},{6,14},{7,15},{8,0},{9,1},... | collective-permute-start | bytes 393224 | tf_op jit(solution)/shard_map/ppermute | solution.py:517
  26.6 1.5 %own3.1 = (f32[16,2,64,128]{3,2,1,0:T(8,128)S(1)}, f32[16,2,64,128]{3,2,1,0:T(8,128)S(1)}) custom-call(s32[1]{0:T(128)} %bitcast.index_ref, s32[4,2,2,16]{3,2,1,0:T(2,128)S(4)} %get-tuple-element.33.beam_ref, s32[4,2,2,16]{3,2,1,0:T(2,128)S(4)} %get-tuple-element.34.shift_ref, f32[4,2,2,16]{3,2,1,0:T(2,128)S(4)} %get-tuple-element.37.base_ref, ...), custom_call_target="tpu_custom_call" | custom-call | flops 2000000 | bytes 1048576 | tf_op jit(solution)/shard_map/own3/pallas_call | solution.py:485
  28.1 5.9 %collective-permute-done.6.received_ref = bf16[5,2,64,128]{3,2,1,0:T(8,128)(2,1)S(1)} collective-permute-done((bf16[5,2,64,128]{3,2,1,0:T(8,128)(2,1)S(1)}, bf16[5,2,64,128]{3,2,1,0:T(8,128)(2,1)S(1)}, u32[]{:S(2)}, u32[]{:S(2)}) %collective-permute-start.6) | collective-permute-done | bytes 163872 | tf_op jit(solution)/shard_map/ppermute | solution.py:517
  34.0 0.6 %lastfirst.1 = (f32[2,512,128]{2,1,0:T(8,128)S(1)}, f32[5,2,128,128]{3,2,1,0:T(8,128)S(1)}) custom-call(s32[1]{0:T(128)} %bitcast.index_ref, s32[4,2,2,16]{3,2,1,0:T(2,128)S(4)} %get-tuple-element.33.beam_ref, s32[4,2,2,16]{3,2,1,0:T(2,128)S(4)} %get-tuple-element.34.shift_ref, s32[4,4]{1,0:T(4,128)S(4)} %get-tuple-element.35.taps_ref, ...), custom_call_target="tpu_custom_call" | custom-call | flops 2000000 | bytes 1048576 | tf_op jit(solution)/shard_map/lastfirst/pallas_call | solution.py:485
  34.6 0.8 %collective-permute-done.5.received_ref = bf16[4,2,64,128]{3,2,1,0:T(8,128)(2,1)S(1)} collective-permute-done((bf16[4,2,64,128]{3,2,1,0:T(8,128)(2,1)S(1)}, bf16[4,2,64,128]{3,2,1,0:T(8,128)(2,1)S(1)}, u32[]{:S(2)}, u32[]{:S(2)}) %collective-permute-start.5) | collective-permute-done | bytes 131104 | tf_op jit(solution)/shard_map/ppermute | solution.py:517
  35.4 1.6 %lastsecond.1 = f32[2,2,512,128]{3,2,1,0:T(8,128)} custom-call(s32[1]{0:T(128)} %bitcast.index_ref, s32[4,2,2,16]{3,2,1,0:T(2,128)S(4)} %get-tuple-element.33.beam_ref, s32[4,2,2,16]{3,2,1,0:T(2,128)S(4)} %get-tuple-element.34.shift_ref, s32[4,4]{1,0:T(4,128)S(4)} %get-tuple-element.35.taps_ref, ...), custom_call_target="tpu_custom_call" | custom-call | flops 2000000 | bytes 1048576 | tf_op jit(solution)/shard_map/lastsecond/pallas_call | solution.py:485
Async XLA Ops:
  3.2 1.9 %collective-permute-start = (bf16[9,2,64,128]{3,2,1,0:T(8,128)(2,1)S(1)}, bf16[9,2,64,128]{3,2,1,0:T(8,128)(2,1)S(1)}, u32[]{:S(2)}, u32[]{:S(2)}) collective-permute-start(bf16[9,2,64,128]{3,2,1,0:T(8,128)(2,1)S(1)} %get-tuple-element.36.rest_0_), channel_id=1, source_target_pairs={{0,1},{1,0},{2,3},{3,2},{4,5},{5,4},{6,7},{7,6},{8,9},{9,8},{10,11... | collective-permute-start | bytes 884744 | tf_op jit(solution)/shard_map/ppermute | solution.py:508
  5.8 7.7 %collective-permute-start.2 = (bf16[5,2,64,128]{3,2,1,0:T(8,128)(2,1)S(1)}, bf16[5,2,64,128]{3,2,1,0:T(8,128)(2,1)S(1)}, u32[]{:S(2)}, u32[]{:S(2)}) collective-permute-start(bf16[5,2,64,128]{3,2,1,0:T(8,128)(2,1)S(1)} %get-tuple-element.43.rest_0_), channel_id=1, source_target_pairs={{0,2},{1,3},{2,0},{3,1},{4,6},{5,7},{6,4},{7,5},{8,10},{9,11},{10,... | collective-permute-start | bytes 491528 | tf_op jit(solution)/shard_map/ppermute | solution.py:517
  8.6 7.5 %collective-permute-start.1 = (bf16[4,2,64,128]{3,2,1,0:T(8,128)(2,1)S(1)}, bf16[4,2,64,128]{3,2,1,0:T(8,128)(2,1)S(1)}, u32[]{:S(2)}, u32[]{:S(2)}) collective-permute-start(bf16[4,2,64,128]{3,2,1,0:T(8,128)(2,1)S(1)} %get-tuple-element.42.rest_1_), channel_id=1, source_target_pairs={{0,2},{1,3},{2,0},{3,1},{4,6},{5,7},{6,4},{7,5},{8,10},{9,11},{10,... | collective-permute-start | bytes 393224 | tf_op jit(solution)/shard_map/ppermute | solution.py:517
  13.8 6.4 %collective-permute-start.4 = (bf16[5,2,64,128]{3,2,1,0:T(8,128)(2,1)S(1)}, bf16[5,2,64,128]{3,2,1,0:T(8,128)(2,1)S(1)}, u32[]{:S(2)}, u32[]{:S(2)}) collective-permute-start(bf16[5,2,64,128]{3,2,1,0:T(8,128)(2,1)S(1)} %get-tuple-element.49.rest_0_), channel_id=1, source_target_pairs={{0,4},{1,5},{2,6},{3,7},{4,0},{5,1},{6,2},{7,3},{8,12},{9,13},{10,... | collective-permute-start | bytes 491528 | tf_op jit(solution)/shard_map/ppermute | solution.py:517
  16.3 7.6 %collective-permute-start.3 = (bf16[4,2,64,128]{3,2,1,0:T(8,128)(2,1)S(1)}, bf16[4,2,64,128]{3,2,1,0:T(8,128)(2,1)S(1)}, u32[]{:S(2)}, u32[]{:S(2)}) collective-permute-start(bf16[4,2,64,128]{3,2,1,0:T(8,128)(2,1)S(1)} %get-tuple-element.48.rest_1_), channel_id=1, source_target_pairs={{0,4},{1,5},{2,6},{3,7},{4,0},{5,1},{6,2},{7,3},{8,12},{9,13},{10,... | collective-permute-start | bytes 393224 | tf_op jit(solution)/shard_map/ppermute | solution.py:517
  20.5 13.5 %collective-permute-start.6 = (bf16[5,2,64,128]{3,2,1,0:T(8,128)(2,1)S(1)}, bf16[5,2,64,128]{3,2,1,0:T(8,128)(2,1)S(1)}, u32[]{:S(2)}, u32[]{:S(2)}) collective-permute-start(bf16[5,2,64,128]{3,2,1,0:T(8,128)(2,1)S(1)} %get-tuple-element.55.rest_0_), channel_id=1, source_target_pairs={{0,8},{1,9},{2,10},{3,11},{4,12},{5,13},{6,14},{7,15},{8,0},{9,1},... | collective-permute-start | bytes 491528 | tf_op jit(solution)/shard_map/ppermute | solution.py:517
  24.1 11.3 %collective-permute-start.5 = (bf16[4,2,64,128]{3,2,1,0:T(8,128)(2,1)S(1)}, bf16[4,2,64,128]{3,2,1,0:T(8,128)(2,1)S(1)}, u32[]{:S(2)}, u32[]{:S(2)}) collective-permute-start(bf16[4,2,64,128]{3,2,1,0:T(8,128)(2,1)S(1)} %get-tuple-element.54.rest_1_), channel_id=1, source_target_pairs={{0,8},{1,9},{2,10},{3,11},{4,12},{5,13},{6,14},{7,15},{8,0},{9,1},... | collective-permute-start | bytes 393224 | tf_op jit(solution)/shard_map/ppermute | solution.py:517

commit v4 on v3

--- a/solution.py
+++ b/solution.py
@@ -14,8 +14,7 @@
 HALO = 32
 LANES = 128
 HALF = 64
-FIRST = 5
-ORDERED = (1, 2)
+PARTS = {0: (9,), 1: (5, 4), 2: (5, 4), 3: (5, 4)}
 SQRT_HALF = 0.7071067811865476
 VMEM_LIMIT = 24 * 2**20
 
@@ -74,12 +73,13 @@
 
 
 def front_kernel(
-    index_ref, raw_hbm, matched_hbm, delays_hbm, phase_hbm, *rest
+    index_ref, raw_hbm, matched_hbm, phase_hbm, *rest
 ):
-    tables, rest = rest[:5], rest[5:]
-    send_ref, rest_ref, rest = rest[0], rest[1], rest[2:]
-    copied, rest = rest[:5], rest[5:]
-    raw, matched, phase, delays, raw32, taps, windows, ext, trig, trig_smem, sems = rest
+    tables, rest = rest[:6], rest[6:]
+    send_ref, ext, trig, rest = rest[0], rest[1], rest[2], rest[3:]
+    copied, rest = rest[:6], rest[6:]
+    delays = copied[0]
+    raw, matched, phase, raw32, taps, windows, sems = rest
     pulses, beams = phase.shape
     rows = raw.shape[0] // 2
     blocks = rows // pulses
@@ -90,14 +90,13 @@
     small = [
         pltpu.make_async_copy(matched_hbm, matched, sems.at[0]),
         pltpu.make_async_copy(phase_hbm, phase, sems.at[1]),
-        pltpu.make_async_copy(delays_hbm, delays, sems.at[2]),
     ]
     small += [
-        pltpu.make_async_copy(source, target, sems.at[4 + i]) for i, (source, target) in enumerate(zip(tables, copied))
+        pltpu.make_async_copy(source, target, sems.at[2 + i]) for i, (source, target) in enumerate(zip(tables, copied))
     ]
     large = [
         pltpu.make_async_copy(
-            raw_hbm.at[pl.ds(pair * size, size)], raw.at[pl.ds(pair * size, size)], sems.at[4 + len(tables) + pair]
+            raw_hbm.at[pl.ds(pair * size, size)], raw.at[pl.ds(pair * size, size)], sems.at[2 + len(tables) + pair]
         )
         for pair in range(pairs)
     ]
@@ -109,11 +108,10 @@
         copy.start()
     small[1].wait()
     scale = 1.0 / math.sqrt(pulses)
-    c, s = cos_sin_turns(phase[...] * (0.5 / math.pi))
-    trig[0] = c * scale
-    trig[1] = s * scale
-    factors = pltpu.make_async_copy(trig, trig_smem, sems.at[3])
-    factors.start()
+    pair_of = cos_sin_turns(phase[...] * (0.5 / math.pi))
+    for part in range(2):
+        for k in range(beams):
+            trig[part, k] = jnp.broadcast_to(pair_of[part][:, k : k + 1] * scale, (pulses, LANES))
     small[0].wait()
     row = lax.broadcasted_iota(jnp.int32, (LANES, LANES), 0)
     column = lax.broadcasted_iota(jnp.int32, (LANES, LANES), 1)
@@ -156,39 +154,36 @@
             b = made[part * LANES + HALF : (part + 1) * LANES]
             store_extended(ext, (2 * pair, part), jnp.where(lane < HALF, a, pltpu.roll(b, HALF, 1)))
             store_extended(ext, (2 * pair + 1, part), jnp.where(lane < HALF, pltpu.roll(a, HALF, 1), b))
-    factors.wait()
     small[2].wait()
-    urgent = (1 - side_bit) * 7
     count = send_ref.shape[0]
-    piece = 32
-
-    def beam(m, carry, sent):
-        k = (urgent + m) % beams
-        for first_row in range(0, HALF, piece):
-            real = imag = None
-            for p in range(pulses):
-                start = delays[p, k] + (HALO + first_row)
-                x = ext[p, 0, pl.ds(start, piece), :]
-                y = ext[p, 1, pl.ds(start, piece), :]
-                cosine = trig_smem[0, p, k]
-                sine = trig_smem[1, p, k]
-                re = x * cosine - y * sine
-                im = x * sine + y * cosine
-                real = re if real is None else real + re
-                imag = im if imag is None else imag + im
-            rows_here = pl.ds(first_row, piece)
-            if sent:
-                send_ref[m, 0, rows_here] = real.astype(jnp.bfloat16)
-                send_ref[m, 1, rows_here] = imag.astype(jnp.bfloat16)
-            else:
-                rest_ref[m - count, 0, rows_here] = real
-                rest_ref[m - count, 1, rows_here] = imag
+    start = order_start(0, index_ref[0] ^ 1)
+
+    def beam(m, carry):
+        k = (1 - side_bit) * 7 + slot_at(m, start, count)
+        for first_row in range(0, HALF, 32):
+            pair = projected(k, first_row, 32, delays, trig, ext)
+            for part in range(2):
+                send_ref[m, part, pl.ds(first_row, 32)] = pair[part].astype(jnp.bfloat16)
         return carry
 
-    lax.fori_loop(0, count, functools.partial(beam, sent=True), 0, unroll=3)
-    lax.fori_loop(count, beams, functools.partial(beam, sent=False), 0, unroll=7)
+    lax.fori_loop(0, count, beam, 0, unroll=3)
     for copy in small[3:]:
         copy.wait()
+
+
+def projected(k, first_row, rows, delays, trig, ext):
+    real = imag = None
+    for p in range(ext.shape[0]):
+        here = pl.ds(delays[p, k] + (HALO + first_row), rows)
+        x = ext[p, 0, here, :]
+        y = ext[p, 1, here, :]
+        cosine = trig[0, k, pl.ds(p, 1), :]
+        sine = trig[1, k, pl.ds(p, 1), :]
+        re = x * cosine - y * sine
+        im = x * sine + y * cosine
+        real = re if real is None else real + re
+        imag = im if imag is None else imag + im
+    return real, imag
 
 
 def tap_factors(taps_ref, level):
@@ -214,6 +209,9 @@
 
 
 def order_start(level, index):
+    if level == 0:
+        first_beam = 7 * (1 - ((index >> 1) & 1)) + order_start(1, index ^ 2)
+        return jnp.maximum(first_beam // 2 + (index & 1) - 1, 0)
     first, second, third = (index >> 1) & 1, (index >> 2) & 1, (index >> 3) & 1
     if level == 1:
         low = (1 - third) * first
@@ -234,17 +232,16 @@
     return jnp.where(slot >= count, slot - count, slot)
 
 
-def merged(level, index, k, first_row, rows, tables, factors, count, ext, partial_ref, turn_ref):
+def merged(level, index, k, at, first_row, rows, tables, factors, count, ext, partial_ref, turn_ref):
     beam_ref, shift_ref = tables
     side_bit = (index >> level) % 2
     other = (level, side_bit, 1 - side_bit, k)
     slot = beam_ref[other] - side_bit * 7
-    if level in ORDERED:
-        slot = place_of(slot, order_start(level, index), count)
+    slot = place_of(slot, order_start(level, index), count)
     start = shift_ref[other] + (HALO + first_row)
     here = pl.ds(first_row, rows)
-    real, imag = times(filtered(ext, slot, start, rows, *factors), (turn_ref[k, 0, here], turn_ref[k, 1, here]))
-    return real + partial_ref[k, 0, here], imag + partial_ref[k, 1, here]
+    real, imag = times(filtered(ext, slot, start, rows, *factors), (turn_ref[at, 0, here], turn_ref[at, 1, here]))
+    return real + partial_ref[at, 0, here], imag + partial_ref[at, 1, here]
 
 
 def turns(base, rate, bins):
@@ -259,46 +256,87 @@
     return tuple(jnp.concatenate([g[i] for g in groups], axis=0) for i in range(2))
 
 
-def own_kernel(
-    level, bins, count, index_ref, beam_ref, shift_ref, base_ref, rate_ref, taps_ref, *rest
+def read_sent(refs, place, part):
+    value = None
+    first = 0
+    for ref in refs:
+        size = ref.shape[0]
+        here = ref[jnp.clip(place - first, 0, size - 1), part].astype(jnp.float32)
+        value = here if value is None else jnp.where(place >= first, here, value)
+        first += size
+    return value
+
+
+def bottom_beam(index, rank, count, beams):
+    first = (1 - ((index >> 1) & 1)) * 7
+    if rank < count:
+        return first + slot_at(rank, order_start(1, index ^ 2), count)
+    return (first + rank) % beams
+
+
+def bottom_own_kernel(
+    bins, count, first_place, first_rank, index_ref, beam_ref, shift_ref, base_ref, rate_ref, taps_ref, delays, pulse_ext,
+    trig, *rest
 ):
-    if level == 0:
-        (send_ref, rest_ref, partial_ref, turn_ref, ext) = rest
-    else:
-        (first_ref, second_ref, received_ext, last_partial, last_turn, partial_ref, turn_ref, ext) = rest
+    if first_place > 0:
+        copy_extended(rest[0], rest[-1])
+        rest = rest[1:]
+    partial_ref, turn_ref, ext = rest
+    index = index_ref[0]
+    side_bit = index % 2
+    start = order_start(0, index)
+    for place in range(first_place, ext.shape[0]):
+        k = side_bit * 7 + slot_at(place, start, count)
+        pieces = [projected(k, first_row, 32, delays, trig, pulse_ext) for first_row in range(0, HALF, 32)]
+        for part in range(2):
+            store_extended(ext, (place, part), jnp.concatenate([x[part] for x in pieces], axis=0))
+    factors = tap_factors(taps_ref, 0)
+    for at in range(partial_ref.shape[0]):
+        k = bottom_beam(index, first_rank + at, count, delays.shape[1])
+        own = (0, side_bit, side_bit, k)
+        other = (0, side_bit, 1 - side_bit, k)
+        slot = place_of(beam_ref[own] - side_bit * 7, start, count)
+        turn = turns(base_ref[own], rate_ref[own], bins)
+        for first_row in range(0, HALF, 32):
+            here = slice(first_row, first_row + 32)
+            pair = times(
+                filtered(ext, slot, shift_ref[own] + (HALO + first_row), 32, *factors), (turn[0][here], turn[1][here])
+            )
+            partial_ref[at, 0, here], partial_ref[at, 1, here] = pair
+        turn_ref[at, 0], turn_ref[at, 1] = turns(base_ref[other], rate_ref[other], bins)
+
+
+def own_kernel(level, bins, count, index_ref, beam_ref, shift_ref, base_ref, rate_ref, taps_ref, *rest):
+    sent = len(PARTS[level])
+    sent_refs, rest = rest[:sent], list(rest[sent:])
+    received_ext, last_partial, last_turn = rest[:3]
+    rest = rest[3:]
+    own_turn = rest.pop(0) if level == 2 else None
+    partial_ref = rest.pop(0)
+    turn_ref = rest.pop(0) if level != 2 else None
+    next_own, next_turn = (rest.pop(0), rest.pop(0)) if level == 1 else (None, None)
+    ext = rest.pop(0)
     index = index_ref[0]
     side_bit = (index >> level) % 2
+    next_bit = (index >> 2) % 2
     beams = partial_ref.shape[0]
     shared = 2 * count - beams
     low_beam = side_bit * 7
     urgent = (1 - side_bit) * 7
 
-    start = order_start(level, index ^ (1 << level))
     for i in range(shared):
-        slot = 7 * side_bit + i
+        place = place_of(7 * side_bit + i, order_start(level, index ^ (1 << level)), count)
         for part in range(2):
-            if level == 0:
-                body = send_ref[slot, part].astype(jnp.float32)
-            else:
-                place = place_of(slot, start, count)
-                in_first = place < FIRST
-                body = jnp.where(
-                    in_first,
-                    first_ref[jnp.minimum(place, FIRST - 1), part].astype(jnp.float32),
-                    second_ref[jnp.maximum(place - FIRST, 0), part].astype(jnp.float32),
-                )
-            store_extended(ext, (7 * (1 - side_bit) + i, part), body)
-    if level > 0:
-        last_factors = tap_factors(taps_ref, level - 1)
+            store_extended(ext, (7 * (1 - side_bit) + i, part), read_sent(sent_refs, place, part))
+    last_factors = tap_factors(taps_ref, level - 1)
 
     def remaining(m, carry):
         k = (urgent + m) % beams
-        if level == 0:
-            pair = rest_ref[m - count, 0], rest_ref[m - count, 1]
-        else:
-            pair = merged(
-                level - 1, index, k, 0, HALF, (beam_ref, shift_ref), last_factors, count, received_ext, last_partial, last_turn
-            )
+        at = m - PARTS[1][0] if level == 1 else k
+        pair = merged(
+            level - 1, index, k, at, 0, HALF, (beam_ref, shift_ref), last_factors, count, received_ext, last_partial,
+            last_turn,
+        )
         for part in range(2):
             store_extended(ext, (k - low_beam, part), pair[part])
         return carry
@@ -311,7 +349,10 @@
         other = (level, side_bit, 1 - side_bit, k)
         slot = beam_ref[own] - low_beam
         start = shift_ref[own] + HALO
-        turn = turns(base_ref[own], rate_ref[own], bins)
+        if own_turn is None:
+            turn = turns(base_ref[own], rate_ref[own], bins)
+        else:
+            turn = own_turn[k, 0], own_turn[k, 1]
         for first_row in range(0, HALF, 32):
             here = slice(first_row, first_row + 32)
             real, imag = times(
@@ -319,19 +360,21 @@
             )
             partial_ref[k, 0, here] = real
             partial_ref[k, 1, here] = imag
-        turn_ref[k, 0], turn_ref[k, 1] = turns(base_ref[other], rate_ref[other], bins)
+        if turn_ref is not None:
+            turn_ref[k, 0], turn_ref[k, 1] = turns(base_ref[other], rate_ref[other], bins)
+        if next_own is not None:
+            for target, side in ((next_own, next_bit), (next_turn, 1 - next_bit)):
+                entry = (level + 1, next_bit, side, k)
+                target[k, 0], target[k, 1] = turns(base_ref[entry], rate_ref[entry], bins)
         return carry
 
     lax.fori_loop(0, beams, beam, 0, unroll=2)
 
 
-def extend_received(received_ref, ext, first, unroll):
-    def extend(slot, carry):
+def extend_received(received_ref, ext, first, number, source=0):
+    for i in range(number):
         for part in range(2):
-            store_extended(ext, (first + slot, part), received_ref[slot, part].astype(jnp.float32))
-        return carry
-
-    lax.fori_loop(0, received_ref.shape[0], extend, 0, unroll=unroll)
+            store_extended(ext, (first + i, part), received_ref[source + i, part].astype(jnp.float32))
 
 
 def copy_extended(source, target):
@@ -339,60 +382,79 @@
         target[slot] = source[slot]
 
 
-def send_parents(level, index, places, sends, tables, factors, count, ext, partial_ref, turn_ref):
+def send_parents(level, index, first_place, sends, tables, factors, count, ext, partial_ref, turn_ref, offset=None):
     next_bit = (index >> (level + 1)) % 2
     start = order_start(level + 1, index ^ (2 << level))
-    for place in places:
-        k = (1 - next_bit) * 7 + slot_at(place, start, count)
-        target, at = (sends[0], place) if place < FIRST else (sends[-1], place - FIRST)
-        for first_row in range(0, HALF, 32):
-            pair = merged(level, index, k, first_row, 32, tables, factors, count, ext, partial_ref, turn_ref)
-            for part in range(2):
-                target[at, part, pl.ds(first_row, 32)] = pair[part].astype(jnp.bfloat16)
-
-
-def bottom_kernel(
-    count, index_ref, beam_ref, shift_ref, taps_ref, received_ref, partial_ref, turn_ref, first_ref, second_ref, ext,
+    place = first_place
+    for target in sends:
+        for at in range(target.shape[0]):
+            k = (1 - next_bit) * 7 + slot_at(place, start, count)
+            row = k if offset is None else place - offset
+            for first_row in range(0, HALF, 32):
+                pair = merged(level, index, k, row, first_row, 32, tables, factors, count, ext, partial_ref, turn_ref)
+                for part in range(2):
+                    target[at, part, pl.ds(first_row, 32)] = pair[part].astype(jnp.bfloat16)
+            place += 1
+
+
+def bottom_first_kernel(
+    count, index_ref, beam_ref, shift_ref, taps_ref, received_ref, partial_ref, turn_ref, send_ref, ext
 ):
-    extend_received(received_ref, ext, 0, 3)
+    extend_received(received_ref, ext, 0, ext.shape[0])
     send_parents(
-        0, index_ref[0], range(count), (first_ref, second_ref), (beam_ref, shift_ref), tap_factors(taps_ref, 0), count,
-        ext, partial_ref, turn_ref,
+        0, index_ref[0], 0, (send_ref,), (beam_ref, shift_ref), tap_factors(taps_ref, 0), count, ext, partial_ref,
+        turn_ref, 0,
+    )
+
+
+def bottom_second_kernel(
+    count, index_ref, beam_ref, shift_ref, taps_ref, received_ref, first_ext, partial_ref, turn_ref, *outs
+):
+    sends, ext = outs[:-1], outs[-1]
+    first = first_ext.shape[0]
+    extend_received(received_ref, ext, first, count - first, first)
+    copy_extended(first_ext, ext)
+    send_parents(
+        0, index_ref[0], first, sends, (beam_ref, shift_ref), tap_factors(taps_ref, 0), count, ext, partial_ref,
+        turn_ref, first,
     )
 
 
 def middle_first_kernel(
     level, count, index_ref, beam_ref, shift_ref, taps_ref, received_ref, partial_ref, turn_ref, send_ref, ext,
 ):
-    extend_received(received_ref, ext, 0, 5)
+    extend_received(received_ref, ext, 0, received_ref.shape[0])
     send_parents(
-        level, index_ref[0], range(FIRST), (send_ref,), (beam_ref, shift_ref), tap_factors(taps_ref, level), count,
+        level, index_ref[0], 0, (send_ref,), (beam_ref, shift_ref), tap_factors(taps_ref, level), count,
         ext, partial_ref, turn_ref,
     )
 
 
 def middle_second_kernel(
-    level, count, index_ref, beam_ref, shift_ref, taps_ref, received_ref, first_ext, partial_ref, turn_ref, send_ref, ext,
+    level, count, index_ref, beam_ref, shift_ref, taps_ref, received_ref, first_ext, partial_ref, turn_ref, *outs
 ):
-    extend_received(received_ref, ext, FIRST, 4)
+    sends, ext = outs[:-1], outs[-1]
+    extend_received(received_ref, ext, first_ext.shape[0], received_ref.shape[0])
     copy_extended(first_ext, ext)
     send_parents(
-        level, index_ref[0], range(FIRST, count), (send_ref,), (beam_ref, shift_ref), tap_factors(taps_ref, level), count,
+        level, index_ref[0], PARTS[level + 1][0], sends, (beam_ref, shift_ref), tap_factors(taps_ref, level), count,
         ext, partial_ref, turn_ref,
     )
 
 
-def place_pair(level, index, m, out_ref, high, low, tables, factors, count, ext, partial_ref, turn_ref):
+def make_pair(level, index, q, tables, factors, count, ext, partial_ref, turn_ref):
+    even = merged(level, index, 2 * q, 2 * q, 0, HALF, tables, factors, count, ext, partial_ref, turn_ref)
+    odd = merged(level, index, 2 * q + 1, 2 * q + 1, 0, HALF, tables, factors, count, ext, partial_ref, turn_ref)
+    return even, odd
+
+
+def place_pair(even, odd, out_ref, where, low):
     lane = lane_iota(HALF)
-    even = merged(level, index, 2 * m, 0, HALF, tables, factors, count, ext, partial_ref, turn_ref)
-    odd = merged(level, index, 2 * m + 1, 0, HALF, tables, factors, count, ext, partial_ref, turn_ref)
-    for part in range(2):
-        turned = jnp.concatenate([even[part], odd[part]], axis=0).T
-        a = turned[:HALF]
-        b = turned[HALF:]
-        where = (part,) if high is None else (part, high)
-        out_ref[(*where, pl.ds(low, HALF, stride=8))] = jnp.where(lane < HALF, a, pltpu.roll(b, HALF, 1))
-        out_ref[(*where, pl.ds(low + 1, HALF, stride=8))] = jnp.where(lane < HALF, pltpu.roll(a, HALF, 1), b)
+    turned = jnp.concatenate([even, odd], axis=0).T
+    a = turned[:HALF]
+    b = turned[HALF:]
+    out_ref[(*where, pl.ds(low, HALF, stride=8))] = jnp.where(lane < HALF, a, pltpu.roll(b, HALF, 1))
+    out_ref[(*where, pl.ds(low + 1, HALF, stride=8))] = jnp.where(lane < HALF, pltpu.roll(a, HALF, 1), b)
 
 
 EARLY = 3
@@ -401,32 +463,36 @@
 def last_first_kernel(
     level, count, index_ref, beam_ref, shift_ref, taps_ref, received_ref, partial_ref, turn_ref, tiles_ref, ext,
 ):
-    extend_received(received_ref, ext, 0, 5)
+    extend_received(received_ref, ext, 0, received_ref.shape[0])
     factors = tap_factors(taps_ref, level)
-    for m in range(EARLY):
-        place_pair(
-            level, index_ref[0], m, tiles_ref, None, 2 * m, (beam_ref, shift_ref), factors, count, ext, partial_ref, turn_ref
+    for q in range(EARLY):
+        even, odd = make_pair(
+            level, index_ref[0], q, (beam_ref, shift_ref), factors, count, ext, partial_ref, turn_ref
         )
+        for part in range(2):
+            place_pair(even[part], odd[part], tiles_ref, (part,), 2 * q)
 
 
 def last_second_kernel(
     level, count, index_ref, beam_ref, shift_ref, taps_ref, received_ref, first_ext, tiles_ref, partial_ref, turn_ref, out_hbm,
     ext, tiles, sems,
 ):
+    extend_received(received_ref, ext, first_ext.shape[0], received_ref.shape[0])
+    copy_extended(first_ext, ext)
     tiles[:, 0] = tiles_ref[...]
-    extend_received(received_ref, ext, FIRST, 4)
-    copy_extended(first_ext, ext)
     factors = tap_factors(taps_ref, level)
     copies = []
-    for m in range(EARLY, partial_ref.shape[0] // 2):
-        high, low = m // 4, 2 * (m % 4)
-        place_pair(
-            level, index_ref[0], m, tiles, high, low, (beam_ref, shift_ref), factors, count, ext, partial_ref, turn_ref
+    for q in range(EARLY, partial_ref.shape[0] // 2):
+        even, odd = make_pair(
+            level, index_ref[0], q, (beam_ref, shift_ref), factors, count, ext, partial_ref, turn_ref
         )
-        if low == 6:
-            copy = pltpu.make_async_copy(tiles.at[:, high], out_hbm.at[:, high], sems.at[high])
-            copy.start()
-            copies.append(copy)
+        high, low = q // 4, 2 * (q % 4)
+        for part in range(2):
+            place_pair(even[part], odd[part], tiles, (part, high), low)
+            if low == 6:
+                copy = pltpu.make_async_copy(tiles.at[part, high], out_hbm.at[part, high], sems.at[part, high])
+                copy.start()
+                copies.append(copy)
     for copy in copies:
         copy.wait()
 
@@ -449,28 +515,25 @@
     index = lax.axis_index("pulse").astype(jnp.int32).reshape(1)
     f32, bf16 = jnp.float32, jnp.bfloat16
     image_shape = jax.ShapeDtypeStruct((beams, 2, HALF, LANES), f32)
-    rest_shape = jax.ShapeDtypeStruct((beams - slots, 2, HALF, LANES), f32)
     send_shape = jax.ShapeDtypeStruct((slots, 2, HALF, LANES), bf16)
     rows = pulses * blocks
-    inputs = (beam_map, range_shift, phase_base, phase_rate, tap_offsets)
-    sources = (raw_echoes.reshape(rows * parts, hop), matched, delays, pulse_phase, *inputs)
-    send, rest, *tables = pl.pallas_call(
+    inputs = (delays, beam_map, range_shift, phase_base, phase_rate, tap_offsets)
+    sources = (raw_echoes.reshape(rows * parts, hop), matched, pulse_phase, *inputs)
+    pulse_shape = jax.ShapeDtypeStruct((pulses, 2, HALF + 2 * HALO, LANES), f32)
+    trig_shape = jax.ShapeDtypeStruct((2, beams, pulses, LANES), f32)
+    send, pulse_ext, trig, delay_table, *tables = pl.pallas_call(
         front_kernel,
-        out_shape=(send_shape, rest_shape, *(pltpu.SMEM(x.shape, x.dtype) for x in inputs)),
-        in_specs=[SMEM_SPEC] + [HBM_SPEC] * (4 + len(inputs)),
-        out_specs=(VMEM_SPEC, VMEM_SPEC, *(SMEM_SPEC for x in inputs)),
+        out_shape=(send_shape, pulse_shape, trig_shape, *(pltpu.SMEM(x.shape, x.dtype) for x in inputs)),
+        in_specs=[SMEM_SPEC] + [HBM_SPEC] * len(sources),
+        out_specs=(VMEM_SPEC, VMEM_SPEC, VMEM_SPEC, *(SMEM_SPEC for x in inputs)),
         scratch_shapes=[
             pltpu.VMEM((parts * rows, LANES), bf16),
             pltpu.VMEM(matched.shape, f32),
             pltpu.VMEM(pulse_phase.shape, f32),
-            pltpu.SMEM(delays.shape, jnp.int32),
             pltpu.VMEM((16 + parts * rows, LANES), f32),
             pltpu.VMEM((2 * LANES, 4 * LANES), bf16),
             pltpu.VMEM((rows, 4 * LANES), bf16),
-            pltpu.VMEM((pulses, 2, HALF + 2 * HALO, LANES), f32),
-            pltpu.VMEM((2, pulses, beams), f32),
-            pltpu.SMEM((2, pulses, beams), f32),
-            pltpu.SemaphoreType.DMA((4 + len(inputs) + rows // LANES,)),
+            pltpu.SemaphoreType.DMA((2 + len(inputs) + rows // LANES,)),
         ],
         compiler_params=params(),
         name="front",
@@ -494,47 +557,75 @@
         )(*operands)
 
     own_scalars = (index, *tables)
-    second = slots - FIRST
     long = HALF + 2 * HALO
-    images = (image_shape, image_shape)
     ext_scratch = [pltpu.VMEM((slots, 2, long, LANES), f32)]
 
-    def own(level, *operands):
+    def own(level, outs, *operands):
         return kernel(
-            functools.partial(own_kernel, level, bins, slots), images, own_scalars + operands, f"own{level}", ext_scratch,
-            scalar_count=len(own_scalars),
+            functools.partial(own_kernel, level, bins, slots), (image_shape,) * outs, own_scalars + operands, f"own{level}",
+            ext_scratch, scalar_count=len(own_scalars),
         )
 
     received = lax.ppermute(send, "pulse", route("pulse", 0))
-    partial, turn = own(0, send, rest)
-    *sends, ext = kernel(
-        functools.partial(bottom_kernel, slots),
-        (shape(FIRST), shape(second), shape(slots, f32, long)),
+    first, later = PARTS[1]
+    bottom_scalars = (*own_scalars, delay_table)
+    partial, turn, own_ext = kernel(
+        functools.partial(bottom_own_kernel, bins, slots, 0, 0),
+        (shape(first, f32), shape(first, f32), shape(first, f32, long)),
+        (*bottom_scalars, pulse_ext, trig),
+        "bottomownfirst",
+        scalar_count=len(bottom_scalars),
+    )
+    early, first_ext = kernel(
+        functools.partial(bottom_first_kernel, slots),
+        (shape(first), shape(first, f32, long)),
         (*scalars, received, partial, turn),
-        "bottom",
-    )
+        "bottomfirst",
+    )
+    partial, turn = kernel(
+        functools.partial(bottom_own_kernel, bins, slots, first, first),
+        (shape(beams - first, f32), shape(beams - first, f32)),
+        (*bottom_scalars, pulse_ext, trig, own_ext),
+        "bottomownsecond",
+        ext_scratch,
+        scalar_count=len(bottom_scalars),
+    )
+    late, ext = kernel(
+        functools.partial(bottom_second_kernel, slots),
+        (shape(later), shape(slots, f32, long)),
+        (*scalars, received, first_ext, partial, turn),
+        "bottomsecond",
+    )
+    sends = (early, late)
     for level in range(1, levels):
         received = [lax.ppermute(x, "pulse", route("pulse", level)) for x in sends]
-        partial, turn = own(level, *sends, ext, partial, turn)
+        if level == 1:
+            partial, turn, own_turn, next_turn = own(level, 4, *sends, ext, partial, turn)
+        elif level == 2:
+            (partial,) = own(level, 1, *sends, ext, partial, turn, own_turn)
+            turn = next_turn
+        else:
+            partial, turn = own(level, 2, *sends, ext, partial, turn)
         if level < levels - 1:
+            following = PARTS[level + 1]
             early, first_ext = kernel(
                 functools.partial(middle_first_kernel, level, slots),
-                (shape(FIRST), shape(FIRST, f32, long)),
+                (shape(following[0]), shape(PARTS[level][0], f32, long)),
                 (*scalars, received[0], partial, turn),
                 f"middle{level}first",
             )
-            late, ext = kernel(
+            *late, ext = kernel(
                 functools.partial(middle_second_kernel, level, slots),
-                (shape(second), shape(slots, f32, long)),
+                (*(shape(n) for n in following[1:]), shape(slots, f32, long)),
                 (*scalars, received[1], first_ext, partial, turn),
                 f"middle{level}second",
             )
-            sends = (early, late)
+            sends = (early, *late)
         else:
             tiles = jax.ShapeDtypeStruct((2, HALF * 8, LANES), f32)
             tiles, first_ext = kernel(
                 functools.partial(last_first_kernel, level, slots),
-                (tiles, shape(FIRST, f32, long)),
+                (tiles, shape(PARTS[level][0], f32, long)),
                 (*scalars, received[0], partial, turn),
                 "lastfirst",
             )
@@ -544,7 +635,7 @@
                 (*scalars, received[1], first_ext, tiles, partial, turn),
                 "lastsecond",
                 ext_scratch
-                + [pltpu.VMEM((2, beams // 8, HALF * 8, LANES), f32), pltpu.SemaphoreType.DMA((beams // 8,))],
+                + [pltpu.VMEM((2, beams // 8, HALF * 8, LANES), f32), pltpu.SemaphoreType.DMA((2, beams // 8))],
                 HBM_SPEC,
             )
     out = out.reshape(2, beams // 8, HALF, 8, LANES)

time: 37.2 us -> 35.9 us (0.965)
  waiting for transfers between devices: 10.7 us -> 9.36 us
    ppermute x6, waiting for transfers between devices: 10.7 us -> 8.94 us  [local(): received = [lax.ppermute(x, 'pulse', route('pulse', level)) for x in sends]]
    pallas_call x1, Pallas kernels: 3.22 us -> 2.72 us  [local(): pl.pallas_call(front_kernel, out_shape=(send_shape, pulse_shape, trig_sha...]
    ppermute x1, waiting for transfers between devices: 0.01 us -> 0.42 us  [local(): received = lax.ppermute(send, 'pulse', route('pulse', 0))]
    pallas_call x11 -> x13, Pallas kernels: 9.76 us -> 10.1 us  [kernel(): pl.pallas_call(function, out_shape=out_shape, in_specs=[SMEM_SPEC] * scal...]
  transfers between devices with their start and end apart: 7 -> 7, of which waited for: 4 -> 5; matrix products, arithmetic and copies ran while one was open for 0% -> 0% of each run, Pallas kernels for 20% -> 23%
where the time goes in v4:
time: 35.9 us; the launch traced here: 35.8 us
  starting transfers between devices  13.5 us (38%)
  Pallas kernels  12.8 us (36%)
  waiting for transfers between devices  9.36 us (26%)
    ppermute x6, starting transfers between devices, local(): received = [lax.ppermute(x, 'pulse', route('pulse', level)) for x in sends]  13 us
    pallas_call x13, Pallas kernels, kernel(): pl.pallas_call(function, out_shape=out_shape, in_specs=[SMEM_SPEC] * scal...  10.1 us
    ppermute x6, waiting for transfers between devices, local(): received = [lax.ppermute(x, 'pulse', route('pulse', level)) for x in sends]  8.94 us
    pallas_call x1, Pallas kernels, local(): pl.pallas_call(front_kernel, out_shape=(send_shape, pulse_shape, trig_sha...  2.72 us
  transfers between devices with their start and end apart: 7, of which 5 were waited for; matrix products, arithmetic and copies ran while one was open for 0% of the time, Pallas kernels for 23%

profile of v4, /device:TPU:0, one launch (start us, length us, event | category | flops | bytes accessed | tf_op | source)
XLA Modules:
  0.0 35.8 jit_solution(5683196676048056992)
XLA Ops:
  0.0 2.7 %front.1 = (bf16[9,2,64,128]{3,2,1,0:T(8,128)(2,1)S(1)}, f32[8,2,128,128]{3,2,1,0:T(8,128)S(1)}, f32[2,16,8,128]{3,2,1,0:T(8,128)S(1)}, s32[8,16]{1,0:T(8,128)S(...) custom-call(s32[1]{0:T(128)} %bitcast.index_ref, ...), custom_call_target="tpu_custom_call" | custom-call | tf_op jit(solution)/shard_map/front/pallas_call | solution.py:524
  2.7 0.5 %collective-permute-start = (bf16[9,2,64,128]{3,2,1,0:T(8,128)(2,1)S(1)}, bf16[9,2,64,128]{3,2,1,0:T(8,128)(2,1)S(1)}, u32[]{:S(2)}, u32[]{:S(2)}) collective-permute-start(bf16[9,2,64,128]{3,2,1,0:T(8,128)(2,1)S(1)} %get-tuple-element.42), channel_id=1, source_target_pairs={{0,1},{1,0},{2,3},{3,2},{4,5},{5,4},{6,7},{7,6},{8,9},{9,8},{10,11... | collective-permute-start | bytes 884744 | tf_op jit(solution)/shard_map/ppermute | solution.py:569
  3.2 0.8 %bottomownfirst.1 = (f32[5,2,64,128]{3,2,1,0:T(8,128)S(1)}, f32[5,2,64,128]{3,2,1,0:T(8,128)S(1)}, f32[5,2,128,128]{3,2,1,0:T(8,128)S(1)}) custom-call(s32[1]{0:T(128)} %bitcast.index_ref, s32[4,2,2,16]{3,2,1,0:T(2,128)S(4)} %get-tuple-element.39.beam_ref, s32[4,2,2,16]{3,2,1,0:T(2,128)S(4)} %get-tuple-element.40.shift_ref, ...), custom_call_target="tpu_custom_call" | custom-call | flops 2000000 | bytes 1048576 | tf_op jit(solution)/shard_map/bottomownfirst/pallas_call | solution.py:548
  4.0 0.4 %collective-permute-done.received_ref = bf16[9,2,64,128]{3,2,1,0:T(8,128)(2,1)S(1)} collective-permute-done((bf16[9,2,64,128]{3,2,1,0:T(8,128)(2,1)S(1)}, bf16[9,2,64,128]{3,2,1,0:T(8,128)(2,1)S(1)}, u32[]{:S(2)}, u32[]{:S(2)}) %collective-permute-start) | collective-permute-done | bytes 294944 | tf_op jit(solution)/shard_map/ppermute | solution.py:569
  4.5 0.3 bottomfirst.1
  4.8 2.9 %collective-permute-start.2 = (bf16[5,2,64,128]{3,2,1,0:T(8,128)(2,1)S(1)}, bf16[5,2,64,128]{3,2,1,0:T(8,128)(2,1)S(1)}, u32[]{:S(2)}, u32[]{:S(2)}) collective-permute-start(bf16[5,2,64,128]{3,2,1,0:T(8,128)(2,1)S(1)} %get-tuple-element.55.rest_0_), channel_id=1, source_target_pairs={{0,2},{1,3},{2,0},{3,1},{4,6},{5,7},{6,4},{7,5},{8,10},{9,11},{10,... | collective-permute-start | bytes 491528 | tf_op jit(solution)/shard_map/ppermute | solution.py:601
  7.7 1.0 %bottomownsecond.1 = (f32[11,2,64,128]{3,2,1,0:T(8,128)S(1)}, f32[11,2,64,128]{3,2,1,0:T(8,128)S(1)}) custom-call(s32[1]{0:T(128)} %bitcast.index_ref, s32[4,2,2,16]{3,2,1,0:T(2,128)S(4)} %get-tuple-element.39.beam_ref, s32[4,2,2,16]{3,2,1,0:T(2,128)S(4)} %get-tuple-element.40.shift_ref, f32[4,2,2,16]{3,2,1,0:T(2,128)S(4)} %get-tuple-element.43.base_ref, ...), custom_call_target="tpu_custom_call" | custom-call | flops 2000000 | bytes 1048576 | tf_op jit(solution)/shard_map/bottomownsecond/pallas_call | solution.py:548
  8.7 0.3 bottomsecond.1
  9.0 0.1 collective-permute-start.1
  9.1 2.0 %own1.1 = (f32[16,2,64,128]{3,2,1,0:T(8,128)S(1)}, f32[16,2,64,128]{3,2,1,0:T(8,128)S(1)}, f32[16,2,64,128]{3,2,1,0:T(8,128)S(1)}, f32[16,2,64,128]{3,2,1,0:T(8,128)S(1)}) custom-call(s32[1]{0:T(128)} %bitcast.index_ref, s32[4,2,2,16]{3,2,1,0:T(2,128)S(4)} %get-tuple-element.39.beam_ref, s32[4,2,2,16]{3,2,1,0:T(2,128)S(4)} %get-tuple-element.40.shift_ref, ...), custom_call_target="tpu_custom_call" | custom-call | flops 2000000 | bytes 1048576 | tf_op jit(solution)/shard_map/own1/pallas_call | solution.py:548
  11.1 1.6 %collective-permute-done.2.received_ref = bf16[5,2,64,128]{3,2,1,0:T(8,128)(2,1)S(1)} collective-permute-done((bf16[5,2,64,128]{3,2,1,0:T(8,128)(2,1)S(1)}, bf16[5,2,64,128]{3,2,1,0:T(8,128)(2,1)S(1)}, u32[]{:S(2)}, u32[]{:S(2)}) %collective-permute-start.2) | collective-permute-done | bytes 163872 | tf_op jit(solution)/shard_map/ppermute | solution.py:601
  12.7 0.3 middle1first.1
  13.0 2.2 %collective-permute-start.4 = (bf16[5,2,64,128]{3,2,1,0:T(8,128)(2,1)S(1)}, bf16[5,2,64,128]{3,2,1,0:T(8,128)(2,1)S(1)}, u32[]{:S(2)}, u32[]{:S(2)}) collective-permute-start(bf16[5,2,64,128]{3,2,1,0:T(8,128)(2,1)S(1)} %get-tuple-element.61.rest_0_), channel_id=1, source_target_pairs={{0,4},{1,5},{2,6},{3,7},{4,0},{5,1},{6,2},{7,3},{8,12},{9,13},{10,... | collective-permute-start | bytes 491528 | tf_op jit(solution)/shard_map/ppermute | solution.py:601
  15.2 0.0 collective-permute-done.1.received_ref
  15.2 0.3 middle1second.1
  15.5 1.7 %collective-permute-start.3 = (bf16[4,2,64,128]{3,2,1,0:T(8,128)(2,1)S(1)}, bf16[4,2,64,128]{3,2,1,0:T(8,128)(2,1)S(1)}, u32[]{:S(2)}, u32[]{:S(2)}) collective-permute-start(bf16[4,2,64,128]{3,2,1,0:T(8,128)(2,1)S(1)} %get-tuple-element.60.rest_1_), channel_id=1, source_target_pairs={{0,4},{1,5},{2,6},{3,7},{4,0},{5,1},{6,2},{7,3},{8,12},{9,13},{10,... | collective-permute-start | bytes 393224 | tf_op jit(solution)/shard_map/ppermute | solution.py:601
  17.2 1.0 %own2.1.partial_ref.rest_3_ = f32[16,2,64,128]{3,2,1,0:T(8,128)S(1)} custom-call(s32[1]{0:T(128)} %bitcast.index_ref, s32[4,2,2,16]{3,2,1,0:T(2,128)S(4)} %get-tuple-element.39.beam_ref, s32[4,2,2,16]{3,2,1,0:T(2,128)S(4)} %get-tuple-element.40.shift_ref, f32[4,2,2,16]{3,2,1,0:T(2,128)S(4)} %get-tuple-element.43.base_ref, ...), custom_call_target="tpu_custom_call" | custom-call | flops 2000000 | bytes 1048576 | tf_op jit(solution)/shard_map/own2/pallas_call | solution.py:548
  18.1 1.4 %collective-permute-done.4.received_ref = bf16[5,2,64,128]{3,2,1,0:T(8,128)(2,1)S(1)} collective-permute-done((bf16[5,2,64,128]{3,2,1,0:T(8,128)(2,1)S(1)}, bf16[5,2,64,128]{3,2,1,0:T(8,128)(2,1)S(1)}, u32[]{:S(2)}, u32[]{:S(2)}) %collective-permute-start.4) | collective-permute-done | bytes 163872 | tf_op jit(solution)/shard_map/ppermute | solution.py:601
  19.5 0.3 middle2first.1
  19.8 3.6 %collective-permute-start.6 = (bf16[5,2,64,128]{3,2,1,0:T(8,128)(2,1)S(1)}, bf16[5,2,64,128]{3,2,1,0:T(8,128)(2,1)S(1)}, u32[]{:S(2)}, u32[]{:S(2)}) collective-permute-start(bf16[5,2,64,128]{3,2,1,0:T(8,128)(2,1)S(1)} %get-tuple-element.67.rest_0_), channel_id=1, source_target_pairs={{0,8},{1,9},{2,10},{3,11},{4,12},{5,13},{6,14},{7,15},{8,0},{9,1},... | collective-permute-start | bytes 491528 | tf_op jit(solution)/shard_map/ppermute | solution.py:601
  23.4 0.0 collective-permute-done.3.received_ref
  23.4 0.3 middle2second.1
  23.6 2.5 %collective-permute-start.5 = (bf16[4,2,64,128]{3,2,1,0:T(8,128)(2,1)S(1)}, bf16[4,2,64,128]{3,2,1,0:T(8,128)(2,1)S(1)}, u32[]{:S(2)}, u32[]{:S(2)}) collective-permute-start(bf16[4,2,64,128]{3,2,1,0:T(8,128)(2,1)S(1)} %get-tuple-element.66.rest_1_), channel_id=1, source_target_pairs={{0,8},{1,9},{2,10},{3,11},{4,12},{5,13},{6,14},{7,15},{8,0},{9,1},... | collective-permute-start | bytes 393224 | tf_op jit(solution)/shard_map/ppermute | solution.py:601
  26.1 1.5 %own3.1 = (f32[16,2,64,128]{3,2,1,0:T(8,128)S(1)}, f32[16,2,64,128]{3,2,1,0:T(8,128)S(1)}) custom-call(s32[1]{0:T(128)} %bitcast.index_ref, s32[4,2,2,16]{3,2,1,0:T(2,128)S(4)} %get-tuple-element.39.beam_ref, s32[4,2,2,16]{3,2,1,0:T(2,128)S(4)} %get-tuple-element.40.shift_ref, f32[4,2,2,16]{3,2,1,0:T(2,128)S(4)} %get-tuple-element.43.base_ref, ...), custom_call_target="tpu_custom_call" | custom-call | flops 2000000 | bytes 1048576 | tf_op jit(solution)/shard_map/own3/pallas_call | solution.py:548
  27.6 5.2 %collective-permute-done.6.received_ref = bf16[5,2,64,128]{3,2,1,0:T(8,128)(2,1)S(1)} collective-permute-done((bf16[5,2,64,128]{3,2,1,0:T(8,128)(2,1)S(1)}, bf16[5,2,64,128]{3,2,1,0:T(8,128)(2,1)S(1)}, u32[]{:S(2)}, u32[]{:S(2)}) %collective-permute-start.6) | collective-permute-done | bytes 163872 | tf_op jit(solution)/shard_map/ppermute | solution.py:601
  32.8 0.6 %lastfirst.1 = (f32[2,512,128]{2,1,0:T(8,128)S(1)}, f32[5,2,128,128]{3,2,1,0:T(8,128)S(1)}) custom-call(s32[1]{0:T(128)} %bitcast.index_ref, s32[4,2,2,16]{3,2,1,0:T(2,128)S(4)} %get-tuple-element.39.beam_ref, s32[4,2,2,16]{3,2,1,0:T(2,128)S(4)} %get-tuple-element.40.shift_ref, s32[4,4]{1,0:T(4,128)S(4)} %get-tuple-element.41.taps_ref, ...), custom_call_target="tpu_custom_call" | custom-call | flops 2000000 | bytes 1048576 | tf_op jit(solution)/shard_map/lastfirst/pallas_call | solution.py:548
  33.4 0.8 %collective-permute-done.5.received_ref = bf16[4,2,64,128]{3,2,1,0:T(8,128)(2,1)S(1)} collective-permute-done((bf16[4,2,64,128]{3,2,1,0:T(8,128)(2,1)S(1)}, bf16[4,2,64,128]{3,2,1,0:T(8,128)(2,1)S(1)}, u32[]{:S(2)}, u32[]{:S(2)}) %collective-permute-start.5) | collective-permute-done | bytes 131104 | tf_op jit(solution)/shard_map/ppermute | solution.py:601
  34.2 1.6 %lastsecond.1 = f32[2,2,512,128]{3,2,1,0:T(8,128)} custom-call(s32[1]{0:T(128)} %bitcast.index_ref, s32[4,2,2,16]{3,2,1,0:T(2,128)S(4)} %get-tuple-element.39.beam_ref, s32[4,2,2,16]{3,2,1,0:T(2,128)S(4)} %get-tuple-element.40.shift_ref, s32[4,4]{1,0:T(4,128)S(4)} %get-tuple-element.41.taps_ref, ...), custom_call_target="tpu_custom_call" | custom-call | flops 2000000 | bytes 1048576 | tf_op jit(solution)/shard_map/lastsecond/pallas_call | solution.py:548
Async XLA Ops:
  2.7 1.7 %collective-permute-start = (bf16[9,2,64,128]{3,2,1,0:T(8,128)(2,1)S(1)}, bf16[9,2,64,128]{3,2,1,0:T(8,128)(2,1)S(1)}, u32[]{:S(2)}, u32[]{:S(2)}) collective-permute-start(bf16[9,2,64,128]{3,2,1,0:T(8,128)(2,1)S(1)} %get-tuple-element.42), channel_id=1, source_target_pairs={{0,1},{1,0},{2,3},{3,2},{4,5},{5,4},{6,7},{7,6},{8,9},{9,8},{10,11... | collective-permute-start | bytes 884744 | tf_op jit(solution)/shard_map/ppermute | solution.py:569
  4.8 7.9 %collective-permute-start.2 = (bf16[5,2,64,128]{3,2,1,0:T(8,128)(2,1)S(1)}, bf16[5,2,64,128]{3,2,1,0:T(8,128)(2,1)S(1)}, u32[]{:S(2)}, u32[]{:S(2)}) collective-permute-start(bf16[5,2,64,128]{3,2,1,0:T(8,128)(2,1)S(1)} %get-tuple-element.55.rest_0_), channel_id=1, source_target_pairs={{0,2},{1,3},{2,0},{3,1},{4,6},{5,7},{6,4},{7,5},{8,10},{9,11},{10,... | collective-permute-start | bytes 491528 | tf_op jit(solution)/shard_map/ppermute | solution.py:601
  9.0 6.2 %collective-permute-start.1 = (bf16[4,2,64,128]{3,2,1,0:T(8,128)(2,1)S(1)}, bf16[4,2,64,128]{3,2,1,0:T(8,128)(2,1)S(1)}, u32[]{:S(2)}, u32[]{:S(2)}) collective-permute-start(bf16[4,2,64,128]{3,2,1,0:T(8,128)(2,1)S(1)} %get-tuple-element.54.rest_1_), channel_id=1, source_target_pairs={{0,2},{1,3},{2,0},{3,1},{4,6},{5,7},{6,4},{7,5},{8,10},{9,11},{10,... | collective-permute-start | bytes 393224 | tf_op jit(solution)/shard_map/ppermute | solution.py:601
  13.0 6.5 %collective-permute-start.4 = (bf16[5,2,64,128]{3,2,1,0:T(8,128)(2,1)S(1)}, bf16[5,2,64,128]{3,2,1,0:T(8,128)(2,1)S(1)}, u32[]{:S(2)}, u32[]{:S(2)}) collective-permute-start(bf16[5,2,64,128]{3,2,1,0:T(8,128)(2,1)S(1)} %get-tuple-element.61.rest_0_), channel_id=1, source_target_pairs={{0,4},{1,5},{2,6},{3,7},{4,0},{5,1},{6,2},{7,3},{8,12},{9,13},{10,... | collective-permute-start | bytes 491528 | tf_op jit(solution)/shard_map/ppermute | solution.py:601
  15.5 7.9 %collective-permute-start.3 = (bf16[4,2,64,128]{3,2,1,0:T(8,128)(2,1)S(1)}, bf16[4,2,64,128]{3,2,1,0:T(8,128)(2,1)S(1)}, u32[]{:S(2)}, u32[]{:S(2)}) collective-permute-start(bf16[4,2,64,128]{3,2,1,0:T(8,128)(2,1)S(1)} %get-tuple-element.60.rest_1_), channel_id=1, source_target_pairs={{0,4},{1,5},{2,6},{3,7},{4,0},{5,1},{6,2},{7,3},{8,12},{9,13},{10,... | collective-permute-start | bytes 393224 | tf_op jit(solution)/shard_map/ppermute | solution.py:601
  19.8 13.0 %collective-permute-start.6 = (bf16[5,2,64,128]{3,2,1,0:T(8,128)(2,1)S(1)}, bf16[5,2,64,128]{3,2,1,0:T(8,128)(2,1)S(1)}, u32[]{:S(2)}, u32[]{:S(2)}) collective-permute-start(bf16[5,2,64,128]{3,2,1,0:T(8,128)(2,1)S(1)} %get-tuple-element.67.rest_0_), channel_id=1, source_target_pairs={{0,8},{1,9},{2,10},{3,11},{4,12},{5,13},{6,14},{7,15},{8,0},{9,1},... | collective-permute-start | bytes 491528 | tf_op jit(solution)/shard_map/ppermute | solution.py:601
  23.6 10.5 %collective-permute-start.5 = (bf16[4,2,64,128]{3,2,1,0:T(8,128)(2,1)S(1)}, bf16[4,2,64,128]{3,2,1,0:T(8,128)(2,1)S(1)}, u32[]{:S(2)}, u32[]{:S(2)}) collective-permute-start(bf16[4,2,64,128]{3,2,1,0:T(8,128)(2,1)S(1)} %get-tuple-element.66.rest_1_), channel_id=1, source_target_pairs={{0,8},{1,9},{2,10},{3,11},{4,12},{5,13},{6,14},{7,15},{8,0},{9,1},... | collective-permute-start | bytes 393224 | tf_op jit(solution)/shard_map/ppermute | solution.py:601

commit v5 on v4

--- a/solution.py
+++ b/solution.py
@@ -14,7 +14,7 @@
 HALO = 32
 LANES = 128
 HALF = 64
-PARTS = {0: (9,), 1: (5, 4), 2: (5, 4), 3: (5, 4)}
+PARTS = {0: (5, 4), 1: (5, 4), 2: (5, 4), 3: (5, 4)}
 SQRT_HALF = 0.7071067811865476
 VMEM_LIMIT = 24 * 2**20
 
@@ -39,6 +39,26 @@
 
 SMEM_SPEC = pl.BlockSpec(memory_space=pltpu.SMEM)
 VMEM_SPEC = pl.BlockSpec(memory_space=pltpu.VMEM)
+COSTS = {
+    "bottomownfirst": 800,
+    "bottomfirst": 300,
+    "bottomownsecond": 1050,
+    "bottomsecond": 270,
+    "own1": 1500,
+    "frontsecond": 350,
+    "turns2": 500,
+    "middle1first": 310,
+    "own2first": 600,
+    "middle1second": 180,
+    "middle2first": 320,
+    "own2second": 640,
+    "middle2second": 260,
+    "own3": 1470,
+    "lastfirst": 570,
+    "lastsecond": 1550,
+}
+COSTS = {name: 1000 * cost for name, cost in COSTS.items()}
+
 HBM_SPEC = pl.BlockSpec(memory_space=pltpu.HBM)
 
 
@@ -85,7 +105,6 @@
     blocks = rows // pulses
     pairs = rows // LANES
     size = raw.shape[0] // pairs
-    side_bit = index_ref[0] % 2
 
     small = [
         pltpu.make_async_copy(matched_hbm, matched, sems.at[0]),
@@ -100,19 +119,16 @@
         )
         for pair in range(pairs)
     ]
-    small[1].start()
-    small[0].start()
-    for copy in large:
+    for copy in large[:1] + small[:2] + large[1:] + small[2:]:
         copy.start()
-    for copy in small[2:]:
-        copy.start()
-    small[1].wait()
+    raw32[0:16] = jnp.zeros((16, LANES), jnp.float32)
+    for copy in small[:2] + large:
+        copy.wait()
     scale = 1.0 / math.sqrt(pulses)
     pair_of = cos_sin_turns(phase[...] * (0.5 / math.pi))
     for part in range(2):
         for k in range(beams):
             trig[part, k] = jnp.broadcast_to(pair_of[part][:, k : k + 1] * scale, (pulses, LANES))
-    small[0].wait()
     row = lax.broadcasted_iota(jnp.int32, (LANES, LANES), 0)
     column = lax.broadcasted_iota(jnp.int32, (LANES, LANES), 1)
     for part in range(2):
@@ -130,11 +146,9 @@
             taps[LANES:, 0:LANES] = before
             taps[0:LANES, 3 * LANES :] = -now
             taps[LANES:, 2 * LANES : 3 * LANES] = now
-    raw32[0:16] = jnp.zeros((16, LANES), jnp.float32)
     first = lax.broadcasted_iota(jnp.int32, (LANES, LANES), 0) % blocks == 0
     lane = lane_iota(HALF)
     for pair in range(pairs):
-        large[pair].wait()
         raw32[16 + pair * size : 16 + (pair + 1) * size] = raw[pair * size : (pair + 1) * size, :].astype(jnp.float32)
         mine = slice(pair * LANES, (pair + 1) * LANES)
         for part in range(2):
@@ -155,20 +169,24 @@
             store_extended(ext, (2 * pair, part), jnp.where(lane < HALF, a, pltpu.roll(b, HALF, 1)))
             store_extended(ext, (2 * pair + 1, part), jnp.where(lane < HALF, pltpu.roll(a, HALF, 1), b))
     small[2].wait()
-    count = send_ref.shape[0]
-    start = order_start(0, index_ref[0] ^ 1)
-
-    def beam(m, carry):
-        k = (1 - side_bit) * 7 + slot_at(m, start, count)
+    send_pulses(index_ref[0], 0, send_ref, delays, trig, ext)
+    for copy in small[3:]:
+        copy.wait()
+
+
+def send_pulses(index, first_place, send_ref, delays, trig, ext):
+    count = sum(PARTS[0])
+    start = order_start(0, index ^ 1)
+    for at in range(send_ref.shape[0]):
+        k = (1 - index % 2) * 7 + slot_at(first_place + at, start, count)
         for first_row in range(0, HALF, 32):
             pair = projected(k, first_row, 32, delays, trig, ext)
             for part in range(2):
-                send_ref[m, part, pl.ds(first_row, 32)] = pair[part].astype(jnp.bfloat16)
-        return carry
-
-    lax.fori_loop(0, count, beam, 0, unroll=3)
-    for copy in small[3:]:
-        copy.wait()
+                send_ref[at, part, pl.ds(first_row, 32)] = pair[part].astype(jnp.bfloat16)
+
+
+def front_second_kernel(index_ref, delays, pulse_ext, trig, after_ref, send_ref):
+    send_pulses(index_ref[0], PARTS[0][0], send_ref, delays, trig, pulse_ext)
 
 
 def projected(k, first_row, rows, delays, trig, ext):
@@ -267,10 +285,10 @@
     return value
 
 
-def bottom_beam(index, rank, count, beams):
-    first = (1 - ((index >> 1) & 1)) * 7
+def rank_beam(level, index, rank, count, beams):
+    first = (1 - ((index >> (level + 1)) & 1)) * 7
     if rank < count:
-        return first + slot_at(rank, order_start(1, index ^ 2), count)
+        return first + slot_at(rank, order_start(level + 1, index ^ (2 << level)), count)
     return (first + rank) % beams
 
 
@@ -292,7 +310,7 @@
             store_extended(ext, (place, part), jnp.concatenate([x[part] for x in pieces], axis=0))
     factors = tap_factors(taps_ref, 0)
     for at in range(partial_ref.shape[0]):
-        k = bottom_beam(index, first_rank + at, count, delays.shape[1])
+        k = rank_beam(0, index, first_rank + at, count, delays.shape[1])
         own = (0, side_bit, side_bit, k)
         other = (0, side_bit, 1 - side_bit, k)
         slot = place_of(beam_ref[own] - side_bit * 7, start, count)
@@ -311,14 +329,11 @@
     sent_refs, rest = rest[:sent], list(rest[sent:])
     received_ext, last_partial, last_turn = rest[:3]
     rest = rest[3:]
-    own_turn = rest.pop(0) if level == 2 else None
     partial_ref = rest.pop(0)
-    turn_ref = rest.pop(0) if level != 2 else None
-    next_own, next_turn = (rest.pop(0), rest.pop(0)) if level == 1 else (None, None)
+    turn_ref = rest.pop(0)
     ext = rest.pop(0)
     index = index_ref[0]
     side_bit = (index >> level) % 2
-    next_bit = (index >> 2) % 2
     beams = partial_ref.shape[0]
     shared = 2 * count - beams
     low_beam = side_bit * 7
@@ -332,7 +347,7 @@
 
     def remaining(m, carry):
         k = (urgent + m) % beams
-        at = m - PARTS[1][0] if level == 1 else k
+        at = m - PARTS[1][0] if level == 1 else m
         pair = merged(
             level - 1, index, k, at, 0, HALF, (beam_ref, shift_ref), last_factors, count, received_ext, last_partial,
             last_turn,
@@ -349,10 +364,7 @@
         other = (level, side_bit, 1 - side_bit, k)
         slot = beam_ref[own] - low_beam
         start = shift_ref[own] + HALO
-        if own_turn is None:
-            turn = turns(base_ref[own], rate_ref[own], bins)
-        else:
-            turn = own_turn[k, 0], own_turn[k, 1]
+        turn = turns(base_ref[own], rate_ref[own], bins)
         for first_row in range(0, HALF, 32):
             here = slice(first_row, first_row + 32)
             real, imag = times(
@@ -360,21 +372,69 @@
             )
             partial_ref[k, 0, here] = real
             partial_ref[k, 1, here] = imag
-        if turn_ref is not None:
-            turn_ref[k, 0], turn_ref[k, 1] = turns(base_ref[other], rate_ref[other], bins)
-        if next_own is not None:
-            for target, side in ((next_own, next_bit), (next_turn, 1 - next_bit)):
-                entry = (level + 1, next_bit, side, k)
-                target[k, 0], target[k, 1] = turns(base_ref[entry], rate_ref[entry], bins)
+        turn_ref[k, 0], turn_ref[k, 1] = turns(base_ref[other], rate_ref[other], bins)
         return carry
 
     lax.fori_loop(0, beams, beam, 0, unroll=2)
 
 
-def extend_received(received_ref, ext, first, number, source=0):
+def turns_kernel(level, bins, index_ref, base_ref, rate_ref, after_ref, own_ref, other_ref):
+    index = index_ref[0]
+    side_bit = (index >> level) % 2
+    beams = own_ref.shape[0]
+
+    def beam(rank, carry):
+        k = ((1 - ((index >> (level + 1)) & 1)) * 7 + rank) % beams
+        for target, side in ((own_ref, side_bit), (other_ref, 1 - side_bit)):
+            entry = (level, side_bit, side, k)
+            target[rank, 0], target[rank, 1] = turns(base_ref[entry], rate_ref[entry], bins)
+        return carry
+
+    lax.fori_loop(0, beams, beam, 0, unroll=4)
+
+
+def split_own_kernel(
+    level, count, late, index_ref, beam_ref, shift_ref, taps_ref, *rest
+):
+    if late:
+        received_ext, last_partial, last_turn, own_turn, own_ext, partial_ref, ext = rest
+        first_place, first_rank = own_ext.shape[0], own_ext.shape[0]
+        copy_extended(own_ext, ext)
+    else:
+        first_ext, received_ref, last_partial, last_turn, own_turn, received_ext, partial_ref, ext = rest
+        first_place, first_rank = 0, 0
+        extend_received(received_ref, received_ext, first_ext.shape[0], received_ref.shape[0])
+        copy_extended(first_ext, received_ext)
+    index = index_ref[0]
+    side_bit = (index >> level) % 2
+    start = order_start(level, index)
+    last_factors = tap_factors(taps_ref, level - 1)
+    for place in range(first_place, ext.shape[0]):
+        k = side_bit * 7 + slot_at(place, start, count)
+        pair = merged(
+            level - 1, index, k, k, 0, HALF, (beam_ref, shift_ref), last_factors, count, received_ext, last_partial,
+            last_turn,
+        )
+        for part in range(2):
+            store_extended(ext, (place, part), pair[part])
+    factors = tap_factors(taps_ref, level)
+    for rank in range(first_rank, partial_ref.shape[0]):
+        k = rank_beam(level, index, rank, count, own_turn.shape[0])
+        own = (level, side_bit, side_bit, k)
+        slot = place_of(beam_ref[own] - side_bit * 7, start, count)
+        for first_row in range(0, HALF, 32):
+            here = pl.ds(first_row, 32)
+            pair = times(
+                filtered(ext, slot, shift_ref[own] + (HALO + first_row), 32, *factors),
+                (own_turn[rank, 0, here], own_turn[rank, 1, here]),
+            )
+            partial_ref[rank, 0, here], partial_ref[rank, 1, here] = pair
+
+
+def extend_received(received_ref, ext, first, number):
     for i in range(number):
         for part in range(2):
-            store_extended(ext, (first + i, part), received_ref[source + i, part].astype(jnp.float32))
+            store_extended(ext, (first + i, part), received_ref[i, part].astype(jnp.float32))
 
 
 def copy_extended(source, target):
@@ -412,7 +472,7 @@
 ):
     sends, ext = outs[:-1], outs[-1]
     first = first_ext.shape[0]
-    extend_received(received_ref, ext, first, count - first, first)
+    extend_received(received_ref, ext, first, count - first)
     copy_extended(first_ext, ext)
     send_parents(
         0, index_ref[0], first, sends, (beam_ref, shift_ref), tap_factors(taps_ref, 0), count, ext, partial_ref,
@@ -421,24 +481,32 @@
 
 
 def middle_first_kernel(
-    level, count, index_ref, beam_ref, shift_ref, taps_ref, received_ref, partial_ref, turn_ref, send_ref, ext,
+    level, offset, count, index_ref, beam_ref, shift_ref, taps_ref, received_ref, partial_ref, turn_ref, send_ref, ext,
 ):
     extend_received(received_ref, ext, 0, received_ref.shape[0])
     send_parents(
         level, index_ref[0], 0, (send_ref,), (beam_ref, shift_ref), tap_factors(taps_ref, level), count,
+        ext, partial_ref, turn_ref, offset,
+    )
+
+
+def late_send_kernel(
+    level, count, index_ref, beam_ref, shift_ref, taps_ref, ext, partial_ref, turn_ref, send_ref,
+):
+    send_parents(
+        level, index_ref[0], PARTS[level + 1][0], (send_ref,), (beam_ref, shift_ref), tap_factors(taps_ref, level), count,
         ext, partial_ref, turn_ref,
     )
 
 
 def middle_second_kernel(
-    level, count, index_ref, beam_ref, shift_ref, taps_ref, received_ref, first_ext, partial_ref, turn_ref, *outs
-):
-    sends, ext = outs[:-1], outs[-1]
+    level, count, index_ref, beam_ref, shift_ref, taps_ref, received_ref, first_ext, partial_ref, turn_ref, send_ref, ext
+):
     extend_received(received_ref, ext, first_ext.shape[0], received_ref.shape[0])
     copy_extended(first_ext, ext)
     send_parents(
-        level, index_ref[0], PARTS[level + 1][0], sends, (beam_ref, shift_ref), tap_factors(taps_ref, level), count,
-        ext, partial_ref, turn_ref,
+        level, index_ref[0], PARTS[level + 1][0], (send_ref,), (beam_ref, shift_ref), tap_factors(taps_ref, level), count,
+        ext, partial_ref, turn_ref, 0,
     )
 
 
@@ -515,7 +583,7 @@
     index = lax.axis_index("pulse").astype(jnp.int32).reshape(1)
     f32, bf16 = jnp.float32, jnp.bfloat16
     image_shape = jax.ShapeDtypeStruct((beams, 2, HALF, LANES), f32)
-    send_shape = jax.ShapeDtypeStruct((slots, 2, HALF, LANES), bf16)
+    send_shape = jax.ShapeDtypeStruct((PARTS[0][0], 2, HALF, LANES), bf16)
     rows = pulses * blocks
     inputs = (delays, beam_map, range_shift, phase_base, phase_rate, tap_offsets)
     sources = (raw_echoes.reshape(rows * parts, hop), matched, pulse_phase, *inputs)
@@ -552,12 +620,13 @@
             out_specs=jax.tree.map(lambda x: VMEM_SPEC, out_shape) if out_specs is None else out_specs,
             scratch_shapes=list(scratch),
             compiler_params=params(),
-            cost_estimate=pl.CostEstimate(flops=2 * 10**6, bytes_accessed=2**20, transcendentals=0),
+            cost_estimate=pl.CostEstimate(flops=COSTS[name], bytes_accessed=2**20, transcendentals=0),
             name=name,
         )(*operands)
 
     own_scalars = (index, *tables)
     long = HALF + 2 * HALO
+    images = (image_shape, image_shape)
     ext_scratch = [pltpu.VMEM((slots, 2, long, LANES), f32)]
 
     def own(level, outs, *operands):
@@ -566,7 +635,10 @@
             ext_scratch, scalar_count=len(own_scalars),
         )
 
-    received = lax.ppermute(send, "pulse", route("pulse", 0))
+    def exchange(x, level):
+        return lax.ppermute(x, "pulse", route("pulse", level))
+
+    received = exchange(send, 0)
     first, later = PARTS[1]
     bottom_scalars = (*own_scalars, delay_table)
     partial, turn, own_ext = kernel(
@@ -582,6 +654,13 @@
         (*scalars, received, partial, turn),
         "bottomfirst",
     )
+    send = kernel(
+        front_second_kernel,
+        shape(PARTS[0][1]),
+        (index, delay_table, pulse_ext, trig, early),
+        "frontsecond",
+        scalar_count=2,
+    )
     partial, turn = kernel(
         functools.partial(bottom_own_kernel, bins, slots, first, first),
         (shape(beams - first, f32), shape(beams - first, f32)),
@@ -593,51 +672,74 @@
     late, ext = kernel(
         functools.partial(bottom_second_kernel, slots),
         (shape(later), shape(slots, f32, long)),
-        (*scalars, received, first_ext, partial, turn),
+        (*scalars, exchange(send, 0), first_ext, partial, turn),
         "bottomsecond",
     )
-    sends = (early, late)
-    for level in range(1, levels):
-        received = [lax.ppermute(x, "pulse", route("pulse", level)) for x in sends]
-        if level == 1:
-            partial, turn, own_turn, next_turn = own(level, 4, *sends, ext, partial, turn)
-        elif level == 2:
-            (partial,) = own(level, 1, *sends, ext, partial, turn, own_turn)
-            turn = next_turn
-        else:
-            partial, turn = own(level, 2, *sends, ext, partial, turn)
-        if level < levels - 1:
-            following = PARTS[level + 1]
-            early, first_ext = kernel(
-                functools.partial(middle_first_kernel, level, slots),
-                (shape(following[0]), shape(PARTS[level][0], f32, long)),
-                (*scalars, received[0], partial, turn),
-                f"middle{level}first",
-            )
-            *late, ext = kernel(
-                functools.partial(middle_second_kernel, level, slots),
-                (*(shape(n) for n in following[1:]), shape(slots, f32, long)),
-                (*scalars, received[1], first_ext, partial, turn),
-                f"middle{level}second",
-            )
-            sends = (early, *late)
-        else:
-            tiles = jax.ShapeDtypeStruct((2, HALF * 8, LANES), f32)
-            tiles, first_ext = kernel(
-                functools.partial(last_first_kernel, level, slots),
-                (tiles, shape(PARTS[level][0], f32, long)),
-                (*scalars, received[0], partial, turn),
-                "lastfirst",
-            )
-            out = kernel(
-                functools.partial(last_second_kernel, level, slots),
-                jax.ShapeDtypeStruct((2, beams // 8, HALF * 8, LANES), f32),
-                (*scalars, received[1], first_ext, tiles, partial, turn),
-                "lastsecond",
-                ext_scratch
-                + [pltpu.VMEM((2, beams // 8, HALF * 8, LANES), f32), pltpu.SemaphoreType.DMA((2, beams // 8))],
-                HBM_SPEC,
-            )
+    received = exchange(early, 1), exchange(late, 1)
+    partial, turn = own(1, 2, early, late, ext, partial, turn)
+    early, first_ext = kernel(
+        functools.partial(middle_first_kernel, 1, None, slots),
+        (shape(PARTS[2][0]), shape(PARTS[1][0], f32, long)),
+        (*scalars, received[0], partial, turn),
+        "middle1first",
+    )
+    received_first = exchange(early, 2)
+    own_turn, next_turn = kernel(
+        functools.partial(turns_kernel, 2, bins),
+        images,
+        (index, base_table, rate_table, early),
+        "turns2",
+        scalar_count=3,
+    )
+    ext, next_partial, own_ext = kernel(
+        functools.partial(split_own_kernel, 2, slots, False),
+        (shape(slots, f32, long), shape(PARTS[3][0], f32), shape(PARTS[2][0], f32, long)),
+        (*scalars, first_ext, received[1], partial, turn, own_turn),
+        "own2first",
+    )
+    last_early, last_ext = kernel(
+        functools.partial(middle_first_kernel, 2, 0, slots),
+        (shape(PARTS[3][0]), shape(PARTS[2][0], f32, long)),
+        (*scalars, received_first, next_partial, next_turn),
+        "middle2first",
+    )
+    last_first = exchange(last_early, 3)
+    late = kernel(
+        functools.partial(late_send_kernel, 1, slots),
+        shape(PARTS[2][1]),
+        (*scalars, ext, partial, turn),
+        "middle1second",
+    )
+    received_second = exchange(late, 2)
+    next_partial = kernel(
+        functools.partial(split_own_kernel, 2, slots, True),
+        image_shape,
+        (*scalars, ext, partial, turn, own_turn, own_ext),
+        "own2second",
+        ext_scratch,
+    )
+    last_late, ext = kernel(
+        functools.partial(middle_second_kernel, 2, slots),
+        (shape(PARTS[3][1]), shape(slots, f32, long)),
+        (*scalars, received_second, last_ext, next_partial, next_turn),
+        "middle2second",
+    )
+    last_second = exchange(last_late, 3)
+    partial, turn = own(3, 2, last_early, last_late, ext, next_partial, next_turn)
+    tiles, first_ext = kernel(
+        functools.partial(last_first_kernel, 3, slots),
+        (jax.ShapeDtypeStruct((2, HALF * 8, LANES), f32), shape(PARTS[3][0], f32, long)),
+        (*scalars, last_first, partial, turn),
+        "lastfirst",
+    )
+    out = kernel(
+        functools.partial(last_second_kernel, 3, slots),
+        jax.ShapeDtypeStruct((2, beams // 8, HALF * 8, LANES), f32),
+        (*scalars, last_second, first_ext, tiles, partial, turn),
+        "lastsecond",
+        ext_scratch + [pltpu.VMEM((2, beams // 8, HALF * 8, LANES), f32), pltpu.SemaphoreType.DMA((2, beams // 8))],
+        HBM_SPEC,
+    )
     out = out.reshape(2, beams // 8, HALF, 8, LANES)
     return jnp.transpose(out, (0, 1, 3, 2, 4)).reshape(2, beams, bins)
 

time: 35.9 us -> 35.8 us (level)
  starting transfers between devices: 13.5 us -> 12.8 us
  Pallas kernels: 12.8 us -> 13.2 us
    ppermute x7 -> x8, starting transfers between devices: 13.5 us -> 12.8 us  [exchange(): return lax.ppermute(x, 'pulse', route('pulse', level))]
    pallas_call x13 -> x16, Pallas kernels: 10.1 us -> 10.7 us  [kernel(): pl.pallas_call(function, out_shape=out_shape, in_specs=[SMEM_SPEC] * scal...]
    ppermute x7 -> x8, waiting for transfers between devices: 9.36 us -> 9.59 us  [exchange(): return lax.ppermute(x, 'pulse', route('pulse', level))]
  transfers between devices with their start and end apart: 7 -> 8, of which waited for: 5 -> 6; matrix products, arithmetic and copies ran while one was open for 0% -> 0% of each run, Pallas kernels for 23% -> 24%
where the time goes in v5:
time: 35.8 us; the launch traced here: 35.7 us
  Pallas kernels  13.2 us (37%)
  starting transfers between devices  12.8 us (36%)
  waiting for transfers between devices  9.59 us (27%)
    ppermute x8, starting transfers between devices, exchange(): return lax.ppermute(x, 'pulse', route('pulse', level))  12.8 us
    pallas_call x16, Pallas kernels, kernel(): pl.pallas_call(function, out_shape=out_shape, in_specs=[SMEM_SPEC] * scal...  10.7 us
    ppermute x8, waiting for transfers between devices, exchange(): return lax.ppermute(x, 'pulse', route('pulse', level))  9.59 us
    pallas_call x1, Pallas kernels, local(): pl.pallas_call(front_kernel, out_shape=(send_shape, pulse_shape, trig_sha...  2.48 us
  transfers between devices with their start and end apart: 8, of which 6 were waited for; matrix products, arithmetic and copies ran while one was open for 0% of the time, Pallas kernels for 24%

profile of v5, /device:TPU:0, one launch (start us, length us, event | category | flops | bytes accessed | tf_op | source)
XLA Modules:
  0.0 35.7 jit_solution(6848258652564117379)
XLA Ops:
  0.0 2.5 %front.1 = (bf16[5,2,64,128]{3,2,1,0:T(8,128)(2,1)S(1)}, f32[8,2,128,128]{3,2,1,0:T(8,128)S(1)}, f32[2,16,8,128]{3,2,1,0:T(8,128)S(1)}, s32[8,16]{1,0:T(8,128)S(...) custom-call(s32[1]{0:T(128)} %bitcast.index_ref, ...), custom_call_target="tpu_custom_call" | custom-call | tf_op jit(solution)/shard_map/front/pallas_call | solution.py:592
  2.5 0.5 %collective-permute-start = (bf16[5,2,64,128]{3,2,1,0:T(8,128)(2,1)S(1)}, bf16[5,2,64,128]{3,2,1,0:T(8,128)(2,1)S(1)}, u32[]{:S(2)}, u32[]{:S(2)}) collective-permute-start(bf16[5,2,64,128]{3,2,1,0:T(8,128)(2,1)S(1)} %get-tuple-element.43), channel_id=1, source_target_pairs={{0,1},{1,0},{2,3},{3,2},{4,5},{5,4},{6,7},{7,6},{8,9},{9,8},{10,11... | collective-permute-start | bytes 491528 | tf_op jit(solution)/shard_map/ppermute | solution.py:639
  3.0 0.8 %bottomownfirst.1 = (f32[5,2,64,128]{3,2,1,0:T(8,128)S(1)}, f32[5,2,64,128]{3,2,1,0:T(8,128)S(1)}, f32[5,2,128,128]{3,2,1,0:T(8,128)S(1)}) custom-call(s32[1]{0:T(128)} %bitcast.index_ref, s32[4,2,2,16]{3,2,1,0:T(2,128)S(4)} %get-tuple-element.40.beam_ref, s32[4,2,2,16]{3,2,1,0:T(2,128)S(4)} %get-tuple-element.41.shift_ref, ...), custom_call_target="tpu_custom_call" | custom-call | flops 800000 | bytes 1048576 | tf_op jit(solution)/shard_map/bottomownfirst/pallas_call | solution.py:616
  3.8 0.2 collective-permute-done.received_ref
  4.0 0.3 bottomfirst.1
  4.3 0.3 frontsecond.1
  4.7 0.4 %collective-permute-start.2 = (bf16[4,2,64,128]{3,2,1,0:T(8,128)(2,1)S(1)}, bf16[4,2,64,128]{3,2,1,0:T(8,128)(2,1)S(1)}, u32[]{:S(2)}, u32[]{:S(2)}) collective-permute-start(bf16[4,2,64,128]{3,2,1,0:T(8,128)(2,1)S(1)} %frontsecond.1), channel_id=1, source_target_pairs={{0,1},{1,0},{2,3},{3,2},{4,5},{5,4},{6,7},{7,6},{8,9},{9,8},{10,11... | collective-permute-start | bytes 393224 | tf_op jit(solution)/shard_map/ppermute | solution.py:639
  5.1 2.6 %collective-permute-start.1 = (bf16[5,2,64,128]{3,2,1,0:T(8,128)(2,1)S(1)}, bf16[5,2,64,128]{3,2,1,0:T(8,128)(2,1)S(1)}, u32[]{:S(2)}, u32[]{:S(2)}) collective-permute-start(bf16[5,2,64,128]{3,2,1,0:T(8,128)(2,1)S(1)} %get-tuple-element.51.after_ref.rest_0_), channel_id=1, source_target_pairs={{0,2},{1,3},{2,0},{3,1},{4,6},{5,7},{6,4},{7,5},{8,10},{9,11},{10,... | collective-permute-start | bytes 491528 | tf_op jit(solution)/shard_map/ppermute | solution.py:639
  7.8 1.0 %bottomownsecond.1 = (f32[11,2,64,128]{3,2,1,0:T(8,128)S(1)}, f32[11,2,64,128]{3,2,1,0:T(8,128)S(1)}) custom-call(s32[1]{0:T(128)} %bitcast.index_ref, s32[4,2,2,16]{3,2,1,0:T(2,128)S(4)} %get-tuple-element.40.beam_ref, s32[4,2,2,16]{3,2,1,0:T(2,128)S(4)} %get-tuple-element.41.shift_ref, f32[4,2,2,16]{3,2,1,0:T(2,128)S(4)} %get-tuple-element.44.base_ref, ...), custom_call_target="tpu_custom_call" | custom-call | flops 1050000 | bytes 1048576 | tf_op jit(solution)/shard_map/bottomownsecond/pallas_call | solution.py:616
  8.8 0.0 collective-permute-done.2.received_ref
  8.8 0.3 bottomsecond.1
  9.1 0.2 collective-permute-start.3
  9.3 1.5 %own1.1 = (f32[16,2,64,128]{3,2,1,0:T(8,128)S(1)}, f32[16,2,64,128]{3,2,1,0:T(8,128)S(1)}) custom-call(s32[1]{0:T(128)} %bitcast.index_ref, s32[4,2,2,16]{3,2,1,0:T(2,128)S(4)} %get-tuple-element.40.beam_ref, s32[4,2,2,16]{3,2,1,0:T(2,128)S(4)} %get-tuple-element.41.shift_ref, f32[4,2,2,16]{3,2,1,0:T(2,128)S(4)} %get-tuple-element.44.base_ref, ...), custom_call_target="tpu_custom_call" | custom-call | flops 1500000 | bytes 1048576 | tf_op jit(solution)/shard_map/own1/pallas_call | solution.py:616
  10.8 2.0 %collective-permute-done.1.received_ref = bf16[5,2,64,128]{3,2,1,0:T(8,128)(2,1)S(1)} collective-permute-done((bf16[5,2,64,128]{3,2,1,0:T(8,128)(2,1)S(1)}, bf16[5,2,64,128]{3,2,1,0:T(8,128)(2,1)S(1)}, u32[]{:S(2)}, u32[]{:S(2)}) %collective-permute-start.1) | collective-permute-done | bytes 163872 | tf_op jit(solution)/shard_map/ppermute | solution.py:639
  12.8 0.3 middle1first.1
  13.1 2.1 %collective-permute-start.5 = (bf16[5,2,64,128]{3,2,1,0:T(8,128)(2,1)S(1)}, bf16[5,2,64,128]{3,2,1,0:T(8,128)(2,1)S(1)}, u32[]{:S(2)}, u32[]{:S(2)}) collective-permute-start(bf16[5,2,64,128]{3,2,1,0:T(8,128)(2,1)S(1)} %get-tuple-element.61.after_ref), channel_id=1, source_target_pairs={{0,4},{1,5},{2,6},{3,7},{4,0},{5,1},{6,2},{7,3},{8,12},{9,13},{10,... | collective-permute-start | bytes 491528 | tf_op jit(solution)/shard_map/ppermute | solution.py:639
  15.3 0.6 %turns2.1 = (f32[16,2,64,128]{3,2,1,0:T(8,128)S(1)}, f32[16,2,64,128]{3,2,1,0:T(8,128)S(1)}) custom-call(s32[1]{0:T(128)} %bitcast.index_ref, f32[4,2,2,16]{3,2,1,0:T(2,128)S(4)} %get-tuple-element.44.base_ref, f32[4,2,2,16]{3,2,1,0:T(2,128)S(4)} %get-tuple-element.45.rate_ref, bf16[5,2,64,128]{3,2,1,0:T(8,128)(2,1)S(1)} %get-tuple-element.61.after_ref), custom_call_target="tpu_custom_call" | custom-call | flops 500000 | bytes 1048576 | tf_op jit(solution)/shard_map/turns2/pallas_call | solution.py:616
  15.8 0.6 %own2first.1 = (f32[9,2,128,128]{3,2,1,0:T(8,128)S(1)}, f32[5,2,64,128]{3,2,1,0:T(8,128)S(1)}, f32[5,2,128,128]{3,2,1,0:T(8,128)S(1)}) custom-call(s32[1]{0:T(128)} %bitcast.index_ref, s32[4,2,2,16]{3,2,1,0:T(2,128)S(4)} %get-tuple-element.40.beam_ref, s32[4,2,2,16]{3,2,1,0:T(2,128)S(4)} %get-tuple-element.41.shift_ref, ...), custom_call_target="tpu_custom_call" | custom-call | flops 600000 | bytes 1048576 | tf_op jit(solution)/shard_map/own2first/pallas_call | solution.py:616
  16.4 0.2 middle1second.1
  16.6 1.3 %collective-permute-start.4 = (bf16[4,2,64,128]{3,2,1,0:T(8,128)(2,1)S(1)}, bf16[4,2,64,128]{3,2,1,0:T(8,128)(2,1)S(1)}, u32[]{:S(2)}, u32[]{:S(2)}) collective-permute-start(bf16[4,2,64,128]{3,2,1,0:T(8,128)(2,1)S(1)} %middle1second.1), channel_id=1, source_target_pairs={{0,4},{1,5},{2,6},{3,7},{4,0},{5,1},{6,2},{7,3},{8,12},{9,13},{10,... | collective-permute-start | bytes 393224 | tf_op jit(solution)/shard_map/ppermute | solution.py:639
  18.0 1.0 %collective-permute-done.5.received_ref = bf16[5,2,64,128]{3,2,1,0:T(8,128)(2,1)S(1)} collective-permute-done((bf16[5,2,64,128]{3,2,1,0:T(8,128)(2,1)S(1)}, bf16[5,2,64,128]{3,2,1,0:T(8,128)(2,1)S(1)}, u32[]{:S(2)}, u32[]{:S(2)}) %collective-permute-start.5) | collective-permute-done | bytes 163872 | tf_op jit(solution)/shard_map/ppermute | solution.py:639
  18.9 0.3 middle2first.1
  19.2 3.1 %collective-permute-start.7 = (bf16[5,2,64,128]{3,2,1,0:T(8,128)(2,1)S(1)}, bf16[5,2,64,128]{3,2,1,0:T(8,128)(2,1)S(1)}, u32[]{:S(2)}, u32[]{:S(2)}) collective-permute-start(bf16[5,2,64,128]{3,2,1,0:T(8,128)(2,1)S(1)} %get-tuple-element.69.rest_0_), channel_id=1, source_target_pairs={{0,8},{1,9},{2,10},{3,11},{4,12},{5,13},{6,14},{7,15},{8,0},{9,1},... | collective-permute-start | bytes 491528 | tf_op jit(solution)/shard_map/ppermute | solution.py:639
  22.4 0.6 %own2second.1.partial_ref.rest_3_ = f32[16,2,64,128]{3,2,1,0:T(8,128)S(1)} custom-call(s32[1]{0:T(128)} %bitcast.index_ref, s32[4,2,2,16]{3,2,1,0:T(2,128)S(4)} %get-tuple-element.40.beam_ref, s32[4,2,2,16]{3,2,1,0:T(2,128)S(4)} %get-tuple-element.41.shift_ref, s32[4,4]{1,0:T(4,128)S(4)} %get-tuple-element.42.taps_ref, ...), custom_call_target="tpu_custom_call" | custom-call | flops 640000 | bytes 1048576 | tf_op jit(solution)/shard_map/own2second/pallas_call | solution.py:616
  23.0 0.4 %collective-permute-done.4.received_ref = bf16[4,2,64,128]{3,2,1,0:T(8,128)(2,1)S(1)} collective-permute-done((bf16[4,2,64,128]{3,2,1,0:T(8,128)(2,1)S(1)}, bf16[4,2,64,128]{3,2,1,0:T(8,128)(2,1)S(1)}, u32[]{:S(2)}, u32[]{:S(2)}) %collective-permute-start.4) | collective-permute-done | bytes 131104 | tf_op jit(solution)/shard_map/ppermute | solution.py:639
  23.4 0.3 middle2second.1
  23.7 2.4 %collective-permute-start.6 = (bf16[4,2,64,128]{3,2,1,0:T(8,128)(2,1)S(1)}, bf16[4,2,64,128]{3,2,1,0:T(8,128)(2,1)S(1)}, u32[]{:S(2)}, u32[]{:S(2)}) collective-permute-start(bf16[4,2,64,128]{3,2,1,0:T(8,128)(2,1)S(1)} %get-tuple-element.68.rest_1_), channel_id=1, source_target_pairs={{0,8},{1,9},{2,10},{3,11},{4,12},{5,13},{6,14},{7,15},{8,0},{9,1},... | collective-permute-start | bytes 393224 | tf_op jit(solution)/shard_map/ppermute | solution.py:639
  26.1 1.5 %own3.1 = (f32[16,2,64,128]{3,2,1,0:T(8,128)S(1)}, f32[16,2,64,128]{3,2,1,0:T(8,128)S(1)}) custom-call(s32[1]{0:T(128)} %bitcast.index_ref, s32[4,2,2,16]{3,2,1,0:T(2,128)S(4)} %get-tuple-element.40.beam_ref, s32[4,2,2,16]{3,2,1,0:T(2,128)S(4)} %get-tuple-element.41.shift_ref, f32[4,2,2,16]{3,2,1,0:T(2,128)S(4)} %get-tuple-element.44.base_ref, ...), custom_call_target="tpu_custom_call" | custom-call | flops 1470000 | bytes 1048576 | tf_op jit(solution)/shard_map/own3/pallas_call | solution.py:616
  27.6 5.1 %collective-permute-done.7.received_ref = bf16[5,2,64,128]{3,2,1,0:T(8,128)(2,1)S(1)} collective-permute-done((bf16[5,2,64,128]{3,2,1,0:T(8,128)(2,1)S(1)}, bf16[5,2,64,128]{3,2,1,0:T(8,128)(2,1)S(1)}, u32[]{:S(2)}, u32[]{:S(2)}) %collective-permute-start.7) | collective-permute-done | bytes 163872 | tf_op jit(solution)/shard_map/ppermute | solution.py:639
  32.7 0.6 %lastfirst.1 = (f32[2,512,128]{2,1,0:T(8,128)S(1)}, f32[5,2,128,128]{3,2,1,0:T(8,128)S(1)}) custom-call(s32[1]{0:T(128)} %bitcast.index_ref, s32[4,2,2,16]{3,2,1,0:T(2,128)S(4)} %get-tuple-element.40.beam_ref, s32[4,2,2,16]{3,2,1,0:T(2,128)S(4)} %get-tuple-element.41.shift_ref, s32[4,4]{1,0:T(4,128)S(4)} %get-tuple-element.42.taps_ref, ...), custom_call_target="tpu_custom_call" | custom-call | flops 570000 | bytes 1048576 | tf_op jit(solution)/shard_map/lastfirst/pallas_call | solution.py:616
  33.3 0.8 %collective-permute-done.6.received_ref = bf16[4,2,64,128]{3,2,1,0:T(8,128)(2,1)S(1)} collective-permute-done((bf16[4,2,64,128]{3,2,1,0:T(8,128)(2,1)S(1)}, bf16[4,2,64,128]{3,2,1,0:T(8,128)(2,1)S(1)}, u32[]{:S(2)}, u32[]{:S(2)}) %collective-permute-start.6) | collective-permute-done | bytes 131104 | tf_op jit(solution)/shard_map/ppermute | solution.py:639
  34.1 1.6 %lastsecond.1 = f32[2,2,512,128]{3,2,1,0:T(8,128)} custom-call(s32[1]{0:T(128)} %bitcast.index_ref, s32[4,2,2,16]{3,2,1,0:T(2,128)S(4)} %get-tuple-element.40.beam_ref, s32[4,2,2,16]{3,2,1,0:T(2,128)S(4)} %get-tuple-element.41.shift_ref, s32[4,4]{1,0:T(4,128)S(4)} %get-tuple-element.42.taps_ref, ...), custom_call_target="tpu_custom_call" | custom-call | flops 1550000 | bytes 1048576 | tf_op jit(solution)/shard_map/lastsecond/pallas_call | solution.py:616
  (1 shorter events, 0.0 us)
Async XLA Ops:
  2.5 1.5 %collective-permute-start = (bf16[5,2,64,128]{3,2,1,0:T(8,128)(2,1)S(1)}, bf16[5,2,64,128]{3,2,1,0:T(8,128)(2,1)S(1)}, u32[]{:S(2)}, u32[]{:S(2)}) collective-permute-start(bf16[5,2,64,128]{3,2,1,0:T(8,128)(2,1)S(1)} %get-tuple-element.43), channel_id=1, source_target_pairs={{0,1},{1,0},{2,3},{3,2},{4,5},{5,4},{6,7},{7,6},{8,9},{9,8},{10,11... | collective-permute-start | bytes 491528 | tf_op jit(solution)/shard_map/ppermute | solution.py:639
  4.7 4.1 %collective-permute-start.2 = (bf16[4,2,64,128]{3,2,1,0:T(8,128)(2,1)S(1)}, bf16[4,2,64,128]{3,2,1,0:T(8,128)(2,1)S(1)}, u32[]{:S(2)}, u32[]{:S(2)}) collective-permute-start(bf16[4,2,64,128]{3,2,1,0:T(8,128)(2,1)S(1)} %frontsecond.1), channel_id=1, source_target_pairs={{0,1},{1,0},{2,3},{3,2},{4,5},{5,4},{6,7},{7,6},{8,9},{9,8},{10,11... | collective-permute-start | bytes 393224 | tf_op jit(solution)/shard_map/ppermute | solution.py:639
  5.1 7.7 %collective-permute-start.1 = (bf16[5,2,64,128]{3,2,1,0:T(8,128)(2,1)S(1)}, bf16[5,2,64,128]{3,2,1,0:T(8,128)(2,1)S(1)}, u32[]{:S(2)}, u32[]{:S(2)}) collective-permute-start(bf16[5,2,64,128]{3,2,1,0:T(8,128)(2,1)S(1)} %get-tuple-element.51.after_ref.rest_0_), channel_id=1, source_target_pairs={{0,2},{1,3},{2,0},{3,1},{4,6},{5,7},{6,4},{7,5},{8,10},{9,11},{10,... | collective-permute-start | bytes 491528 | tf_op jit(solution)/shard_map/ppermute | solution.py:639
  9.1 6.8 %collective-permute-start.3 = (bf16[4,2,64,128]{3,2,1,0:T(8,128)(2,1)S(1)}, bf16[4,2,64,128]{3,2,1,0:T(8,128)(2,1)S(1)}, u32[]{:S(2)}, u32[]{:S(2)}) collective-permute-start(bf16[4,2,64,128]{3,2,1,0:T(8,128)(2,1)S(1)} %get-tuple-element.56.rest_1_), channel_id=1, source_target_pairs={{0,2},{1,3},{2,0},{3,1},{4,6},{5,7},{6,4},{7,5},{8,10},{9,11},{10,... | collective-permute-start | bytes 393224 | tf_op jit(solution)/shard_map/ppermute | solution.py:639
  13.1 5.8 %collective-permute-start.5 = (bf16[5,2,64,128]{3,2,1,0:T(8,128)(2,1)S(1)}, bf16[5,2,64,128]{3,2,1,0:T(8,128)(2,1)S(1)}, u32[]{:S(2)}, u32[]{:S(2)}) collective-permute-start(bf16[5,2,64,128]{3,2,1,0:T(8,128)(2,1)S(1)} %get-tuple-element.61.after_ref), channel_id=1, source_target_pairs={{0,4},{1,5},{2,6},{3,7},{4,0},{5,1},{6,2},{7,3},{8,12},{9,13},{10,... | collective-permute-start | bytes 491528 | tf_op jit(solution)/shard_map/ppermute | solution.py:639
  16.6 6.8 %collective-permute-start.4 = (bf16[4,2,64,128]{3,2,1,0:T(8,128)(2,1)S(1)}, bf16[4,2,64,128]{3,2,1,0:T(8,128)(2,1)S(1)}, u32[]{:S(2)}, u32[]{:S(2)}) collective-permute-start(bf16[4,2,64,128]{3,2,1,0:T(8,128)(2,1)S(1)} %middle1second.1), channel_id=1, source_target_pairs={{0,4},{1,5},{2,6},{3,7},{4,0},{5,1},{6,2},{7,3},{8,12},{9,13},{10,... | collective-permute-start | bytes 393224 | tf_op jit(solution)/shard_map/ppermute | solution.py:639
  19.2 13.4 %collective-permute-start.7 = (bf16[5,2,64,128]{3,2,1,0:T(8,128)(2,1)S(1)}, bf16[5,2,64,128]{3,2,1,0:T(8,128)(2,1)S(1)}, u32[]{:S(2)}, u32[]{:S(2)}) collective-permute-start(bf16[5,2,64,128]{3,2,1,0:T(8,128)(2,1)S(1)} %get-tuple-element.69.rest_0_), channel_id=1, source_target_pairs={{0,8},{1,9},{2,10},{3,11},{4,12},{5,13},{6,14},{7,15},{8,0},{9,1},... | collective-permute-start | bytes 491528 | tf_op jit(solution)/shard_map/ppermute | solution.py:639
  23.7 10.4 %collective-permute-start.6 = (bf16[4,2,64,128]{3,2,1,0:T(8,128)(2,1)S(1)}, bf16[4,2,64,128]{3,2,1,0:T(8,128)(2,1)S(1)}, u32[]{:S(2)}, u32[]{:S(2)}) collective-permute-start(bf16[4,2,64,128]{3,2,1,0:T(8,128)(2,1)S(1)} %get-tuple-element.68.rest_1_), channel_id=1, source_target_pairs={{0,8},{1,9},{2,10},{3,11},{4,12},{5,13},{6,14},{7,15},{8,0},{9,1},... | collective-permute-start | bytes 393224 | tf_op jit(solution)/shard_map/ppermute | solution.py:639

commit v6 on v5

--- a/solution.py
+++ b/solution.py
@@ -14,7 +14,7 @@
 HALO = 32
 LANES = 128
 HALF = 64
-PARTS = {0: (5, 4), 1: (5, 4), 2: (5, 4), 3: (5, 4)}
+PARTS = {0: (9,), 1: (5, 4), 2: (5, 4), 3: (5, 4)}
 SQRT_HALF = 0.7071067811865476
 VMEM_LIMIT = 24 * 2**20
 
@@ -45,7 +45,6 @@
     "bottomownsecond": 1050,
     "bottomsecond": 270,
     "own1": 1500,
-    "frontsecond": 350,
     "turns2": 500,
     "middle1first": 310,
     "own2first": 600,
@@ -185,10 +184,6 @@
                 send_ref[at, part, pl.ds(first_row, 32)] = pair[part].astype(jnp.bfloat16)
 
 
-def front_second_kernel(index_ref, delays, pulse_ext, trig, after_ref, send_ref):
-    send_pulses(index_ref[0], PARTS[0][0], send_ref, delays, trig, pulse_ext)
-
-
 def projected(k, first_row, rows, delays, trig, ext):
     real = imag = None
     for p in range(ext.shape[0]):
@@ -431,10 +426,10 @@
             partial_ref[rank, 0, here], partial_ref[rank, 1, here] = pair
 
 
-def extend_received(received_ref, ext, first, number):
+def extend_received(received_ref, ext, first, number, source=0):
     for i in range(number):
         for part in range(2):
-            store_extended(ext, (first + i, part), received_ref[i, part].astype(jnp.float32))
+            store_extended(ext, (first + i, part), received_ref[source + i, part].astype(jnp.float32))
 
 
 def copy_extended(source, target):
@@ -472,7 +467,7 @@
 ):
     sends, ext = outs[:-1], outs[-1]
     first = first_ext.shape[0]
-    extend_received(received_ref, ext, first, count - first)
+    extend_received(received_ref, ext, first, count - first, first)
     copy_extended(first_ext, ext)
     send_parents(
         0, index_ref[0], first, sends, (beam_ref, shift_ref), tap_factors(taps_ref, 0), count, ext, partial_ref,
@@ -546,7 +541,8 @@
     ext, tiles, sems,
 ):
     extend_received(received_ref, ext, first_ext.shape[0], received_ref.shape[0])
-    copy_extended(first_ext, ext)
+    for slot in range(EARLY - 1, first_ext.shape[0]):
+        ext[slot] = first_ext[slot]
     tiles[:, 0] = tiles_ref[...]
     factors = tap_factors(taps_ref, level)
     copies = []
@@ -654,13 +650,6 @@
         (*scalars, received, partial, turn),
         "bottomfirst",
     )
-    send = kernel(
-        front_second_kernel,
-        shape(PARTS[0][1]),
-        (index, delay_table, pulse_ext, trig, early),
-        "frontsecond",
-        scalar_count=2,
-    )
     partial, turn = kernel(
         functools.partial(bottom_own_kernel, bins, slots, first, first),
         (shape(beams - first, f32), shape(beams - first, f32)),
@@ -672,7 +661,7 @@
     late, ext = kernel(
         functools.partial(bottom_second_kernel, slots),
         (shape(later), shape(slots, f32, long)),
-        (*scalars, exchange(send, 0), first_ext, partial, turn),
+        (*scalars, received, first_ext, partial, turn),
         "bottomsecond",
     )
     received = exchange(early, 1), exchange(late, 1)

time: 35.8 us -> 36.1 us (level)
  waiting for transfers between devices: 9.59 us -> 10 us
    ppermute x8 -> x7, waiting for transfers between devices: 9.59 us -> 10 us  [exchange(): return lax.ppermute(x, 'pulse', route('pulse', level))]
    pallas_call x16 -> x15, Pallas kernels: 10.7 us -> 10.4 us  [kernel(): pl.pallas_call(function, out_shape=out_shape, in_specs=[SMEM_SPEC] * scal...]
    ppermute x8 -> x7, starting transfers between devices: 12.8 us -> 12.6 us  [exchange(): return lax.ppermute(x, 'pulse', route('pulse', level))]
  transfers between devices with their start and end apart: 8 -> 7, of which waited for: 6 -> 5; matrix products, arithmetic and copies ran while one was open for 0% -> 0% of each run, Pallas kernels for 24% -> 24%
where the time goes in v6:
time: 36.1 us; the launch traced here: 36 us
  Pallas kernels  13.2 us (37%)
  starting transfers between devices  12.6 us (35%)
  waiting for transfers between devices  10 us (28%)
    ppermute x7, starting transfers between devices, exchange(): return lax.ppermute(x, 'pulse', route('pulse', level))  12.6 us
    pallas_call x15, Pallas kernels, kernel(): pl.pallas_call(function, out_shape=out_shape, in_specs=[SMEM_SPEC] * scal...  10.4 us
    ppermute x7, waiting for transfers between devices, exchange(): return lax.ppermute(x, 'pulse', route('pulse', level))  10 us
    pallas_call x1, Pallas kernels, local(): pl.pallas_call(front_kernel, out_shape=(send_shape, pulse_shape, trig_sha...  2.78 us
  transfers between devices with their start and end apart: 7, of which 5 were waited for; matrix products, arithmetic and copies ran while one was open for 0% of the time, Pallas kernels for 24%

profile of v6, /device:TPU:0, one launch (start us, length us, event | category | flops | bytes accessed | tf_op | source)
XLA Modules:
  0.0 36.0 jit_solution(8560263631526107067)
XLA Ops:
  0.0 2.8 %front.1 = (bf16[9,2,64,128]{3,2,1,0:T(8,128)(2,1)S(1)}, f32[8,2,128,128]{3,2,1,0:T(8,128)S(1)}, f32[2,16,8,128]{3,2,1,0:T(8,128)S(1)}, s32[8,16]{1,0:T(8,128)S(...) custom-call(s32[1]{0:T(128)} %bitcast.index_ref, ...), custom_call_target="tpu_custom_call" | custom-call | tf_op jit(solution)/shard_map/front/pallas_call | solution.py:588
  2.8 0.5 %collective-permute-start = (bf16[9,2,64,128]{3,2,1,0:T(8,128)(2,1)S(1)}, bf16[9,2,64,128]{3,2,1,0:T(8,128)(2,1)S(1)}, u32[]{:S(2)}, u32[]{:S(2)}) collective-permute-start(bf16[9,2,64,128]{3,2,1,0:T(8,128)(2,1)S(1)} %get-tuple-element.43), channel_id=1, source_target_pairs={{0,1},{1,0},{2,3},{3,2},{4,5},{5,4},{6,7},{7,6},{8,9},{9,8},{10,11... | collective-permute-start | bytes 884744 | tf_op jit(solution)/shard_map/ppermute | solution.py:635
  3.3 0.8 %bottomownfirst.1 = (f32[5,2,64,128]{3,2,1,0:T(8,128)S(1)}, f32[5,2,64,128]{3,2,1,0:T(8,128)S(1)}, f32[5,2,128,128]{3,2,1,0:T(8,128)S(1)}) custom-call(s32[1]{0:T(128)} %bitcast.index_ref, s32[4,2,2,16]{3,2,1,0:T(2,128)S(4)} %get-tuple-element.40.beam_ref, s32[4,2,2,16]{3,2,1,0:T(2,128)S(4)} %get-tuple-element.41.shift_ref, ...), custom_call_target="tpu_custom_call" | custom-call | flops 800000 | bytes 1048576 | tf_op jit(solution)/shard_map/bottomownfirst/pallas_call | solution.py:612
  4.1 0.4 %collective-permute-done.received_ref = bf16[9,2,64,128]{3,2,1,0:T(8,128)(2,1)S(1)} collective-permute-done((bf16[9,2,64,128]{3,2,1,0:T(8,128)(2,1)S(1)}, bf16[9,2,64,128]{3,2,1,0:T(8,128)(2,1)S(1)}, u32[]{:S(2)}, u32[]{:S(2)}) %collective-permute-start) | collective-permute-done | bytes 294944 | tf_op jit(solution)/shard_map/ppermute | solution.py:635
  4.5 0.3 bottomfirst.1
  4.8 2.9 %collective-permute-start.1 = (bf16[5,2,64,128]{3,2,1,0:T(8,128)(2,1)S(1)}, bf16[5,2,64,128]{3,2,1,0:T(8,128)(2,1)S(1)}, u32[]{:S(2)}, u32[]{:S(2)}) collective-permute-start(bf16[5,2,64,128]{3,2,1,0:T(8,128)(2,1)S(1)} %get-tuple-element.51.rest_0_), channel_id=1, source_target_pairs={{0,2},{1,3},{2,0},{3,1},{4,6},{5,7},{6,4},{7,5},{8,10},{9,11},{10,... | collective-permute-start | bytes 491528 | tf_op jit(solution)/shard_map/ppermute | solution.py:635
  7.8 1.0 %bottomownsecond.1 = (f32[11,2,64,128]{3,2,1,0:T(8,128)S(1)}, f32[11,2,64,128]{3,2,1,0:T(8,128)S(1)}) custom-call(s32[1]{0:T(128)} %bitcast.index_ref, s32[4,2,2,16]{3,2,1,0:T(2,128)S(4)} %get-tuple-element.40.beam_ref, s32[4,2,2,16]{3,2,1,0:T(2,128)S(4)} %get-tuple-element.41.shift_ref, f32[4,2,2,16]{3,2,1,0:T(2,128)S(4)} %get-tuple-element.44.base_ref, ...), custom_call_target="tpu_custom_call" | custom-call | flops 1050000 | bytes 1048576 | tf_op jit(solution)/shard_map/bottomownsecond/pallas_call | solution.py:612
  8.8 0.3 bottomsecond.1
  9.1 0.1 collective-permute-start.2
  9.2 1.5 %own1.1 = (f32[16,2,64,128]{3,2,1,0:T(8,128)S(1)}, f32[16,2,64,128]{3,2,1,0:T(8,128)S(1)}) custom-call(s32[1]{0:T(128)} %bitcast.index_ref, s32[4,2,2,16]{3,2,1,0:T(2,128)S(4)} %get-tuple-element.40.beam_ref, s32[4,2,2,16]{3,2,1,0:T(2,128)S(4)} %get-tuple-element.41.shift_ref, f32[4,2,2,16]{3,2,1,0:T(2,128)S(4)} %get-tuple-element.44.base_ref, ...), custom_call_target="tpu_custom_call" | custom-call | flops 1500000 | bytes 1048576 | tf_op jit(solution)/shard_map/own1/pallas_call | solution.py:612
  10.7 2.1 %collective-permute-done.1.received_ref = bf16[5,2,64,128]{3,2,1,0:T(8,128)(2,1)S(1)} collective-permute-done((bf16[5,2,64,128]{3,2,1,0:T(8,128)(2,1)S(1)}, bf16[5,2,64,128]{3,2,1,0:T(8,128)(2,1)S(1)}, u32[]{:S(2)}, u32[]{:S(2)}) %collective-permute-start.1) | collective-permute-done | bytes 163872 | tf_op jit(solution)/shard_map/ppermute | solution.py:635
  12.8 0.3 middle1first.1
  13.1 2.2 %collective-permute-start.4 = (bf16[5,2,64,128]{3,2,1,0:T(8,128)(2,1)S(1)}, bf16[5,2,64,128]{3,2,1,0:T(8,128)(2,1)S(1)}, u32[]{:S(2)}, u32[]{:S(2)}) collective-permute-start(bf16[5,2,64,128]{3,2,1,0:T(8,128)(2,1)S(1)} %get-tuple-element.61.after_ref), channel_id=1, source_target_pairs={{0,4},{1,5},{2,6},{3,7},{4,0},{5,1},{6,2},{7,3},{8,12},{9,13},{10,... | collective-permute-start | bytes 491528 | tf_op jit(solution)/shard_map/ppermute | solution.py:635
  15.3 0.6 %turns2.1 = (f32[16,2,64,128]{3,2,1,0:T(8,128)S(1)}, f32[16,2,64,128]{3,2,1,0:T(8,128)S(1)}) custom-call(s32[1]{0:T(128)} %bitcast.index_ref, f32[4,2,2,16]{3,2,1,0:T(2,128)S(4)} %get-tuple-element.44.base_ref, f32[4,2,2,16]{3,2,1,0:T(2,128)S(4)} %get-tuple-element.45.rate_ref, bf16[5,2,64,128]{3,2,1,0:T(8,128)(2,1)S(1)} %get-tuple-element.61.after_ref), custom_call_target="tpu_custom_call" | custom-call | flops 500000 | bytes 1048576 | tf_op jit(solution)/shard_map/turns2/pallas_call | solution.py:612
  15.8 0.0 collective-permute-done.2.rest_1_
  15.8 0.6 %own2first.1 = (f32[9,2,128,128]{3,2,1,0:T(8,128)S(1)}, f32[5,2,64,128]{3,2,1,0:T(8,128)S(1)}, f32[5,2,128,128]{3,2,1,0:T(8,128)S(1)}) custom-call(s32[1]{0:T(128)} %bitcast.index_ref, s32[4,2,2,16]{3,2,1,0:T(2,128)S(4)} %get-tuple-element.40.beam_ref, s32[4,2,2,16]{3,2,1,0:T(2,128)S(4)} %get-tuple-element.41.shift_ref, ...), custom_call_target="tpu_custom_call" | custom-call | flops 600000 | bytes 1048576 | tf_op jit(solution)/shard_map/own2first/pallas_call | solution.py:612
  16.4 0.2 middle1second.1
  16.6 1.1 %collective-permute-start.3 = (bf16[4,2,64,128]{3,2,1,0:T(8,128)(2,1)S(1)}, bf16[4,2,64,128]{3,2,1,0:T(8,128)(2,1)S(1)}, u32[]{:S(2)}, u32[]{:S(2)}) collective-permute-start(bf16[4,2,64,128]{3,2,1,0:T(8,128)(2,1)S(1)} %middle1second.1), channel_id=1, source_target_pairs={{0,4},{1,5},{2,6},{3,7},{4,0},{5,1},{6,2},{7,3},{8,12},{9,13},{10,... | collective-permute-start | bytes 393224 | tf_op jit(solution)/shard_map/ppermute | solution.py:635
  17.7 1.3 %collective-permute-done.4.received_ref = bf16[5,2,64,128]{3,2,1,0:T(8,128)(2,1)S(1)} collective-permute-done((bf16[5,2,64,128]{3,2,1,0:T(8,128)(2,1)S(1)}, bf16[5,2,64,128]{3,2,1,0:T(8,128)(2,1)S(1)}, u32[]{:S(2)}, u32[]{:S(2)}) %collective-permute-start.4) | collective-permute-done | bytes 163872 | tf_op jit(solution)/shard_map/ppermute | solution.py:635
  19.1 0.3 middle2first.1
  19.4 3.6 %collective-permute-start.6 = (bf16[5,2,64,128]{3,2,1,0:T(8,128)(2,1)S(1)}, bf16[5,2,64,128]{3,2,1,0:T(8,128)(2,1)S(1)}, u32[]{:S(2)}, u32[]{:S(2)}) collective-permute-start(bf16[5,2,64,128]{3,2,1,0:T(8,128)(2,1)S(1)} %get-tuple-element.69.rest_0_), channel_id=1, source_target_pairs={{0,8},{1,9},{2,10},{3,11},{4,12},{5,13},{6,14},{7,15},{8,0},{9,1},... | collective-permute-start | bytes 491528 | tf_op jit(solution)/shard_map/ppermute | solution.py:635
  23.0 0.6 %own2second.1.partial_ref.rest_3_ = f32[16,2,64,128]{3,2,1,0:T(8,128)S(1)} custom-call(s32[1]{0:T(128)} %bitcast.index_ref, s32[4,2,2,16]{3,2,1,0:T(2,128)S(4)} %get-tuple-element.40.beam_ref, s32[4,2,2,16]{3,2,1,0:T(2,128)S(4)} %get-tuple-element.41.shift_ref, s32[4,4]{1,0:T(4,128)S(4)} %get-tuple-element.42.taps_ref, ...), custom_call_target="tpu_custom_call" | custom-call | flops 640000 | bytes 1048576 | tf_op jit(solution)/shard_map/own2second/pallas_call | solution.py:612
  23.6 0.0 collective-permute-done.3.received_ref
  23.6 0.3 middle2second.1
  23.9 2.2 %collective-permute-start.5 = (bf16[4,2,64,128]{3,2,1,0:T(8,128)(2,1)S(1)}, bf16[4,2,64,128]{3,2,1,0:T(8,128)(2,1)S(1)}, u32[]{:S(2)}, u32[]{:S(2)}) collective-permute-start(bf16[4,2,64,128]{3,2,1,0:T(8,128)(2,1)S(1)} %get-tuple-element.68.rest_1_), channel_id=1, source_target_pairs={{0,8},{1,9},{2,10},{3,11},{4,12},{5,13},{6,14},{7,15},{8,0},{9,1},... | collective-permute-start | bytes 393224 | tf_op jit(solution)/shard_map/ppermute | solution.py:635
  26.1 1.5 %own3.1 = (f32[16,2,64,128]{3,2,1,0:T(8,128)S(1)}, f32[16,2,64,128]{3,2,1,0:T(8,128)S(1)}) custom-call(s32[1]{0:T(128)} %bitcast.index_ref, s32[4,2,2,16]{3,2,1,0:T(2,128)S(4)} %get-tuple-element.40.beam_ref, s32[4,2,2,16]{3,2,1,0:T(2,128)S(4)} %get-tuple-element.41.shift_ref, f32[4,2,2,16]{3,2,1,0:T(2,128)S(4)} %get-tuple-element.44.base_ref, ...), custom_call_target="tpu_custom_call" | custom-call | flops 1470000 | bytes 1048576 | tf_op jit(solution)/shard_map/own3/pallas_call | solution.py:612
  27.5 5.4 %collective-permute-done.6.received_ref = bf16[5,2,64,128]{3,2,1,0:T(8,128)(2,1)S(1)} collective-permute-done((bf16[5,2,64,128]{3,2,1,0:T(8,128)(2,1)S(1)}, bf16[5,2,64,128]{3,2,1,0:T(8,128)(2,1)S(1)}, u32[]{:S(2)}, u32[]{:S(2)}) %collective-permute-start.6) | collective-permute-done | bytes 163872 | tf_op jit(solution)/shard_map/ppermute | solution.py:635
  32.9 0.6 %lastfirst.1 = (f32[2,512,128]{2,1,0:T(8,128)S(1)}, f32[5,2,128,128]{3,2,1,0:T(8,128)S(1)}) custom-call(s32[1]{0:T(128)} %bitcast.index_ref, s32[4,2,2,16]{3,2,1,0:T(2,128)S(4)} %get-tuple-element.40.beam_ref, s32[4,2,2,16]{3,2,1,0:T(2,128)S(4)} %get-tuple-element.41.shift_ref, s32[4,4]{1,0:T(4,128)S(4)} %get-tuple-element.42.taps_ref, ...), custom_call_target="tpu_custom_call" | custom-call | flops 570000 | bytes 1048576 | tf_op jit(solution)/shard_map/lastfirst/pallas_call | solution.py:612
  33.5 0.8 %collective-permute-done.5.received_ref = bf16[4,2,64,128]{3,2,1,0:T(8,128)(2,1)S(1)} collective-permute-done((bf16[4,2,64,128]{3,2,1,0:T(8,128)(2,1)S(1)}, bf16[4,2,64,128]{3,2,1,0:T(8,128)(2,1)S(1)}, u32[]{:S(2)}, u32[]{:S(2)}) %collective-permute-start.5) | collective-permute-done | bytes 131104 | tf_op jit(solution)/shard_map/ppermute | solution.py:635
  34.3 1.6 %lastsecond.1 = f32[2,2,512,128]{3,2,1,0:T(8,128)} custom-call(s32[1]{0:T(128)} %bitcast.index_ref, s32[4,2,2,16]{3,2,1,0:T(2,128)S(4)} %get-tuple-element.40.beam_ref, s32[4,2,2,16]{3,2,1,0:T(2,128)S(4)} %get-tuple-element.41.shift_ref, s32[4,4]{1,0:T(4,128)S(4)} %get-tuple-element.42.taps_ref, ...), custom_call_target="tpu_custom_call" | custom-call | flops 1550000 | bytes 1048576 | tf_op jit(solution)/shard_map/lastsecond/pallas_call | solution.py:612
Async XLA Ops:
  2.8 1.7 %collective-permute-start = (bf16[9,2,64,128]{3,2,1,0:T(8,128)(2,1)S(1)}, bf16[9,2,64,128]{3,2,1,0:T(8,128)(2,1)S(1)}, u32[]{:S(2)}, u32[]{:S(2)}) collective-permute-start(bf16[9,2,64,128]{3,2,1,0:T(8,128)(2,1)S(1)} %get-tuple-element.43), channel_id=1, source_target_pairs={{0,1},{1,0},{2,3},{3,2},{4,5},{5,4},{6,7},{7,6},{8,9},{9,8},{10,11... | collective-permute-start | bytes 884744 | tf_op jit(solution)/shard_map/ppermute | solution.py:635
  4.8 7.9 %collective-permute-start.1 = (bf16[5,2,64,128]{3,2,1,0:T(8,128)(2,1)S(1)}, bf16[5,2,64,128]{3,2,1,0:T(8,128)(2,1)S(1)}, u32[]{:S(2)}, u32[]{:S(2)}) collective-permute-start(bf16[5,2,64,128]{3,2,1,0:T(8,128)(2,1)S(1)} %get-tuple-element.51.rest_0_), channel_id=1, source_target_pairs={{0,2},{1,3},{2,0},{3,1},{4,6},{5,7},{6,4},{7,5},{8,10},{9,11},{10,... | collective-permute-start | bytes 491528 | tf_op jit(solution)/shard_map/ppermute | solution.py:635
  9.1 6.8 %collective-permute-start.2 = (bf16[4,2,64,128]{3,2,1,0:T(8,128)(2,1)S(1)}, bf16[4,2,64,128]{3,2,1,0:T(8,128)(2,1)S(1)}, u32[]{:S(2)}, u32[]{:S(2)}) collective-permute-start(bf16[4,2,64,128]{3,2,1,0:T(8,128)(2,1)S(1)} %get-tuple-element.56.rest_1_), channel_id=1, source_target_pairs={{0,2},{1,3},{2,0},{3,1},{4,6},{5,7},{6,4},{7,5},{8,10},{9,11},{10,... | collective-permute-start | bytes 393224 | tf_op jit(solution)/shard_map/ppermute | solution.py:635
  13.1 6.0 %collective-permute-start.4 = (bf16[5,2,64,128]{3,2,1,0:T(8,128)(2,1)S(1)}, bf16[5,2,64,128]{3,2,1,0:T(8,128)(2,1)S(1)}, u32[]{:S(2)}, u32[]{:S(2)}) collective-permute-start(bf16[5,2,64,128]{3,2,1,0:T(8,128)(2,1)S(1)} %get-tuple-element.61.after_ref), channel_id=1, source_target_pairs={{0,4},{1,5},{2,6},{3,7},{4,0},{5,1},{6,2},{7,3},{8,12},{9,13},{10,... | collective-permute-start | bytes 491528 | tf_op jit(solution)/shard_map/ppermute | solution.py:635
  16.6 7.0 %collective-permute-start.3 = (bf16[4,2,64,128]{3,2,1,0:T(8,128)(2,1)S(1)}, bf16[4,2,64,128]{3,2,1,0:T(8,128)(2,1)S(1)}, u32[]{:S(2)}, u32[]{:S(2)}) collective-permute-start(bf16[4,2,64,128]{3,2,1,0:T(8,128)(2,1)S(1)} %middle1second.1), channel_id=1, source_target_pairs={{0,4},{1,5},{2,6},{3,7},{4,0},{5,1},{6,2},{7,3},{8,12},{9,13},{10,... | collective-permute-start | bytes 393224 | tf_op jit(solution)/shard_map/ppermute | solution.py:635
  19.4 13.6 %collective-permute-start.6 = (bf16[5,2,64,128]{3,2,1,0:T(8,128)(2,1)S(1)}, bf16[5,2,64,128]{3,2,1,0:T(8,128)(2,1)S(1)}, u32[]{:S(2)}, u32[]{:S(2)}) collective-permute-start(bf16[5,2,64,128]{3,2,1,0:T(8,128)(2,1)S(1)} %get-tuple-element.69.rest_0_), channel_id=1, source_target_pairs={{0,8},{1,9},{2,10},{3,11},{4,12},{5,13},{6,14},{7,15},{8,0},{9,1},... | collective-permute-start | bytes 491528 | tf_op jit(solution)/shard_map/ppermute | solution.py:635
  23.9 10.5 %collective-permute-start.5 = (bf16[4,2,64,128]{3,2,1,0:T(8,128)(2,1)S(1)}, bf16[4,2,64,128]{3,2,1,0:T(8,128)(2,1)S(1)}, u32[]{:S(2)}, u32[]{:S(2)}) collective-permute-start(bf16[4,2,64,128]{3,2,1,0:T(8,128)(2,1)S(1)} %get-tuple-element.68.rest_1_), channel_id=1, source_target_pairs={{0,8},{1,9},{2,10},{3,11},{4,12},{5,13},{6,14},{7,15},{8,0},{9,1},... | collective-permute-start | bytes 393224 | tf_op jit(solution)/shard_map/ppermute | solution.py:635
